TPU v7x, 32 devices: a whole 2x2x4 slice. The times are simulated.
32 devices in a mesh: row: 8 (over z, core), col: 4 (over y, x).
Axes of the slice: x: 2, y: 2, z: 4, core: 2. Of those that a mesh axis runs over, the one named last changes fastest.
Arguments:
- matrix: bfloat16 [7, 2048, 14, 1024], P(None, 'row', None, 'col'), may hold values from -1 to 3
- pivots: int32 [2, 256], replicated, may hold values from 256 to 14335, as said below
Outputs:
- factored: bfloat16 [7, 2048, 14, 1024], P(None, 'row', None, 'col')
Inputs may be any that keep to these rules, and one draw needn't show every extreme that they name: Within a step s the pivots[s, :] are distinct and lie in (s + 1) * 256 to 14335.
All inputs are finite; a program needn't handle non-finite values.
Results may differ from a plain program's by a relative error of at most 0.0059.
Values may be sent and summed in bfloat16 or wider, within the bound.
No kernel may reach another device: no remote copies, remote signals or barrier semaphores. Data moves between devices by JAX's collectives and lax.ppermute only.
A program may use at most 128 MiB of HBM per device.

v0:
```python
import jax
import jax.numpy as jnp
from jax import lax
from jax.sharding import PartitionSpec as P

STEPS = 2
NEWTON = 3


def broadcast(shard, axis, root):
    mine = lax.axis_index(axis) == root
    return lax.psum(jnp.where(mine, shard, jnp.zeros_like(shard)), axis)


def newton_inverse(diag_block):
    identity = jnp.eye(diag_block.shape[0], dtype=jnp.float32)
    approx = identity / 3.0
    for _ in range(NEWTON):
        product = jnp.dot(diag_block, approx, precision=lax.Precision.HIGHEST)
        approx = jnp.dot(approx, 2.0 * identity - product, precision=lax.Precision.HIGHEST)
    return approx


def body(matrix, pivots):
    row_count = lax.axis_size("row")
    col_count = lax.axis_size("col")
    row_index = lax.axis_index("row")
    col_index = lax.axis_index("col")
    row_cycles, block_size, col_cycles, _ = matrix.shape
    local_rows = row_cycles * block_size
    local_cols = col_cycles * block_size
    current = matrix.reshape(local_rows, local_cols)
    row_positions = jnp.arange(local_rows, dtype=jnp.int32)
    col_positions = jnp.arange(local_cols, dtype=jnp.int32)
    global_row = (
        row_positions // block_size * row_count * block_size
        + row_index * block_size
        + row_positions % block_size
    )
    global_col = (
        col_positions // block_size * col_count * block_size
        + col_index * block_size
        + col_positions % block_size
    )
    identity = jnp.eye(block_size, dtype=jnp.float32)
    for panel_step in range(STEPS):
        after_row = (panel_step + 1) * block_size
        owner_row = panel_step % row_count
        owner_cycle = panel_step // row_count
        owner_col = panel_step % col_count
        panel_cycle = panel_step // col_count
        chosen = pivots[panel_step]
        owner_of = chosen // block_size % row_count
        local_at = chosen // (block_size * row_count) * block_size + chosen % block_size
        is_mine = owner_of == row_index
        picked = jnp.where(
            is_mine[:, None],
            current[jnp.clip(local_at, 0, local_rows - 1)],
            jnp.zeros((), jnp.bfloat16),
        )
        top_rows = current[owner_cycle * block_size : (owner_cycle + 1) * block_size]
        is_top = row_index == owner_row
        new_top = lax.psum(picked, "row").astype(jnp.float32).astype(jnp.bfloat16)
        old_top = broadcast(top_rows, "row", owner_row)
        target = jnp.where(is_mine, local_at, local_rows)
        current = current.at[target].set(old_top, mode="drop")
        kept_rows = current[owner_cycle * block_size : (owner_cycle + 1) * block_size]
        current = current.at[owner_cycle * block_size : (owner_cycle + 1) * block_size].set(
            jnp.where(is_top, new_top, kept_rows)
        )
        panel_block = current[:, panel_cycle * block_size : (panel_cycle + 1) * block_size]
        is_owner = col_index == owner_col
        diag_block = jnp.where(
            is_owner,
            new_top[:, panel_cycle * block_size : (panel_cycle + 1) * block_size].astype(
                jnp.float32
            ),
            3.0 * identity,
        )
        below_mask = (global_row >= after_row)[:, None]
        inverse = newton_inverse(diag_block)
        own_lower = jnp.where(
            below_mask,
            jnp.dot(panel_block.astype(jnp.float32), inverse, precision=lax.Precision.HIGHEST),
            0.0,
        ).astype(jnp.bfloat16)
        lower_panel = broadcast(own_lower, "col", owner_col)
        right_mask = (global_col >= after_row)[None, :]
        upper_rows = jnp.where(right_mask, new_top, jnp.zeros_like(new_top))
        change = jnp.dot(lower_panel, upper_rows, preferred_element_type=jnp.float32)
        current = (current.astype(jnp.float32) - change).astype(jnp.bfloat16)
        old_panel = current[:, panel_cycle * block_size : (panel_cycle + 1) * block_size]
        current = current.at[:, panel_cycle * block_size : (panel_cycle + 1) * block_size].set(
            jnp.where(jnp.logical_and(is_owner, below_mask), lower_panel, old_panel)
        )
    return current.reshape(row_cycles, block_size, col_cycles, block_size)


def solution(mesh):
    return jax.shard_map(
        body,
        mesh=mesh,
        in_specs=(P(None, "row", None, "col"), P()),
        out_specs=P(None, "row", None, "col"),
        check_vma=False,
    )
```

profile of v0, /device:TPU:0, one launch (start us, length us, event | category | flops | bytes accessed | tf_op | source)
XLA Modules:
  0.0 464.7 jit_solution(9562401692902992597)
XLA Ops:
  6.5 12.6 %copy.6 = bf16[7,256,14,256]{3,2,1,0:T(8,128)(2,1)S(1)} copy(bf16[7,256,14,256]{3,1,2,0:T(8,128)(2,1)} %param.10) | data formatting | bytes 25690112 | tf_op args[0]
  19.1 0.7 copy-done.4
  19.9 15.8 %copy.11 = bf16[224,8,14,256]{3,1,2,0:T(8,128)(2,1)} copy(bf16[224,8,14,256]{3,2,1,0:T(8,128)(2,1)S(1)} %bitcast.68) | data formatting | bytes 25690112
  35.6 2.5 copy.10
  38.2 1.6 broadcast_select_fusion.2
  39.9 2.7 copy.8
  42.6 9.8 %gather_fusion = bf16[256,3584]{1,0:T(8,128)(2,1)S(1)} fusion(bf16[1792,3584]{1,0:T(8,128)(2,1)} %bitcast.66, s32[1024]{0:T(1024)S(1)} %pad_clamp_fusion.1), kind=kCustom, calls=%fused_computation | custom fusion | bytes 3671040 | tf_op jit(solution)/shard_map/gather | solution.py:58
  52.4 1.4 broadcast_select_fusion.1
  53.9 0.5 all-reduce.7.cloned.1.call-start
  54.5 87.8 %all-reduce.13.cloned.1.call-done = (bf16[256,3584]{1,0:T(8,128)(2,1)}, bf16[256,3584]{1,0:T(8,128)(2,1)}) async-done(((bf16[256,3584]{1,0:T(8,128)(2,1)}, bf16[256,3584]{1,0:T(8,128)(2,1)}), (bf16[256,3584]{1,0:T(8,128)(2,1)}, bf16[256,3584]{1,0:T(8,128)(2,1)})) %all-reduce.13.cloned.1.call-update) | async-done | bytes 3670032 | tf_op jit(solution)/shard_map/psum | solution.py:12
  142.3 16.5 %scatter_fusion = bf16[1792,3584]{1,0:T(8,128)(2,1)} fusion(bf16[1792,3584]{1,0:T(8,128)(2,1)} %bitcast.67, s32[256]{0:T(256)S(1)} %bitcast.70, bf16[256,3584]{1,0:T(8,128)(2,1)} %get-tuple-element.55), kind=kCustom, calls=%fused_computation.2 | custom fusion | bytes 5506048 | tf_op jit(solution)/shard_map/scatter | solution.py:66
  158.8 3.2 fusion.5
  162.7 0.4 convolution_subtract_fusion.4
  163.5 0.4 convolution_subtract_fusion.3
  164.3 3.1 fusion.3
  167.4 0.6 compare_reduce_fusion
  168.1 50.0 %all-reduce.7.cloned.1.call-done = bf16[1792,256]{1,0:T(8,128)(2,1)} async-done(((bf16[1792,256]{1,0:T(8,128)(2,1)}), bf16[1792,256]{1,0:T(8,128)(2,1)}) %all-reduce.7.cloned.1.call-update) | async-done | bytes 917520 | tf_op jit(solution)/shard_map/psum | solution.py:12
  218.2 11.5 %subtract_convert_fusion.1 = bf16[1792,3584]{1,0:T(8,128)(2,1)} fusion(bf16[1792,3584]{1,0:T(8,128)(2,1)} %fusion.5, bf16[1792,256]{1,0:T(8,128)(2,1)} %all-reduce.7.cloned.1.call-done, bf16[256,3584]{1,0:T(8,128)(2,1)S(1)} %copy-done, pred[3584]{0:T(1024)(128)(4,1)S(1)} %broadcast_compare_fusion.1), kind=kOutput, calls=%fused_computation.5 | convolution fusion | flops 3308519424 | bytes 28446208 | tf_op jit(solution)/shard_map/dot_general | solution.py:90
  229.7 3.3 fusion.10
  232.9 9.8 %gather_fusion.1 = bf16[256,3584]{1,0:T(8,128)(2,1)S(1)} fusion(bf16[1792,3584]{1,0:T(8,128)(2,1)} %fusion.10, s32[1024]{0:T(1024)S(1)} %pad_clamp_fusion), kind=kCustom, calls=%fused_computation.1 | custom fusion | bytes 3671040 | tf_op jit(solution)/shard_map/gather | solution.py:58
  242.8 3.6 slice_select_fusion.1
  246.7 86.9 %all-reduce.11.cloned.1.call-done = (bf16[256,3584]{1,0:T(8,128)(2,1)}, bf16[256,3584]{1,0:T(8,128)(2,1)}) async-done(((bf16[256,3584]{1,0:T(8,128)(2,1)}, bf16[256,3584]{1,0:T(8,128)(2,1)}), (bf16[256,3584]{1,0:T(8,128)(2,1)}, bf16[256,3584]{1,0:T(8,128)(2,1)})) %all-reduce.11.cloned.1.call-update) | async-done | bytes 3670032 | tf_op jit(solution)/shard_map/psum | solution.py:12
  333.6 16.5 %scatter_fusion.1 = bf16[1792,3584]{1,0:T(8,128)(2,1)} fusion(bf16[1792,3584]{1,0:T(8,128)(2,1)} %fusion.10, s32[256]{0:T(256)S(1)} %bitcast.71, bf16[256,3584]{1,0:T(8,128)(2,1)} %get-tuple-element.53), kind=kCustom, calls=%fused_computation.3 | custom fusion | bytes 5506048 | tf_op jit(solution)/shard_map/scatter | solution.py:66
  350.2 3.2 fusion.4
  354.1 0.4 convolution_subtract_fusion.1
  354.9 0.4 convolution_subtract_fusion
  355.7 3.1 fusion.2
  358.8 50.7 %all-reduce.9.cloned.1.call-done = bf16[1792,256]{1,0:T(8,128)(2,1)} async-done(((bf16[1792,256]{1,0:T(8,128)(2,1)}), bf16[1792,256]{1,0:T(8,128)(2,1)}) %all-reduce.9.cloned.1.call-update) | async-done | bytes 917520 | tf_op jit(solution)/shard_map/psum | solution.py:12
  409.6 11.5 %subtract_convert_fusion = bf16[1792,3584]{1,0:T(8,128)(2,1)} fusion(bf16[1792,3584]{1,0:T(8,128)(2,1)} %fusion.4, bf16[1792,256]{1,0:T(8,128)(2,1)} %all-reduce.9.cloned.1.call-done, bf16[256,3584]{1,0:T(8,128)(2,1)S(1)} %copy-done.1, pred[3584]{0:T(1024)(128)(4,1)S(1)} %broadcast_compare_fusion), kind=kOutput, calls=%fused_computation.4 | convolution fusion | flops 3308519424 | bytes 28446208 | tf_op jit(solution)/shard_map/dot_general | solution.py:90
  421.1 3.3 fusion.11
  424.3 22.4 %reshape.600 = bf16[7,256,14,256]{3,2,1,0:T(8,128)(2,1)} reshape(bf16[1792,3584]{1,0:T(8,128)(2,1)} %fusion.11) | data formatting | bytes 25690112 | tf_op jit(solution)/shard_map/reshape | solution.py:96
  446.8 10.9 %copy.9 = bf16[7,256,14,256]{3,1,2,0:T(8,128)(2,1)} copy(bf16[7,256,14,256]{3,2,1,0:T(8,128)(2,1)} %reshape.600) | data formatting | bytes 25690112 | tf_op jit(solution)/shard_map/reshape | solution.py:96
  (40 shorter events, 3.6 us)
Async XLA Ops:
  6.5 135.8 %all-reduce.13.cloned.1.call-start = ((), (), s32[]{:S(2)}) async-start(), calls=%async_computation.3 | async-start | bytes 7340032 | tf_op jit(solution)/shard_map/psum | solution.py:12
  19.1 0.7 copy-start.4
  19.8 15.8 %slice-start = ((bf16[7,256,14,256]{3,1,2,0:T(8,128)(2,1)}), bf16[1,256,14,256]{3,1,2,0:T(8,128)(2,1)S(1)}, s32[]{:S(2)}) async-start(bf16[7,256,14,256]{3,1,2,0:T(8,128)(2,1)} %param.10), calls=%async_computation.4 | async-start | bytes 3670016 | tf_op jit(solution)/shard_map/slice | solution.py:61
  53.9 164.3 %all-reduce.7.cloned.1.call-start = ((), (), s32[]{:S(2)}) async-start(), calls=%async_computation | async-start | bytes 1835008 | tf_op jit(solution)/shard_map/psum | solution.py:12
  142.3 16.5 %copy-start = (bf16[256,3584]{1,0:T(8,128)(2,1)S(1)}, bf16[256,3584]{1,0:T(8,128)(2,1)}, u32[]{:S(2)}) copy-start(bf16[256,3584]{1,0:T(8,128)(2,1)} %get-tuple-element.56) | copy-start | bytes 5505028
  167.4 166.2 %all-reduce.11.cloned.1.call-start = ((), (), s32[]{:S(2)}) async-start(), calls=%async_computation.2 | async-start | bytes 7340032 | tf_op jit(solution)/shard_map/psum | solution.py:12
  218.2 11.5 %copy-start.2 = (bf16[1792,256]{1,0:T(8,128)(2,1)S(1)}, bf16[1792,256]{1,0:T(8,128)(2,1)}, u32[]{:S(2)}) copy-start(bf16[1792,256]{1,0:T(8,128)(2,1)} %all-reduce.7.cloned.1.call-done) | copy-start | bytes 2752516
  246.4 163.1 %all-reduce.9.cloned.1.call-start = ((), (), s32[]{:S(2)}) async-start(), calls=%async_computation.1 | async-start | bytes 1835008 | tf_op jit(solution)/shard_map/psum | solution.py:12
  333.6 16.5 %copy-start.1 = (bf16[256,3584]{1,0:T(8,128)(2,1)S(1)}, bf16[256,3584]{1,0:T(8,128)(2,1)}, u32[]{:S(2)}) copy-start(bf16[256,3584]{1,0:T(8,128)(2,1)} %get-tuple-element.54) | copy-start | bytes 5505028
  409.5 11.5 %copy-start.3 = (bf16[1792,256]{1,0:T(8,128)(2,1)S(1)}, bf16[1792,256]{1,0:T(8,128)(2,1)}, u32[]{:S(2)}) copy-start(bf16[1792,256]{1,0:T(8,128)(2,1)} %all-reduce.9.cloned.1.call-done) | copy-start | bytes 2752516
Sparse Core Ops, SparseCore 0:
  54.0 88.2 all-reduce.12
  167.5 50.6 all-reduce.6
  246.6 87.0 all-reduce.10
  358.9 50.6 all-reduce.8
where the time goes:
time: 473 us; the launch traced here: 465 us
  waiting for transfers between devices  276 us (58%)
  local copies, waits for them, and re-layouts  120 us (25%)
  matrix products  33.8 us (7%)
  other arithmetic  20.3 us (4%)
  between operations  13.8 us (3%)
    psum x4, waiting for transfers between devices, broadcast(): return lax.psum(jnp.where(mine, shard, jnp.zeros_like(shard)), axis)  276 us
    reshape x2, local copies, waits for them, and re-layouts, body(): return current.reshape(row_cycles, block_size, col_cycles, block_size)  33.4 us
    scatter x2, local copies, waits for them, and re-layouts, body(): current = current.at[target].set(old_top, mode='drop')  33 us
    unnamed x13, local copies, waits for them, and re-layouts  31.6 us
    dot_general x2, matrix products, body(): jnp.dot(lower_panel, upper_rows, preferred_element_type=jnp.float32)  23 us
    gather x2, local copies, waits for them, and re-layouts, body(): current[jnp.clip(local_at, 0, local_rows - 1)]  19.7 us
  transfers between devices with their start and end apart: 4, of which 4 were waited for; matrix products, arithmetic and copies ran while one was open for 0% of the time, Pallas kernels for 0%

commit v1 on v0

v1 whole, which is shorter than its diff:
```python
import functools

import jax
import jax.numpy as jnp
from jax import lax
from jax.experimental import pallas as pl
from jax.experimental.pallas import tpu as pltpu
from jax.sharding import PartitionSpec as P

STEPS = 2
NEWTON = 3
CHUNKS = 4
F32 = jnp.float32
BF16 = jnp.bfloat16
VMEM_LIMIT = 56 * 1024 * 1024


def dot(a, b):
    return jnp.dot(a, b, preferred_element_type=F32)


def dot_full(a, b):
    return jnp.dot(a, b, precision=lax.Precision.HIGHEST, preferred_element_type=F32)


def gather_kernel(rows_ref, block_ref, mine_ref, other_ref, onehot):
    cycles, slots, size = onehot.shape

    @pl.when(pl.program_id(0) == 0)
    def _():
        wanted = rows_ref[...]
        for cycle in range(cycles):
            at = lax.broadcasted_iota(jnp.int32, (slots, size), 1) + cycle * size
            onehot[cycle] = jnp.where(wanted == at, 1.0, 0.0).astype(BF16)

    total = dot(onehot[0], block_ref[0, 0])
    for cycle in range(1, cycles):
        total += dot(onehot[cycle], block_ref[cycle, 0])
    mine_ref[0] = total[: slots // 2].astype(BF16)
    other_ref[0] = total[slots // 2 :].astype(BF16)


def gather_rows(matrix, rows, first, count):
    cycles, _, size, _ = matrix.shape
    slots = rows.shape[0]
    half = jax.ShapeDtypeStruct((count, slots // 2, size), BF16)
    half_spec = pl.BlockSpec((1, slots // 2, size), lambda j: (j, 0, 0))
    return pl.pallas_call(
        gather_kernel,
        grid=(count,),
        in_specs=[
            pl.BlockSpec((slots, 1), lambda j: (0, 0)),
            pl.BlockSpec((cycles, 1, size, size), lambda j: (0, j + first, 0, 0)),
        ],
        out_specs=[half_spec, half_spec],
        out_shape=[half, half],
        scratch_shapes=[pltpu.VMEM((cycles, slots, size), BF16)],
        compiler_params=pltpu.CompilerParams(vmem_limit_bytes=VMEM_LIMIT),
        cost_estimate=pl.CostEstimate(
            flops=2 * slots * cycles * size * size * count,
            bytes_accessed=2 * (cycles * size + slots) * size * count,
            transcendentals=0,
        ),
        name="gather_rows",
    )(rows, matrix)


def newton_inverse(diag, identity):
    third = 1.0 / 3.0
    approx = (2.0 * identity - diag * third) * third
    for _ in range(NEWTON - 1):
        approx = dot_full(approx, 2.0 * identity - dot_full(diag, approx))
    return approx


def split_dot(a, b):
    high = b.astype(BF16)
    rest = b - high.astype(F32)
    mid = rest.astype(BF16)
    low = (rest - mid.astype(F32)).astype(BF16)
    return dot(a, low) + dot(a, mid) + dot(a, high)


def whole_rows(place, new_mine, x_other, own_other, me_other):
    new_other = jnp.where(me_other, own_other, x_other)
    first_core = place[1] == 0
    return (
        jnp.where(first_core, new_mine, new_other),
        jnp.where(first_core, new_other, new_mine),
    )


def old_rows(place, x_mine, x_other, top_mine, top_other):
    first_chip = place[0] == 0
    return jnp.concatenate(
        [
            jnp.where(first_chip, top_mine, x_mine),
            jnp.where(first_chip, top_other, x_other),
        ],
        axis=0,
    )


def panel_kernel(
    place, slot_ref, me_ref, panel_ref, new_ref, xm_ref, xo_ref, own_ref, top_ref,
    lower0_ref, lower1_ref, corner_ref, put_ref, keep_ref,
):
    cycles, _, size, _ = panel_ref.shape
    slots = slot_ref.shape[1]
    row = 2 * place[0] + place[1]
    me_other = me_ref[...] != 0
    new0, new1, old = [], [], []
    for b in range(2):
        first, second = whole_rows(place, new_ref[b], xo_ref[b], own_ref[b], me_other)
        new0.append(first)
        new1.append(second)
        old.append(old_rows(place, xm_ref[b], xo_ref[b], panel_ref[0, b], top_ref[b]))
    identity = jnp.where(
        lax.broadcasted_iota(jnp.int32, (size, size), 0)
        == lax.broadcasted_iota(jnp.int32, (size, size), 1),
        1.0,
        0.0,
    ).astype(F32)
    inverse0 = newton_inverse(new0[0].astype(F32), identity)
    corner = split_dot(new1[0], inverse0).astype(BF16)
    corner_ref[...] = corner
    inverse1 = newton_inverse(
        (new1[1].astype(F32) - dot(corner, new0[1])).astype(BF16).astype(F32), identity
    )
    for cycle in range(cycles):
        at = lax.broadcasted_iota(jnp.int32, (size, slots), 0) + cycle * size
        put = jnp.where(slot_ref[...] == at, 1.0, 0.0)
        keep = 1.0 - jnp.sum(put, axis=1, keepdims=True)
        put = put.astype(BF16)
        put_ref[cycle] = put
        keep_ref[cycle] = keep
        left = dot(put, old[0]) + keep * panel_ref[cycle, 0].astype(F32)
        right = dot(put, old[1]) + keep * panel_ref[cycle, 1].astype(F32)
        if cycle == 0:
            left = jnp.where(row == 0, new0[0].astype(F32), jnp.where(row == 1, new1[0].astype(F32), left))
            right = jnp.where(row == 0, new0[1].astype(F32), jnp.where(row == 1, new1[1].astype(F32), right))
        lower = split_dot(left.astype(BF16), inverse0)
        if cycle == 0:
            lower = jnp.where(row == 0, 0.0, lower)
        lower = lower.astype(BF16)
        lower0_ref[cycle] = lower
        right = (right - dot(lower, new0[1])).astype(BF16)
        lower = split_dot(right, inverse1)
        if cycle == 0:
            lower = jnp.where(row <= 1, 0.0, lower)
        lower1_ref[cycle] = lower.astype(BF16)


def factor_panels(place, slot_of, me_other, panel, rows):
    cycles, _, size, _ = panel.shape
    slots = slot_of.shape[1]
    vmem = pl.BlockSpec(memory_space=pltpu.VMEM)
    lower = jax.ShapeDtypeStruct((cycles, size, size), BF16)
    return pl.pallas_call(
        panel_kernel,
        in_specs=[pl.BlockSpec(memory_space=pltpu.SMEM)] + [vmem] * 8,
        out_specs=[vmem] * 5,
        out_shape=[
            lower,
            lower,
            jax.ShapeDtypeStruct((size, size), BF16),
            jax.ShapeDtypeStruct((cycles, size, slots), BF16),
            jax.ShapeDtypeStruct((cycles, size, 1), F32),
        ],
        compiler_params=pltpu.CompilerParams(vmem_limit_bytes=VMEM_LIMIT),
        cost_estimate=pl.CostEstimate(
            flops=8_000_000_000, bytes_accessed=8_000_000, transcendentals=0
        ),
        name="factor_panels",
    )(place, slot_of, me_other, panel, *rows)


def update_kernel(
    first, place, me_ref, block_ref, new_ref, xm_ref, xo_ref, own_ref, top_ref,
    lower0_ref, lower1_ref, corner_ref, put_ref, keep_ref, *rest,
):
    out_ref = rest[-1]
    cycles = lower0_ref.shape[0]
    row = 2 * place[0] + place[1]
    upper0, new1 = whole_rows(place, new_ref[0], xo_ref[0], own_ref[0], me_ref[...] != 0)
    old = old_rows(place, xm_ref[0], xo_ref[0], block_ref[0, 0], top_ref[0])
    upper1 = (new1.astype(F32) - dot(corner_ref[...], upper0)).astype(BF16)
    for cycle in range(cycles):
        block = dot(put_ref[cycle], old) + keep_ref[cycle] * block_ref[cycle, 0].astype(F32)
        if cycle == 0:
            block = jnp.where(row == 0, upper0.astype(F32), jnp.where(row == 1, new1.astype(F32), block))
        block = (block - dot(lower0_ref[cycle], upper0)).astype(BF16).astype(F32)
        out_ref[cycle, 0] = (block - dot(lower1_ref[cycle], upper1)).astype(BF16)
    if first == 0:

        @pl.when(jnp.logical_and(pl.program_id(0) == 0, place[2] == 0))
        def _():
            for cycle in range(cycles):
                block = lower0_ref[cycle]
                if cycle == 0:
                    block = jnp.where(row == 0, upper0, block)
                out_ref[cycle, 0] = block

        @pl.when(jnp.logical_and(pl.program_id(0) == 0, place[2] == 1))
        def _():
            for cycle in range(cycles):
                block = lower1_ref[cycle]
                if cycle == 0:
                    block = jnp.where(row == 0, upper0, jnp.where(row == 1, upper1, block))
                out_ref[cycle, 0] = block


def update_columns(place, me_other, matrix, rows, factors, first, count, result):
    cycles, blocks, size, _ = matrix.shape
    slots = factors[3].shape[2]
    column = pl.BlockSpec((1, slots // 2, size), lambda j: (j, 0, 0))
    whole = lambda a: pl.BlockSpec(a.shape, lambda j, n=a.ndim: (0,) * n)
    blocks_spec = pl.BlockSpec((cycles, 1, size, size), lambda j: (0, j + first, 0, 0))
    operands = [place, me_other, matrix, *rows, *factors]
    in_specs = [pl.BlockSpec(memory_space=pltpu.SMEM), whole(me_other), blocks_spec]
    in_specs += [column] * 4
    in_specs += [pl.BlockSpec((1, size, size), lambda j: (j + first, 0, 0))]
    in_specs += [whole(f) for f in factors]
    aliases = {}
    if result is not None:
        aliases = {len(operands): 0}
        operands.append(result)
        in_specs.append(pl.BlockSpec(memory_space=pl.ANY))
    return pl.pallas_call(
        functools.partial(update_kernel, first),
        grid=(count,),
        in_specs=in_specs,
        out_specs=blocks_spec,
        out_shape=jax.ShapeDtypeStruct(matrix.shape, BF16),
        input_output_aliases=aliases,
        compiler_params=pltpu.CompilerParams(vmem_limit_bytes=VMEM_LIMIT),
        cost_estimate=pl.CostEstimate(
            flops=2 * cycles * size * size * (slots + 2 * size) * count,
            bytes_accessed=4 * cycles * size * size * count,
            transcendentals=0,
        ),
        name="update_columns",
    )(*operands)


def permutation(pivots):
    size = pivots.shape[1]
    index = jnp.arange(size, dtype=jnp.int32)
    pivot0, pivot1 = pivots[0], pivots[1]
    again = pivot0[:, None] == pivot1[None, :]
    inner = pivot0[:, None] == size + index[None, :]
    second = size + index + jnp.sum(jnp.where(inner, index[:, None] - size - index[None, :], 0), 0)
    source1 = pivot1 + jnp.sum(jnp.where(again, index[:, None] - pivot1[None, :], 0), 0)
    leaves0 = index + jnp.sum(jnp.where(again, second[None, :] - index[:, None], 0), 1)
    return jnp.concatenate([pivot0, source1]), jnp.concatenate([leaves0, second])


def send_panels(own, cols):
    col = lax.axis_index("col")
    if cols == 4:
        cross = lax.ppermute(own, "col", [(0, 1), (1, 0)])
        pieces = []
        parts = 2
        step = own.shape[0] // parts if own.shape[0] % parts == 0 else 0
        cuts = [own[i * step : (i + 1) * step] for i in range(parts)] if step else [own]
        for cut in cuts:
            down = lax.ppermute(cut, "col", [(0, 2), (1, 3)])
            over = lax.ppermute(down, "col", [(2, 3), (3, 2)])
            pieces.append((down, over))
        down = jnp.concatenate([p[0] for p in pieces], 0)
        over = jnp.concatenate([p[1] for p in pieces], 0)
        first = jnp.where(col == 0, own, jnp.where(col == 1, cross, jnp.where(col == 2, down, over)))
        second = jnp.where(col == 1, own, jnp.where(col == 0, cross, jnp.where(col == 3, down, over)))
        return first, second
    zero = jnp.zeros_like(own)
    both = jnp.stack([jnp.where(col == 0, own, zero), jnp.where(col == 1, own, zero)])
    both = lax.psum(both, "col")
    return both[0], both[1]


def body(matrix, pivots):
    rows = lax.axis_size("row")
    cols = lax.axis_size("col")
    chips = rows // 2
    row = lax.axis_index("row")
    col = lax.axis_index("col")
    chip = row // 2
    core = row % 2
    cycles, size, blocks, _ = matrix.shape
    slots = STEPS * size
    matrix = matrix.transpose(0, 2, 1, 3)

    source, leaves = permutation(pivots)
    device_of = lambda r: r // size % rows
    local_of = lambda r: r // (size * rows) * size + r % size
    owner = device_of(source) // 2
    me = device_of(source) == row
    from_row = jnp.where(jnp.logical_and(chip == 0, owner != 0), leaves, source)
    taken = jnp.where(device_of(from_row) == row, local_of(from_row), -1)
    outside = jnp.logical_and(me, source >= slots)
    lands = jnp.where(outside, local_of(source), -1)
    absolute = jnp.arange(slots, dtype=jnp.int32)
    lands_top = jnp.max(jnp.where(leaves[None, :] == absolute[:, None], lands[None, :], -1), 1)
    lands = jnp.where(chip == 0, lands_top, lands)
    arrange = lambda v: jnp.where(core == 0, v, jnp.roll(v, size))
    owner = arrange(owner)
    me = arrange(me)
    taken = arrange(taken)[:, None]
    lands = arrange(lands)[None, :]
    me_other = me[size:, None].astype(jnp.int32)
    me_mine = me[None, :size, None]
    owner_mine = owner[None, :size, None]
    place = jnp.stack([chip, core, col]).astype(jnp.int32)

    swap = [(r, r ^ 1) for r in range(rows)]

    def hop_pairs(h):
        pairs = []
        for a, b in ((h, h + 1), (chips - 1 - h, chips - 2 - h)):
            pairs += [(2 * a, 2 * b), (2 * a + 1, 2 * b + 1)]
        return pairs

    def exchange(mine, other):
        native = mine + lax.ppermute(other, "row", swap)
        own = jnp.logical_or(chip == 0, owner_mine == chip)
        received = []
        for h in range(chips - 1):
            out = native if h == 0 else jnp.where(own, native, received[-1])
            received.append(lax.ppermute(out, "row", hop_pairs(h)))
        new = native
        old = native
        for h in range(chips - 1):
            left = jnp.logical_and(chip - 1 == h, owner_mine < chip)
            right = jnp.logical_and(chips - 2 - chip == h, owner_mine > chip)
            new = jnp.where(jnp.logical_or(left, right), received[h], new)
            old = jnp.where(chip - 1 == h, received[h], old)
        theirs = jnp.logical_and(owner_mine == chip, jnp.logical_not(me_mine))
        x_mine = jnp.where(me_mine, old, new)
        x_send = jnp.where(jnp.logical_and(theirs, chip != 0), old, new)
        return new, x_mine, lax.ppermute(x_send, "row", swap), other

    panel_mine, panel_other = gather_rows(matrix, taken, 0, 1)
    native = jnp.concatenate([panel_mine, panel_other], 1)
    native0, native1 = send_panels(native[0], cols)
    raw0, raw1 = send_panels(matrix[:, 0].reshape(cycles * size, size), cols)
    panel = jnp.stack([raw0.reshape(cycles, size, size), raw1.reshape(cycles, size, size)], 1)
    first_swap = [(0, 1), (1, 0)]
    panel_top = lax.ppermute(panel[0], "row", first_swap)
    natives = jnp.stack([native0, native1])
    panel_rows = exchange(natives[:, :size], natives[:, size:])

    top = lax.ppermute(matrix[0], "row", first_swap)
    base, extra = divmod(blocks, CHUNKS)
    counts = [base + (1 if i < extra else 0) for i in range(CHUNKS)]
    starts = [sum(counts[:i]) for i in range(CHUNKS)]
    chunk_rows = []
    for first, count in zip(starts, counts):
        chunk_rows.append(exchange(*gather_rows(matrix, taken, first, count)))

    factors = factor_panels(place, lands, me_other, panel, (*panel_rows, panel_top))
    result = None
    for first, count, chunk in zip(starts, counts, chunk_rows):
        result = update_columns(
            place, me_other, matrix, (*chunk, top), factors, first, count, result
        )
    return result.transpose(0, 2, 1, 3)


def solution(mesh):
    return jax.shard_map(
        body,
        mesh=mesh,
        in_specs=(P(None, "row", None, "col"), P()),
        out_specs=P(None, "row", None, "col"),
        check_vma=False,
    )
```

time: 473 us -> 209 us (0.44); the launches traced: 465 us -> 207 us
  waiting for transfers between devices: 276 us -> 51.4 us
  local copies, waits for them, and re-layouts: 120 us -> 12.8 us
  Pallas kernels: 0 us -> 71 us
  starting transfers between devices: 0.81 us -> 51.2 us
  matrix products: 33.8 us -> 0 us
  between operations: 13.8 us -> 0.84 us
    psum x4 -> x0, waiting for transfers between devices: 276 us -> none  [broadcast(): return lax.psum(jnp.where(mine, shard, jnp.zeros_like(shard)), axis)]
    pallas_call x0 -> x10, Pallas kernels: none -> 71 us  [the longest x4 35.6 us: update_columns(): pl.pallas_call(functools.partial(update_kernel, first), grid=(count,), in...]
    ppermute x0 -> x37, waiting for transfers between devices: none -> 51.4 us  [the longest x15 51.4 us: exchange(): received.append(lax.ppermute(out, 'row', hop_pairs(h)))]
    ppermute x0 -> x37, starting transfers between devices: none -> 51.2 us  [the longest x15 21.9 us: exchange(): received.append(lax.ppermute(out, 'row', hop_pairs(h)))]
    dot_general x16 -> x0, matrix products: 33.8 us -> none  [the longest x2 23 us: body(): jnp.dot(lower_panel, upper_rows, preferred_element_type=jnp.float32)]
    reshape x2 -> x0, local copies, waits for them, and re-layouts: 33.4 us -> none  [body(): return current.reshape(row_cycles, block_size, col_cycles, block_size)]
    scatter x2 -> x0, local copies, waits for them, and re-layouts: 33 us -> none  [body(): current = current.at[target].set(old_top, mode='drop')]
    unnamed x13 -> x40, local copies, waits for them, and re-layouts: 31.6 us -> 4.78 us
  transfers between devices with their start and end apart: 4 -> 37, of which waited for: 4 -> 8; matrix products, arithmetic and copies ran while one was open for 0% -> 12% of each run, Pallas kernels for 0% -> 28%
where the time goes in v1:
time: 209 us; the launch traced here: 207 us
  Pallas kernels  71 us (34%)
  waiting for transfers between devices  51.4 us (25%)
  starting transfers between devices  51.2 us (24%)
  other arithmetic  20.1 us (10%)
  local copies, waits for them, and re-layouts  12.8 us (6%)
    ppermute x15, waiting for transfers between devices, exchange(): received.append(lax.ppermute(out, 'row', hop_pairs(h)))  51.4 us
    pallas_call x4, Pallas kernels, update_columns(): pl.pallas_call(functools.partial(update_kernel, first), grid=(count,), in...  35.6 us
    pallas_call x5, Pallas kernels, gather_rows(): pl.pallas_call(gather_kernel, grid=(count,), in_specs=[pl.BlockSpec((slot...  23.4 us
    ppermute x15, starting transfers between devices, exchange(): received.append(lax.ppermute(out, 'row', hop_pairs(h)))  21.9 us
    ppermute x4, starting transfers between devices, send_panels(): down = lax.ppermute(cut, 'col', [(0, 2), (1, 3)])  12.7 us
    pallas_call x1, Pallas kernels, factor_panels(): pl.pallas_call(panel_kernel, in_specs=[pl.BlockSpec(memory_space=pltpu.SM...  12 us
    ppermute x2, starting transfers between devices, send_panels(): cross = lax.ppermute(own, 'col', [(0, 1), (1, 0)])  7.31 us
    unnamed x40, local copies, waits for them, and re-layouts  4.78 us
  transfers between devices with their start and end apart: 37, of which 8 were waited for; matrix products, arithmetic and copies ran while one was open for 12% of the time, Pallas kernels for 28%

profile of v1, /device:TPU:0, one launch (start us, length us, event | category | flops | bytes accessed | tf_op | source)
XLA Modules:
  0.0 207.3 jit_solution(13770922447956454073)
XLA Ops:
  2.7 1.6 fusion.12.rows_ref
  4.3 5.5 %gather_rows.8 = (bf16[4,256,256]{2,1,0:T(8,128)(2,1)}, bf16[4,256,256]{2,1,0:T(8,128)(2,1)}) custom-call(s32[512,1]{1,0:T(8,128)} %fusion.12.rows_ref, bf16[7,14,256,256]{3,2,1,0:T(8,128)(2,1)} %bitcast.41), custom_call_target="tpu_custom_call" | custom-call | flops 1879048192 | bytes 4718592 | tf_op jit(solution)/shard_map/gather_rows/pallas_call | solution.py:48
  10.3 2.6 %gather_rows.6 = (bf16[1,256,256]{2,1,0:T(8,128)(2,1)}, bf16[1,256,256]{2,1,0:T(8,128)(2,1)}) custom-call(s32[512,1]{1,0:T(8,128)} %fusion.12.rows_ref, bf16[7,14,256,256]{3,2,1,0:T(8,128)(2,1)} %bitcast.42), custom_call_target="tpu_custom_call" | custom-call | flops 469762048 | bytes 1179648 | tf_op jit(solution)/shard_map/gather_rows/pallas_call | solution.py:48
  12.9 4.4 %collective-permute-start.12 = (bf16[256,256]{1,0:T(8,128)(2,1)}, bf16[256,256]{1,0:T(8,128)(2,1)S(1)}, u32[]{:S(2)}, u32[]{:S(2)}) collective-permute-start(bf16[256,256]{1,0:T(8,128)(2,1)} %bitcast.58), channel_id=1, source_target_pairs={{0,2},{1,3},{4,6},{5,7},{8,10},{9,11},{12,14},{13,15},{16,18},{17,... | collective-permute-start | bytes 393224 | tf_op jit(solution)/shard_map/ppermute | solution.py:267
  19.6 3.4 %collective-permute-start.11 = (bf16[512,256]{1,0:T(8,128)(2,1)S(1)}, bf16[512,256]{1,0:T(8,128)(2,1)S(1)}, u32[]{:S(2)}, u32[]{:S(2)}) collective-permute-start(bf16[512,256]{1,0:T(8,128)(2,1)S(1)} %maximum_bitcast_fusion), channel_id=1, source_target_pairs={{0,1},{1,0},{4,5},{5,4},{8,9},{9,8},{12,13},{13,12},{16,17},{17,16... | collective-permute-start | bytes 786440 | tf_op jit(solution)/shard_map/ppermute | solution.py:261
  25.1 2.1 collective-permute-start.7
  27.2 2.9 %slice_bitcast_fusion = bf16[14,256,256]{2,1,0:T(8,128)(2,1)} fusion(bf16[7,14,256,256]{3,2,1,0:T(8,128)(2,1)} %bitcast.44), kind=kLoop, calls=%fused_computation.3 | loop fusion | bytes 3670016 | tf_op jit(solution)/shard_map/squeeze | solution.py:352
  30.8 4.9 %gather_rows.5 = (bf16[3,256,256]{2,1,0:T(8,128)(2,1)}, bf16[3,256,256]{2,1,0:T(8,128)(2,1)}) custom-call(s32[512,1]{1,0:T(8,128)} %fusion.12.rows_ref, bf16[7,14,256,256]{3,2,1,0:T(8,128)(2,1)} %bitcast.45), custom_call_target="tpu_custom_call" | custom-call | flops 1409286144 | bytes 3538944 | tf_op jit(solution)/shard_map/gather_rows/pallas_call | solution.py:48
  37.1 5.0 %collective-permute-start.8 = (bf16[896,256]{1,0:T(8,128)(2,1)S(1)}, bf16[896,256]{1,0:T(8,128)(2,1)}, u32[]{:S(2)}, u32[]{:S(2)}) collective-permute-start(bf16[896,256]{1,0:T(8,128)(2,1)S(1)} %get-tuple-element.64), channel_id=1, source_target_pairs={{0,2},{1,3},{4,6},{5,7},{8,10},{9,11},{12,14},{13,15},{16,18},{17,... | collective-permute-start | bytes 1376264 | tf_op jit(solution)/shard_map/ppermute | solution.py:267
  43.0 4.8 %gather_rows.7 = (bf16[3,256,256]{2,1,0:T(8,128)(2,1)}, bf16[3,256,256]{2,1,0:T(8,128)(2,1)}) custom-call(s32[512,1]{1,0:T(8,128)} %fusion.12.rows_ref, bf16[7,14,256,256]{3,2,1,0:T(8,128)(2,1)} %bitcast.46), custom_call_target="tpu_custom_call" | custom-call | flops 1409286144 | bytes 3538944 | tf_op jit(solution)/shard_map/gather_rows/pallas_call | solution.py:48
  47.9 5.6 %gather_rows.9 = (bf16[4,256,256]{2,1,0:T(8,128)(2,1)}, bf16[4,256,256]{2,1,0:T(8,128)(2,1)}) custom-call(s32[512,1]{1,0:T(8,128)} %fusion.12.rows_ref, bf16[7,14,256,256]{3,2,1,0:T(8,128)(2,1)} %bitcast.47), custom_call_target="tpu_custom_call" | custom-call | flops 1879048192 | bytes 4718592 | tf_op jit(solution)/shard_map/gather_rows/pallas_call | solution.py:48
  54.7 3.5 %collective-permute-start.17 = (bf16[2,256,256]{2,1,0:T(8,128)(2,1)}, bf16[2,256,256]{2,1,0:T(8,128)(2,1)S(1)}, u32[]{:S(2)}, u32[]{:S(2)}) collective-permute-start(bf16[2,256,256]{2,1,0:T(8,128)(2,1)} %fusion.14), channel_id=1, source_target_pairs={{0,8},{4,12},{24,16},{28,20},{1,9},{5,13},{25,17},{29,21},{2,10},{... | collective-permute-start | bytes 786440 | tf_op jit(solution)/shard_map/ppermute | solution.py:329
  62.1 3.9 %collective-permute-start.6 = (bf16[1792,256]{1,0:T(8,128)(2,1)S(1)}, bf16[1792,256]{1,0:T(8,128)(2,1)S(1)}, u32[]{:S(2)}, u32[]{:S(2)}) collective-permute-start(bf16[1792,256]{1,0:T(8,128)(2,1)S(1)} %bitcast.53), channel_id=1, source_target_pairs={{0,1},{1,0},{4,5},{5,4},{8,9},{9,8},{12,13},{13,12},{16,17},{17,16... | collective-permute-start | bytes 2752520 | tf_op jit(solution)/shard_map/ppermute | solution.py:261
  72.6 4.2 %collective-permute-done.1 = bf16[3,256,256]{2,1,0:T(8,128)(2,1)S(1)} collective-permute-done((bf16[3,256,256]{2,1,0:T(8,128)(2,1)S(1)}, bf16[3,256,256]{2,1,0:T(8,128)(2,1)S(1)}, u32[]{:S(2)}, u32[]{:S(2)}) %collective-permute-start.1) | collective-permute-done | bytes 393248 | tf_op jit(solution)/shard_map/ppermute | solution.py:329
  76.8 1.9 collective-permute-start.5
  78.7 5.3 %collective-permute-done.23 = bf16[3,256,256]{2,1,0:T(8,128)(2,1)S(1)} collective-permute-done((bf16[3,256,256]{2,1,0:T(8,128)(2,1)S(1)}, bf16[3,256,256]{2,1,0:T(8,128)(2,1)S(1)}, u32[]{:S(2)}, u32[]{:S(2)}) %collective-permute-start.23) | collective-permute-done | bytes 393248 | tf_op jit(solution)/shard_map/ppermute | solution.py:329
  84.0 4.4 %collective-permute-start.28 = (bf16[4,256,256]{2,1,0:T(8,128)(2,1)S(1)}, bf16[4,256,256]{2,1,0:T(8,128)(2,1)S(1)}, u32[]{:S(2)}, u32[]{:S(2)}) collective-permute-start(bf16[4,256,256]{2,1,0:T(8,128)(2,1)S(1)} %add.280), channel_id=1, source_target_pairs={{0,8},{4,12},{24,16},{28,20},{1,9},{5,13},{25,17},{29,21},{2,10},{... | collective-permute-start | bytes 1572872 | tf_op jit(solution)/shard_map/ppermute | solution.py:329
  93.2 7.6 %collective-permute-done.28 = bf16[4,256,256]{2,1,0:T(8,128)(2,1)S(1)} collective-permute-done((bf16[4,256,256]{2,1,0:T(8,128)(2,1)S(1)}, bf16[4,256,256]{2,1,0:T(8,128)(2,1)S(1)}, u32[]{:S(2)}, u32[]{:S(2)}) %collective-permute-start.28) | collective-permute-done | bytes 524320 | tf_op jit(solution)/shard_map/ppermute | solution.py:329
  101.5 8.4 %collective-permute-done.33 = bf16[4,256,256]{2,1,0:T(8,128)(2,1)S(1)} collective-permute-done((bf16[4,256,256]{2,1,0:T(8,128)(2,1)S(1)}, bf16[4,256,256]{2,1,0:T(8,128)(2,1)S(1)}, u32[]{:S(2)}, u32[]{:S(2)}) %collective-permute-start.33) | collective-permute-done | bytes 524320 | tf_op jit(solution)/shard_map/ppermute | solution.py:329
  114.4 12.6 %collective-permute-done.19 = bf16[2,256,256]{2,1,0:T(8,128)(2,1)S(1)} collective-permute-done((bf16[2,256,256]{2,1,0:T(8,128)(2,1)S(1)}, bf16[2,256,256]{2,1,0:T(8,128)(2,1)S(1)}, u32[]{:S(2)}, u32[]{:S(2)}) %collective-permute-start.19) | collective-permute-done | bytes 262176 | tf_op jit(solution)/shard_map/ppermute | solution.py:329
  129.4 1.9 collective-permute-start.21
  133.0 2.4 %collective-permute-done.25 = bf16[3,256,256]{2,1,0:T(8,128)(2,1)S(1)} collective-permute-done((bf16[3,256,256]{2,1,0:T(8,128)(2,1)S(1)}, bf16[3,256,256]{2,1,0:T(8,128)(2,1)S(1)}, u32[]{:S(2)}, u32[]{:S(2)}) %collective-permute-start.25) | collective-permute-done | bytes 393248 | tf_op jit(solution)/shard_map/ppermute | solution.py:329
  136.7 3.8 %collective-permute-done.3 = bf16[3,256,256]{2,1,0:T(8,128)(2,1)S(1)} collective-permute-done((bf16[3,256,256]{2,1,0:T(8,128)(2,1)S(1)}, bf16[3,256,256]{2,1,0:T(8,128)(2,1)S(1)}, u32[]{:S(2)}, u32[]{:S(2)}) %collective-permute-start.3) | collective-permute-done | bytes 393248 | tf_op jit(solution)/shard_map/ppermute | solution.py:329
  140.6 1.5 collective-permute-start.35
  142.0 1.6 broadcast_select_fusion.8
  145.2 12.0 %factor_panels.1 = (bf16[7,256,256]{2,1,0:T(8,128)(2,1)}, bf16[7,256,256]{2,1,0:T(8,128)(2,1)}, bf16[256,256]{1,0:T(8,128)(2,1)}, bf16[7,256,512]{2,1,0:T(8,128)(2,1)}, f32[7,256,1]{2,1,0:T(8,128)}) custom-call(s32[3]{0:T(128)} %pad_add_fusion.7.place, s32[1,512]{1,0:T(1,128)} %broadcast_select_fusion.21.slot_ref, s32[256,1]{1,0:T(8,128)} %copy.40.me_ref, ...), custom_call_target="tpu_custom_call" | custom-call | flops 8000000000 | bytes 8000000 | tf_op jit(solution)/shard_map/factor_panels/pallas_call | solution.py:159
  157.2 7.0 %collective-permute-done.35 = bf16[4,256,256]{2,1,0:T(8,128)(2,1)} collective-permute-done((bf16[4,256,256]{2,1,0:T(8,128)(2,1)}, bf16[4,256,256]{2,1,0:T(8,128)(2,1)}, u32[]{:S(2)}, u32[]{:S(2)}) %collective-permute-start.35) | collective-permute-done | bytes 524320 | tf_op jit(solution)/shard_map/ppermute | solution.py:329
  164.2 2.5 %broadcast_select_fusion = (bf16[4,256,256]{2,1,0:T(8,128)(2,1)S(1)}, bf16[4,256,256]{2,1,0:T(8,128)(2,1)S(1)}, bf16[4,256,256]{2,1,0:T(8,128)(2,1)S(1)}, bf16[4...) fusion(pred[256]{0:T(512)(128)(4,1)S(1)} %get-tuple-element.74, ...), kind=kLoop, calls=%fused_computation.14 | loop fusion | flops 3670016 | bytes 7341059 | tf_op jit(solution)/shard_map/jit(_where)/select_n | solution.py:339
  170.9 9.7 %update_columns.4.rest_0_ = bf16[7,14,256,256]{3,2,1,0:T(8,128)(2,1)} custom-call(s32[3]{0:T(128)} %pad_add_fusion.7.place, s32[256,1]{1,0:T(8,128)} %copy.40.me_ref, bf16[7,14,256,256]{3,2,1,0:T(8,128)(2,1)} %bitcast.48, bf16[4,256,256]{2,1,0:T(8,128)(2,1)} %copy-done.2, bf16[4,256,256]{2,1,0:T(8,128)(2,1)} %get-tuple-element.88.xm_ref, ...), custom_call_target="tpu_custom_call" | custom-call | flops 3758096384 | bytes 7340032 | tf_op jit(solution)/shard_map/update_columns/pallas_call | solution.py:229
  181.4 9.6 %update_columns.5.rest_0_ = bf16[7,14,256,256]{3,2,1,0:T(8,128)(2,1)} custom-call(s32[3]{0:T(128)} %pad_add_fusion.7.place, s32[256,1]{1,0:T(8,128)} %copy.40.me_ref, bf16[7,14,256,256]{3,2,1,0:T(8,128)(2,1)} %bitcast.49, bf16[4,256,256]{2,1,0:T(8,128)(2,1)} %copy-done.1, ...), custom_call_target="tpu_custom_call", output_to_operand_aliasing={{}: (13, {})} | custom-call | flops 3758096384 | bytes 7340032 | tf_op jit(solution)/shard_map/update_columns/pallas_call | solution.py:229
  191.0 8.1 %update_columns.6.rest_0_ = bf16[7,14,256,256]{3,2,1,0:T(8,128)(2,1)} custom-call(s32[3]{0:T(128)} %pad_add_fusion.7.place, s32[256,1]{1,0:T(8,128)} %copy.40.me_ref, bf16[7,14,256,256]{3,2,1,0:T(8,128)(2,1)} %bitcast.50, bf16[3,256,256]{2,1,0:T(8,128)(2,1)} %copy-done.4, ...), custom_call_target="tpu_custom_call", output_to_operand_aliasing={{}: (13, {})} | custom-call | flops 2818572288 | bytes 5505024 | tf_op jit(solution)/shard_map/update_columns/pallas_call | solution.py:229
  199.2 8.2 %update_columns.7 = bf16[7,14,256,256]{3,2,1,0:T(8,128)(2,1)} custom-call(s32[3]{0:T(128)} %pad_add_fusion.7.place, s32[256,1]{1,0:T(8,128)} %copy.40.me_ref, bf16[7,14,256,256]{3,2,1,0:T(8,128)(2,1)} %bitcast.51, bf16[3,256,256]{2,1,0:T(8,128)(2,1)} %copy-done.3, bf16[3,256,256]{2,1,0:T(8,128)(2,1)} %get-tuple-element.95.xm_ref, ...), custom_call_target="tpu_custom_call", output_to_operand_aliasing={{}: (13, {})} | custom-call | flops 2818572288 | bytes 5505024 | tf_op jit(solution)/shard_map/update_columns/pallas_call | solution.py:229
  (153 shorter events, 43.6 us)
Async XLA Ops:
  9.9 57.4 %collective-permute-start.27 = (bf16[4,256,256]{2,1,0:T(8,128)(2,1)}, bf16[4,256,256]{2,1,0:T(8,128)(2,1)S(1)}, u32[]{:S(2)}, u32[]{:S(2)}) collective-permute-start(bf16[4,256,256]{2,1,0:T(8,128)(2,1)} %get-tuple-element.32.own_ref), channel_id=1, source_target_pairs={{0,4},{4,0},{8,12},{12,8},{16,20},{20,16},{24,28},{28,24},{1,5},{5... | collective-permute-start | bytes 1572872 | tf_op jit(solution)/shard_map/ppermute | solution.py:324
  12.9 22.8 %collective-permute-start.12 = (bf16[256,256]{1,0:T(8,128)(2,1)}, bf16[256,256]{1,0:T(8,128)(2,1)S(1)}, u32[]{:S(2)}, u32[]{:S(2)}) collective-permute-start(bf16[256,256]{1,0:T(8,128)(2,1)} %bitcast.58), channel_id=1, source_target_pairs={{0,2},{1,3},{4,6},{5,7},{8,10},{9,11},{12,14},{13,15},{16,18},{17,... | collective-permute-start | bytes 393224 | tf_op jit(solution)/shard_map/ppermute | solution.py:267
  17.3 19.0 %collective-permute-start.13 = (bf16[256,256]{1,0:T(8,128)(2,1)}, bf16[256,256]{1,0:T(8,128)(2,1)S(1)}, u32[]{:S(2)}, u32[]{:S(2)}) collective-permute-start(bf16[256,256]{1,0:T(8,128)(2,1)} %bitcast.59), channel_id=1, source_target_pairs={{0,2},{1,3},{4,6},{5,7},{8,10},{9,11},{12,14},{13,15},{16,18},{17,... | collective-permute-start | bytes 393224 | tf_op jit(solution)/shard_map/ppermute | solution.py:267
  19.6 22.5 %collective-permute-start.11 = (bf16[512,256]{1,0:T(8,128)(2,1)S(1)}, bf16[512,256]{1,0:T(8,128)(2,1)S(1)}, u32[]{:S(2)}, u32[]{:S(2)}) collective-permute-start(bf16[512,256]{1,0:T(8,128)(2,1)S(1)} %maximum_bitcast_fusion), channel_id=1, source_target_pairs={{0,1},{1,0},{4,5},{5,4},{8,9},{9,8},{12,13},{13,12},{16,17},{17,16... | collective-permute-start | bytes 786440 | tf_op jit(solution)/shard_map/ppermute | solution.py:261
  25.1 36.9 %collective-permute-start.7 = (bf16[896,256]{1,0:T(8,128)(2,1)}, bf16[896,256]{1,0:T(8,128)(2,1)}, u32[]{:S(2)}, u32[]{:S(2)}) collective-permute-start(bf16[896,256]{1,0:T(8,128)(2,1)} %get-tuple-element.65), channel_id=1, source_target_pairs={{0,2},{1,3},{4,6},{5,7},{8,10},{9,11},{12,14},{13,15},{16,18},{17,... | collective-permute-start | bytes 1376264 | tf_op jit(solution)/shard_map/ppermute | solution.py:267
  37.1 28.9 %collective-permute-start.8 = (bf16[896,256]{1,0:T(8,128)(2,1)S(1)}, bf16[896,256]{1,0:T(8,128)(2,1)}, u32[]{:S(2)}, u32[]{:S(2)}) collective-permute-start(bf16[896,256]{1,0:T(8,128)(2,1)S(1)} %get-tuple-element.64), channel_id=1, source_target_pairs={{0,2},{1,3},{4,6},{5,7},{8,10},{9,11},{12,14},{13,15},{16,18},{17,... | collective-permute-start | bytes 1376264 | tf_op jit(solution)/shard_map/ppermute | solution.py:267
  42.4 11.0 %collective-permute-start.16 = (bf16[2,256,256]{2,1,0:T(8,128)(2,1)S(1)}, bf16[2,256,256]{2,1,0:T(8,128)(2,1)S(1)}, u32[]{:S(2)}, u32[]{:S(2)}) collective-permute-start(bf16[2,256,256]{2,1,0:T(8,128)(2,1)S(1)} %pad_maximum_fusion.1.own_ref), channel_id=1, source_target_pairs={{0,4},{4,0},{8,12},{12,8},{16,20},{20,16},{24,28},{28,24},{1,5},{5... | collective-permute-start | bytes 786440 | tf_op jit(solution)/shard_map/ppermute | solution.py:324
  53.5 17.4 %collective-permute-start.32 = (bf16[4,256,256]{2,1,0:T(8,128)(2,1)}, bf16[4,256,256]{2,1,0:T(8,128)(2,1)S(1)}, u32[]{:S(2)}, u32[]{:S(2)}) collective-permute-start(bf16[4,256,256]{2,1,0:T(8,128)(2,1)} %get-tuple-element.34.own_ref), channel_id=1, source_target_pairs={{0,4},{4,0},{8,12},{12,8},{16,20},{20,16},{24,28},{28,24},{1,5},{5... | collective-permute-start | bytes 1572872 | tf_op jit(solution)/shard_map/ppermute | solution.py:324
  54.7 17.0 %collective-permute-start.17 = (bf16[2,256,256]{2,1,0:T(8,128)(2,1)}, bf16[2,256,256]{2,1,0:T(8,128)(2,1)S(1)}, u32[]{:S(2)}, u32[]{:S(2)}) collective-permute-start(bf16[2,256,256]{2,1,0:T(8,128)(2,1)} %fusion.14), channel_id=1, source_target_pairs={{0,8},{4,12},{24,16},{28,20},{1,9},{5,13},{25,17},{29,21},{2,10},{... | collective-permute-start | bytes 786440 | tf_op jit(solution)/shard_map/ppermute | solution.py:329
  62.1 28.7 %collective-permute-start.6 = (bf16[1792,256]{1,0:T(8,128)(2,1)S(1)}, bf16[1792,256]{1,0:T(8,128)(2,1)S(1)}, u32[]{:S(2)}, u32[]{:S(2)}) collective-permute-start(bf16[1792,256]{1,0:T(8,128)(2,1)S(1)} %bitcast.53), channel_id=1, source_target_pairs={{0,1},{1,0},{4,5},{5,4},{8,9},{9,8},{12,13},{13,12},{16,17},{17,16... | collective-permute-start | bytes 2752520 | tf_op jit(solution)/shard_map/ppermute | solution.py:261
  66.0 10.8 %collective-permute-start.1 = (bf16[3,256,256]{2,1,0:T(8,128)(2,1)S(1)}, bf16[3,256,256]{2,1,0:T(8,128)(2,1)S(1)}, u32[]{:S(2)}, u32[]{:S(2)}) collective-permute-start(bf16[3,256,256]{2,1,0:T(8,128)(2,1)S(1)} %add.268), channel_id=1, source_target_pairs={{0,8},{4,12},{24,16},{28,20},{1,9},{5,13},{25,17},{29,21},{2,10},{... | collective-permute-start | bytes 1179656 | tf_op jit(solution)/shard_map/ppermute | solution.py:329
  67.3 16.7 %collective-permute-start.23 = (bf16[3,256,256]{2,1,0:T(8,128)(2,1)S(1)}, bf16[3,256,256]{2,1,0:T(8,128)(2,1)S(1)}, u32[]{:S(2)}, u32[]{:S(2)}) collective-permute-start(bf16[3,256,256]{2,1,0:T(8,128)(2,1)S(1)} %add.279), channel_id=1, source_target_pairs={{0,8},{4,12},{24,16},{28,20},{1,9},{5,13},{25,17},{29,21},{2,10},{... | collective-permute-start | bytes 1179656 | tf_op jit(solution)/shard_map/ppermute | solution.py:329
  70.9 17.7 %collective-permute-start.9 = (bf16[896,256]{1,0:T(8,128)(2,1)}, bf16[896,256]{1,0:T(8,128)(2,1)S(1)}, u32[]{:S(2)}, u32[]{:S(2)}) collective-permute-start(bf16[896,256]{1,0:T(8,128)(2,1)} %collective-permute-done.7), channel_id=1, source_target_pairs={{2,3},{3,2},{6,7},{7,6},{10,11},{11,10},{14,15},{15,14},{18,19},{1... | collective-permute-start | bytes 1376264 | tf_op jit(solution)/shard_map/ppermute | solution.py:268
  71.8 18.2 %collective-permute-start.10 = (bf16[896,256]{1,0:T(8,128)(2,1)}, bf16[896,256]{1,0:T(8,128)(2,1)S(1)}, u32[]{:S(2)}, u32[]{:S(2)}) collective-permute-start(bf16[896,256]{1,0:T(8,128)(2,1)} %collective-permute-done.8), channel_id=1, source_target_pairs={{2,3},{3,2},{6,7},{7,6},{10,11},{11,10},{14,15},{15,14},{18,19},{1... | collective-permute-start | bytes 1376264 | tf_op jit(solution)/shard_map/ppermute | solution.py:268
  76.8 92.7 %collective-permute-start.5 = (bf16[14,256,256]{2,1,0:T(8,128)(2,1)}, bf16[14,256,256]{2,1,0:T(8,128)(2,1)S(1)}, u32[]{:S(2)}, u32[]{:S(2)}) collective-permute-start(bf16[14,256,256]{2,1,0:T(8,128)(2,1)} %slice_bitcast_fusion), channel_id=1, source_target_pairs={{0,4},{4,0},{1,5},{5,1},{2,6},{6,2},{3,7},{7,3}} | collective-permute-start | bytes 5505032 | tf_op jit(solution)/shard_map/ppermute | solution.py:352
  84.0 16.8 %collective-permute-start.28 = (bf16[4,256,256]{2,1,0:T(8,128)(2,1)S(1)}, bf16[4,256,256]{2,1,0:T(8,128)(2,1)S(1)}, u32[]{:S(2)}, u32[]{:S(2)}) collective-permute-start(bf16[4,256,256]{2,1,0:T(8,128)(2,1)S(1)} %add.280), channel_id=1, source_target_pairs={{0,8},{4,12},{24,16},{28,20},{1,9},{5,13},{25,17},{29,21},{2,10},{... | collective-permute-start | bytes 1572872 | tf_op jit(solution)/shard_map/ppermute | solution.py:329
  88.6 21.3 %collective-permute-start.33 = (bf16[4,256,256]{2,1,0:T(8,128)(2,1)S(1)}, bf16[4,256,256]{2,1,0:T(8,128)(2,1)S(1)}, u32[]{:S(2)}, u32[]{:S(2)}) collective-permute-start(bf16[4,256,256]{2,1,0:T(8,128)(2,1)S(1)} %add.281), channel_id=1, source_target_pairs={{0,8},{4,12},{24,16},{28,20},{1,9},{5,13},{25,17},{29,21},{2,10},{... | collective-permute-start | bytes 1572872 | tf_op jit(solution)/shard_map/ppermute | solution.py:329
  90.0 20.8 %collective-permute-start.18 = (bf16[2,256,256]{2,1,0:T(8,128)(2,1)S(1)}, bf16[2,256,256]{2,1,0:T(8,128)(2,1)S(1)}, u32[]{:S(2)}, u32[]{:S(2)}) collective-permute-start(bf16[2,256,256]{2,1,0:T(8,128)(2,1)S(1)} %broadcast_select_fusion.19), channel_id=1, source_target_pairs={{8,16},{12,20},{16,8},{20,12},{9,17},{13,21},{17,9},{21,13},{10,18... | collective-permute-start | bytes 786440 | tf_op jit(solution)/shard_map/ppermute | solution.py:329
  90.7 20.9 %collective-permute-start.2 = (bf16[3,256,256]{2,1,0:T(8,128)(2,1)S(1)}, bf16[3,256,256]{2,1,0:T(8,128)(2,1)S(1)}, u32[]{:S(2)}, u32[]{:S(2)}) collective-permute-start(bf16[3,256,256]{2,1,0:T(8,128)(2,1)S(1)} %get-tuple-element.99), channel_id=1, source_target_pairs={{8,16},{12,20},{16,8},{20,12},{9,17},{13,21},{17,9},{21,13},{10,18... | collective-permute-start | bytes 1179656 | tf_op jit(solution)/shard_map/ppermute | solution.py:329
  100.8 12.1 %collective-permute-start.24 = (bf16[3,256,256]{2,1,0:T(8,128)(2,1)S(1)}, bf16[3,256,256]{2,1,0:T(8,128)(2,1)S(1)}, u32[]{:S(2)}, u32[]{:S(2)}) collective-permute-start(bf16[3,256,256]{2,1,0:T(8,128)(2,1)S(1)} %get-tuple-element.98), channel_id=1, source_target_pairs={{8,16},{12,20},{16,8},{20,12},{9,17},{13,21},{17,9},{21,13},{10,18... | collective-permute-start | bytes 1179656 | tf_op jit(solution)/shard_map/ppermute | solution.py:329
  110.1 19.3 %collective-permute-start.29 = (bf16[4,256,256]{2,1,0:T(8,128)(2,1)S(1)}, bf16[4,256,256]{2,1,0:T(8,128)(2,1)S(1)}, u32[]{:S(2)}, u32[]{:S(2)}) collective-permute-start(bf16[4,256,256]{2,1,0:T(8,128)(2,1)S(1)} %get-tuple-element.93), channel_id=1, source_target_pairs={{8,16},{12,20},{16,8},{20,12},{9,17},{13,21},{17,9},{21,13},{10,18... | collective-permute-start | bytes 1572872 | tf_op jit(solution)/shard_map/ppermute | solution.py:329
  110.8 20.6 %collective-permute-start.34 = (bf16[4,256,256]{2,1,0:T(8,128)(2,1)S(1)}, bf16[4,256,256]{2,1,0:T(8,128)(2,1)S(1)}, u32[]{:S(2)}, u32[]{:S(2)}) collective-permute-start(bf16[4,256,256]{2,1,0:T(8,128)(2,1)S(1)} %get-tuple-element.92), channel_id=1, source_target_pairs={{8,16},{12,20},{16,8},{20,12},{9,17},{13,21},{17,9},{21,13},{10,18... | collective-permute-start | bytes 1572872 | tf_op jit(solution)/shard_map/ppermute | solution.py:329
  111.6 15.4 %collective-permute-start.19 = (bf16[2,256,256]{2,1,0:T(8,128)(2,1)S(1)}, bf16[2,256,256]{2,1,0:T(8,128)(2,1)S(1)}, u32[]{:S(2)}, u32[]{:S(2)}) collective-permute-start(bf16[2,256,256]{2,1,0:T(8,128)(2,1)S(1)} %broadcast_select_fusion.18), channel_id=1, source_target_pairs={{16,24},{20,28},{8,0},{12,4},{17,25},{21,29},{9,1},{13,5},{18,26},... | collective-permute-start | bytes 786440 | tf_op jit(solution)/shard_map/ppermute | solution.py:329
  113.1 22.4 %collective-permute-start.25 = (bf16[3,256,256]{2,1,0:T(8,128)(2,1)S(1)}, bf16[3,256,256]{2,1,0:T(8,128)(2,1)S(1)}, u32[]{:S(2)}, u32[]{:S(2)}) collective-permute-start(bf16[3,256,256]{2,1,0:T(8,128)(2,1)S(1)} %get-tuple-element.96), channel_id=1, source_target_pairs={{16,24},{20,28},{8,0},{12,4},{17,25},{21,29},{9,1},{13,5},{18,26},... | collective-permute-start | bytes 1179656 | tf_op jit(solution)/shard_map/ppermute | solution.py:329
  127.0 13.5 %collective-permute-start.3 = (bf16[3,256,256]{2,1,0:T(8,128)(2,1)S(1)}, bf16[3,256,256]{2,1,0:T(8,128)(2,1)S(1)}, u32[]{:S(2)}, u32[]{:S(2)}) collective-permute-start(bf16[3,256,256]{2,1,0:T(8,128)(2,1)S(1)} %get-tuple-element.97), channel_id=1, source_target_pairs={{16,24},{20,28},{8,0},{12,4},{17,25},{21,29},{9,1},{13,5},{18,26},... | collective-permute-start | bytes 1179656 | tf_op jit(solution)/shard_map/ppermute | solution.py:329
  129.4 14.3 %collective-permute-start.21 = (bf16[2,256,256]{2,1,0:T(8,128)(2,1)S(1)}, bf16[2,256,256]{2,1,0:T(8,128)(2,1)S(1)}, u32[]{:S(2)}, u32[]{:S(2)}) collective-permute-start(bf16[2,256,256]{2,1,0:T(8,128)(2,1)S(1)} %fusion.18), channel_id=1, source_target_pairs={{0,4},{4,0},{1,5},{5,1},{2,6},{6,2},{3,7},{7,3}} | collective-permute-start | bytes 786440 | tf_op jit(solution)/shard_map/ppermute | solution.py:348
  131.3 12.4 %collective-permute-start.20 = (bf16[2,256,256]{2,1,0:T(8,128)(2,1)S(1)}, bf16[2,256,256]{2,1,0:T(8,128)(2,1)S(1)}, u32[]{:S(2)}, u32[]{:S(2)}) collective-permute-start(bf16[2,256,256]{2,1,0:T(8,128)(2,1)S(1)} %get-tuple-element.46), channel_id=1, source_target_pairs={{0,4},{4,0},{8,12},{12,8},{16,20},{20,16},{24,28},{28,24},{1,5},{5... | collective-permute-start | bytes 786440 | tf_op jit(solution)/shard_map/ppermute | solution.py:340
  135.5 21.8 %collective-permute-start.30 = (bf16[4,256,256]{2,1,0:T(8,128)(2,1)}, bf16[4,256,256]{2,1,0:T(8,128)(2,1)S(1)}, u32[]{:S(2)}, u32[]{:S(2)}) collective-permute-start(bf16[4,256,256]{2,1,0:T(8,128)(2,1)} %get-tuple-element.91), channel_id=1, source_target_pairs={{16,24},{20,28},{8,0},{12,4},{17,25},{21,29},{9,1},{13,5},{18,26},... | collective-permute-start | bytes 1572872 | tf_op jit(solution)/shard_map/ppermute | solution.py:329
  140.6 23.7 %collective-permute-start.35 = (bf16[4,256,256]{2,1,0:T(8,128)(2,1)}, bf16[4,256,256]{2,1,0:T(8,128)(2,1)}, u32[]{:S(2)}, u32[]{:S(2)}) collective-permute-start(bf16[4,256,256]{2,1,0:T(8,128)(2,1)} %get-tuple-element.90), channel_id=1, source_target_pairs={{16,24},{20,28},{8,0},{12,4},{17,25},{21,29},{9,1},{13,5},{18,26},... | collective-permute-start | bytes 1572872 | tf_op jit(solution)/shard_map/ppermute | solution.py:329
  143.7 47.3 %collective-permute-start.26 = (bf16[3,256,256]{2,1,0:T(8,128)(2,1)}, bf16[3,256,256]{2,1,0:T(8,128)(2,1)}, u32[]{:S(2)}, u32[]{:S(2)}) collective-permute-start(bf16[3,256,256]{2,1,0:T(8,128)(2,1)} %get-tuple-element.43), channel_id=1, source_target_pairs={{0,4},{4,0},{8,12},{12,8},{16,20},{20,16},{24,28},{28,24},{1,5},{5... | collective-permute-start | bytes 1179656 | tf_op jit(solution)/shard_map/ppermute | solution.py:340
  145.2 54.0 %collective-permute-start.4 = (bf16[3,256,256]{2,1,0:T(8,128)(2,1)}, bf16[3,256,256]{2,1,0:T(8,128)(2,1)}, u32[]{:S(2)}, u32[]{:S(2)}) collective-permute-start(bf16[3,256,256]{2,1,0:T(8,128)(2,1)} %get-tuple-element.69), channel_id=1, source_target_pairs={{0,4},{4,0},{8,12},{12,8},{16,20},{20,16},{24,28},{28,24},{1,5},{5... | collective-permute-start | bytes 1179656 | tf_op jit(solution)/shard_map/ppermute | solution.py:340
  167.9 12.6 %collective-permute-start.31 = (bf16[4,256,256]{2,1,0:T(8,128)(2,1)}, bf16[4,256,256]{2,1,0:T(8,128)(2,1)S(1)}, u32[]{:S(2)}, u32[]{:S(2)}) collective-permute-start(bf16[4,256,256]{2,1,0:T(8,128)(2,1)} %get-tuple-element.66), channel_id=1, source_target_pairs={{0,4},{4,0},{8,12},{12,8},{16,20},{20,16},{24,28},{28,24},{1,5},{5... | collective-permute-start | bytes 1572872 | tf_op jit(solution)/shard_map/ppermute | solution.py:340
  (23 other events, 157.2 us)

commit v2 on v0

v2 whole, which is shorter than its diff:
```python
import functools

import jax
import jax.numpy as jnp
from jax import lax
from jax.experimental import pallas as pl
from jax.experimental.pallas import tpu as pltpu
from jax.sharding import PartitionSpec as P

STEPS = 2
NEWTON = 3
F32 = jnp.float32
BF16 = jnp.bfloat16
I32 = jnp.int32
VMEM_LIMIT = 24 * 1024 * 1024
CHEAP = pl.CostEstimate(flops=1024, bytes_accessed=1024, transcendentals=0)
ANY = pl.BlockSpec(memory_space=pl.ANY)
SMEM = pl.BlockSpec(memory_space=pltpu.SMEM)
VMEM = pl.BlockSpec(memory_space=pltpu.VMEM)


def dot(a, b):
    return jnp.dot(a, b, preferred_element_type=F32)


def dot_full(a, b):
    return jnp.dot(a, b, precision=lax.Precision.HIGHEST, preferred_element_type=F32)


def params():
    return pltpu.CompilerParams(vmem_limit_bytes=VMEM_LIMIT)


def iota(shape, dim):
    return lax.broadcasted_iota(I32, shape, dim)


def to_column(row):
    size = row.shape[1]
    diagonal = iota((size, size), 0) == iota((size, size), 1)
    return jnp.sum(jnp.where(diagonal, row.astype(F32), 0.0), axis=1, keepdims=True).astype(I32)


def to_row(column):
    size = column.shape[0]
    diagonal = iota((size, size), 0) == iota((size, size), 1)
    return jnp.sum(jnp.where(diagonal, column.astype(F32), 0.0), axis=0, keepdims=True).astype(I32)


def pick_sum(mask, value, axis):
    return jnp.sum(jnp.where(mask, value.astype(F32), 0.0), axis=axis, keepdims=True).astype(I32)


def start_kernel(
    rows, place, pivot_ref, block_ref,
    onehot_ref, owner_ref, me_ref, lands_ref, raw_a_ref, raw_b_ref, mine_ref, other_ref, token_ref,
):
    cycles, width, size, _ = block_ref.shape
    chip, core = place[0], place[1]
    row = 2 * chip + core

    @pl.when(pl.program_id(0) == 0)
    def _():
        square = (size, size)
        pivot0, pivot1 = pivot_ref[0:1], pivot_ref[1:2]
        column0 = to_column(pivot0)
        down, across = iota(square, 0), iota(square, 1)
        again = column0 == pivot1
        inner = column0 == across + size
        at = iota((1, size), 1)
        second = size + at + pick_sum(inner, down - across - size, 0)
        source1 = pivot1 + pick_sum(again, down - pivot1, 0)
        leaves0 = iota((size, 1), 0) + pick_sum(again, second - down, 1)
        device_of = lambda r: r // size % rows
        local_of = lambda r: r // (size * rows) * size + r % size

        def of_slots(source, leaves):
            device = device_of(source)
            owner = device // 2
            me = device == row
            come = jnp.where(jnp.logical_and(chip == 0, owner != 0), leaves, source)
            taken = jnp.where(device_of(come) == row, local_of(come), -1)
            return owner, me.astype(I32), taken

        first = of_slots(column0, leaves0)
        last = of_slots(to_column(source1), to_column(second))
        swapped = core == 1
        mine = [jnp.where(swapped, b, a) for a, b in zip(first, last)]
        other = [jnp.where(swapped, a, b) for a, b in zip(first, last)]
        for half, values in enumerate((mine, other)):
            owner_ref[half] = values[0]
            me_ref[half] = values[1]
            for cycle in range(cycles):
                hit = values[2] == across + cycle * size
                onehot_ref[half * size : (half + 1) * size, cycle * size : (cycle + 1) * size] = (
                    jnp.where(hit, 1.0, 0.0).astype(BF16)
                )

        slots = STEPS * size
        lands = []
        for source in (pivot0, source1):
            outside = jnp.logical_and(device_of(source) == row, source >= slots)
            lands.append(jnp.where(outside, local_of(source), -1))
        by_top = []
        leaving = (leaves0, to_column(second))
        landing = [to_column(v) for v in lands]
        for half in range(2):
            total = jnp.full((1, size), -1, I32)
            for leave, land in zip(leaving, landing):
                total += pick_sum(leave == across + half * size, land + 1, 0)
            by_top.append(total)
        lands = [jnp.where(chip == 0, a, b) for a, b in zip(by_top, lands)]
        lands_ref[0:1] = jnp.where(swapped, lands[1], lands[0])
        lands_ref[1:2] = jnp.where(swapped, lands[0], lands[1])
        half = raw_a_ref.shape[0]
        raw_a_ref[...] = block_ref[:half, 0]
        raw_b_ref[...] = block_ref[half:, 0]

    gather_step(onehot_ref, block_ref, mine_ref, other_ref)


def gather_step(onehot_ref, block_ref, mine_ref, other_ref):
    cycles, width, size, _ = block_ref.shape
    columns = [
        jnp.concatenate([block_ref[cycle, b] for cycle in range(cycles)], 0) for b in range(width)
    ]
    columns = columns[0] if width == 1 else jnp.concatenate(columns, 1)
    total = dot(onehot_ref[...], columns).astype(BF16)
    for b in range(width):
        mine_ref[b] = total[:size, b * size : (b + 1) * size]
        other_ref[b] = total[size:, b * size : (b + 1) * size]


def constant(shape):
    return pl.BlockSpec(
        shape, lambda *j, n=len(shape): (0,) * n, pipeline_mode=pl.Buffered(1)
    )


def array(*shape, dtype=BF16):
    return jax.ShapeDtypeStruct(shape, dtype)


TOKEN = array(8, 128, dtype=F32)


def start(place, pivots, matrix, count, width, rows):
    cycles, _, size, _ = matrix.shape
    slots = STEPS * size
    half = (cycles + 1) // 2
    part = array(count, size, size)
    part_spec = pl.BlockSpec((width, size, size), lambda j: (j, 0, 0))
    outs = [
        array(slots, cycles * size),
        array(2, size, 1, dtype=I32),
        array(2, size, 1, dtype=I32),
        array(2, size, dtype=I32),
        array(half, size, size),
        array(cycles - half, size, size),
    ]
    return pl.pallas_call(
        functools.partial(start_kernel, rows),
        grid=(count // width,),
        in_specs=[
            SMEM,
            constant(pivots.shape),
            pl.BlockSpec((cycles, width, size, size), lambda j: (0, j, 0, 0)),
        ],
        out_specs=[constant(o.shape) for o in outs] + [part_spec, part_spec, ANY],
        out_shape=outs + [part, part, TOKEN],
        compiler_params=params(),
        cost_estimate=CHEAP,
        name="start",
    )(place, pivots, matrix)


class Chain:
    def __init__(self, token):
        self.token = token
        self.due = []

    def need(self, *arrays):
        self.due += arrays

    def run(self, kernel, name, operands, in_specs, out_shape, out_specs, **options):
        operands, in_specs = list(operands), list(in_specs)
        given, made = len(operands), len(out_shape)
        waits = [self.token, *self.due]
        self.due = []

        def body(*refs):
            kernel(*refs[:given], *refs[given + len(waits) : given + len(waits) + made], *refs[given + len(waits) + made + 1 :])

        *outs, self.token = pl.pallas_call(
            body,
            in_specs=in_specs + [ANY] * len(waits),
            out_specs=list(out_specs) + [ANY],
            out_shape=list(out_shape) + [TOKEN],
            compiler_params=params(),
            cost_estimate=CHEAP,
            name=name,
            **options,
        )(*operands, *waits)
        return outs

    def whole(self, kernel, name, place, operands, out_shape, **options):
        return self.run(
            kernel,
            name,
            (place, *operands),
            [SMEM] + [VMEM] * len(operands),
            out_shape,
            [VMEM] * len(out_shape),
            **options,
        )


def gather_rows(chain, matrix, onehot, first, count, width):
    cycles, _, size, _ = matrix.shape
    part = array(count, size, size)
    part_spec = pl.BlockSpec((width, size, size), lambda j: (j, 0, 0))
    return chain.run(
        gather_step,
        "gather_rows",
        (onehot, matrix),
        [
            constant(onehot.shape),
            pl.BlockSpec((cycles, width, size, size), lambda j: (0, j + first // width, 0, 0)),
        ],
        [part, part],
        [part_spec, part_spec],
        grid=(count // width,),
    )


def meet_kernel(place, mine_ref, theirs_ref, out_ref):
    out_ref[...] = mine_ref[...] + theirs_ref[...]


def merge_kernel(place, owner_ref, native_ref, received_ref, out_ref):
    own = jnp.logical_or(place[0] == 0, owner_ref[0] == place[0])
    for b in range(out_ref.shape[0]):
        out_ref[b] = jnp.where(own, native_ref[b], received_ref[b])


def finish_kernel(place, owner_ref, me_ref, native_ref, *refs):
    *received, mine_ref, send_ref = refs
    chips = len(received) + 1
    chip = place[0]
    owner = owner_ref[0]
    me = me_ref[0] != 0
    passed = jnp.logical_and(owner == chip, chip != 0)
    passed_mine = jnp.logical_and(passed, me)
    passed_other = jnp.logical_and(passed, jnp.logical_not(me))
    for at in range(chips):

        @pl.when(chip == at)
        def _(at=at):
            for b in range(native_ref.shape[0]):
                native = native_ref[b]
                left = received[at - 1][b] if at > 0 else native
                right = received[chips - 2 - at][b] if at < chips - 1 else native
                new = jnp.where(owner < chip, left, jnp.where(owner > chip, right, native))
                mine_ref[b] = jnp.where(passed_mine, left, new)
                send_ref[b] = jnp.where(passed_other, left, new)


def side_kernel(place, own_ref, down_ref, out_ref):
    out_ref[...] = jnp.where(place[2] < 2, own_ref[...], down_ref[...])


def pair_kernel(place, own_ref, down_ref, side_ref, *out_refs):
    near = jnp.where(place[2] < 2, own_ref[...], down_ref[...])
    even = place[2] % 2 == 0
    first = jnp.where(even, near, side_ref[...])
    second = jnp.where(even, side_ref[...], near)
    for i, out_ref in enumerate(out_refs):
        out_ref[0] = first[i]
        out_ref[1] = second[i]


def placement_kernel(place, lands_ref, put_ref, keep_ref):
    cycles, size, slots = put_ref.shape
    for cycle in range(cycles):
        at = iota((size, size), 0) + cycle * size
        halves = []
        for half in range(2):
            hit = jnp.where(lands_ref[half : half + 1] == at, 1.0, 0.0)
            put_ref[cycle, :, half * size : (half + 1) * size] = hit.astype(BF16)
            halves.append(hit)
        filled = jnp.sum(halves[0] + halves[1], axis=1, keepdims=True)
        keep_ref[cycle] = jnp.broadcast_to(1.0 - filled, (size, size)).astype(BF16)


def newton_inverse(diag, identity):
    third = 1.0 / 3.0
    approx = (2.0 * identity - diag * third) * third
    for _ in range(NEWTON - 1):
        approx = dot_full(approx, 2.0 * identity - dot_full(diag, approx))
    return approx


def split_dot(a, b):
    high = b.astype(BF16)
    rest = b - high.astype(F32)
    mid = rest.astype(BF16)
    low = (rest - mid.astype(F32)).astype(BF16)
    return dot(a, low) + dot(a, mid) + dot(a, high)


def whole_rows(place, me_ref, own_mine, own_other, x_mine, x_other):
    mine = jnp.where(me_ref[0] != 0, own_mine, x_mine)
    other = jnp.where(me_ref[1] != 0, own_other, x_other)
    first_core = place[1] == 0
    return jnp.where(first_core, mine, other), jnp.where(first_core, other, mine)


def old_rows(place, x_mine, x_other, top_mine, top_other):
    first_chip = place[0] == 0
    return jnp.concatenate(
        [
            jnp.where(first_chip, top_mine, x_mine),
            jnp.where(first_chip, top_other, x_other),
        ],
        axis=0,
    )


def panel_kernel(place, me_ref, xm_ref, xo_ref, top_ref, onehot_ref, put_ref, keep_ref, *rest):
    *pieces, side_ref, lower1_ref, corner_ref, raw0, raw1, sems = rest
    cycles, size, _ = raw0.shape
    row = 2 * place[0] + place[1]
    slots = STEPS * size

    def fetch(pairs):
        copies = []
        for target, sources in zip((raw0, raw1), pairs):
            at = 0
            for source in sources:
                count = source.shape[0]
                copies.append(
                    pltpu.make_async_copy(source, target.at[at : at + count], sems.at[len(copies)])
                )
                at += count
        for copy in copies:
            copy.start()
        for copy in copies:
            copy.wait()

    if len(pieces) == 2:
        fetch(((pieces[0],), (pieces[1],)))
    else:
        own, down, over = pieces[:2], pieces[2:4], pieces[4:]
        for col, pairs in enumerate(((own, over), (over, own), (down, over), (over, down))):

            @pl.when(place[2] == col)
            def _(pairs=pairs):
                fetch(pairs)

    new0, new1, old = [], [], []
    for b, raw in enumerate((raw0, raw1)):
        own = dot(onehot_ref[...], raw.reshape(cycles * size, size)[...]).astype(BF16)
        upper, below = whole_rows(place, me_ref, own[:size], own[size:], xm_ref[b], xo_ref[b])
        new0.append(upper)
        new1.append(below)
        old.append(old_rows(place, xm_ref[b], xo_ref[b], raw[0], top_ref[b]))
    identity = jnp.where(iota((size, size), 0) == iota((size, size), 1), 1.0, 0.0).astype(F32)
    inverse0 = newton_inverse(new0[0].astype(F32), identity)
    corner = split_dot(new1[0], inverse0).astype(BF16)
    corner_ref[...] = corner
    inverse1 = newton_inverse(
        (new1[1].astype(F32) - dot(corner, new0[1])).astype(BF16).astype(F32), identity
    )
    for cycle in range(cycles):
        put = put_ref[cycle]
        keep = keep_ref[cycle]
        left = (dot(put, old[0]) + (keep * raw0[cycle]).astype(F32)).astype(BF16)
        right = dot(put, old[1]) + (keep * raw1[cycle]).astype(F32)
        if cycle == 0:
            left = jnp.where(row == 0, new0[0], jnp.where(row == 1, new1[0], left))
            right = jnp.where(
                row == 0, new0[1].astype(F32), jnp.where(row == 1, new1[1].astype(F32), right)
            )
        lower = split_dot(left, inverse0)
        if cycle == 0:
            lower = jnp.where(row == 0, 0.0, lower)
        lower = lower.astype(BF16)
        side_ref[cycle, :, :slots] = put
        side_ref[cycle, :, slots:] = -lower
        right = (right - dot(lower, new0[1])).astype(BF16)
        lower = split_dot(right, inverse1)
        if cycle == 0:
            lower = jnp.where(row <= 1, 0.0, lower)
        lower1_ref[cycle] = lower.astype(BF16)


def factor_panels(chain, place, me, rows, tops, onehot, put, keep, pieces):
    cycles, size, _ = keep.shape
    operands = (place, me, *rows, tops, onehot, put, keep)
    return chain.run(
        panel_kernel,
        "factor_panels",
        (*operands, *pieces),
        [SMEM] + [VMEM] * (len(operands) - 1) + [ANY] * len(pieces),
        [
            array(cycles, size, (STEPS + 1) * size),
            array(cycles, size, size),
            array(size, size),
        ],
        [VMEM] * 3,
        scratch_shapes=[
            pltpu.VMEM((cycles, size, size), BF16),
            pltpu.VMEM((cycles, size, size), BF16),
            pltpu.SemaphoreType.DMA((len(pieces),)),
        ],
    )


def update_kernel(
    first, place, me_ref, block_ref, native_ref, own_ref, xm_ref, xo_ref, top_ref,
    side_ref, keep_ref, lower1_ref, corner_ref, *rest,
):
    out_ref = rest[-1]
    cycles, width, size, _ = block_ref.shape
    row = 2 * place[0] + place[1]
    slots = STEPS * size
    upper, below, old = [], [], []
    for b in range(width):
        u, n = whole_rows(place, me_ref, native_ref[b], own_ref[b], xm_ref[b], xo_ref[b])
        upper.append(u)
        below.append(n)
        old.append(old_rows(place, xm_ref[b], xo_ref[b], block_ref[0, b], top_ref[b]))
    join = lambda parts: parts[0] if width == 1 else jnp.concatenate(parts, 1)
    upper, below, old = join(upper), join(below), join(old)
    upper1 = (below.astype(F32) - dot(corner_ref[...], upper)).astype(BF16)
    both = jnp.concatenate([old, upper], 0)
    for cycle in range(cycles):
        keep = keep_ref[cycle]
        kept = join([block_ref[cycle, b] * keep for b in range(width)])
        block = (dot(side_ref[cycle], both) + kept.astype(F32)).astype(BF16)
        if cycle == 0:
            block = jnp.where(row == 0, upper, jnp.where(row == 1, upper1, block))
        block = (block.astype(F32) - dot(lower1_ref[cycle], upper1)).astype(BF16)
        for b in range(width):
            out_ref[cycle, b] = block[:, b * size : (b + 1) * size]
    if first == 0:

        @pl.when(jnp.logical_and(pl.program_id(0) == 0, place[2] == 0))
        def _():
            for cycle in range(cycles):
                block = -side_ref[cycle, :, slots:]
                if cycle == 0:
                    block = jnp.where(row == 0, upper[:, :size], block)
                out_ref[cycle, 0] = block

        @pl.when(jnp.logical_and(pl.program_id(0) == 0, place[2] == 1))
        def _():
            for cycle in range(cycles):
                block = lower1_ref[cycle]
                if cycle == 0:
                    block = jnp.where(
                        row == 0, upper[:, :size], jnp.where(row == 1, upper1[:, :size], block)
                    )
                out_ref[cycle, 0] = block


def update_columns(chain, place, me, matrix, rows, top, factors, first, count, width, result):
    cycles, blocks, size, _ = matrix.shape
    column = pl.BlockSpec((width, size, size), lambda j: (j, 0, 0))
    blocks_spec = pl.BlockSpec(
        (cycles, width, size, size), lambda j: (0, j + first // width, 0, 0)
    )
    operands = [place, me, matrix, *rows, top, *factors]
    in_specs = [SMEM, constant(me.shape), blocks_spec]
    in_specs += [column] * 4
    in_specs += [pl.BlockSpec((width, size, size), lambda j: (j + first // width, 0, 0))]
    in_specs += [constant(f.shape) for f in factors]
    aliases = {}
    if result is not None:
        aliases = {len(operands): 0}
        operands.append(result)
        in_specs.append(ANY)
    return chain.run(
        functools.partial(update_kernel, first),
        "update_columns",
        operands,
        in_specs,
        [array(*matrix.shape)],
        [blocks_spec],
        grid=(count // width,),
        input_output_aliases=aliases,
    )[0]


def split_blocks(blocks):
    width = 2 if blocks % 2 == 0 else 1
    base, extra = divmod(blocks // width - 1, 3)
    counts = [1] + [base + (1 if i < extra else 0) for i in range(3)]
    return width, [width * c for c in counts]


def body(matrix, pivots):
    rows = lax.axis_size("row")
    cols = lax.axis_size("col")
    chips = rows // 2
    row = lax.axis_index("row")
    col = lax.axis_index("col")
    cycles, size, blocks, _ = matrix.shape
    plain = matrix.transpose(0, 2, 1, 3)
    matrix = pltpu.with_memory_space_constraint(plain, pltpu.HBM)
    place = jnp.stack([row // 2, row % 2, col]).astype(I32)
    width, counts = split_blocks(blocks)
    starts = [sum(counts[:i]) for i in range(len(counts))]
    few_cols = cols == 4
    half = (cycles + 1) // 2

    swap = [(r, r ^ 1) for r in range(rows)]
    first_swap = [(0, 1), (1, 0)]
    down_pairs = [(0, 2), (1, 3)]
    side_pairs = [(0, 1), (1, 0), (2, 3), (3, 2)]

    def hop_pairs(h):
        pairs = []
        for a, b in ((h, h + 1), (chips - 1 - h, chips - 2 - h)):
            pairs += [(2 * a, 2 * b), (2 * a + 1, 2 * b + 1)]
        return pairs

    onehot, owner, me, lands, raw_a, raw_b, mine, other, token = start(
        place, pivots, matrix, counts[0], width, rows
    )
    chain = Chain(token)
    native, others, theirs, x_mine, x_send, x_other = {0: mine}, {0: other}, {}, {}, {}, {}
    hops = {i: [] for i in range(len(counts))}
    received = {i: [] for i in range(len(counts))}

    def swap_others(*chunks):
        own = [others[i] for i in chunks]
        own = own[0] if len(own) == 1 else jnp.concatenate(own, 0)
        theirs[chunks] = lax.ppermute(own, "row", swap)

    def gather(i, count):
        a, b = gather_rows(chain, matrix, onehot, starts[i], count, width)
        return a, b

    def meet(mine, theirs):
        return chain.whole(meet_kernel, "meet", place, (mine, theirs), [array(*mine.shape)])[0]

    def hop(i):
        h = len(hops[i])
        if h == 0:
            out = native[i]
        else:
            received[i].append(hops[i][h - 1])
            out = chain.whole(
                merge_kernel,
                "merge",
                place,
                (owner, native[i], received[i][h - 1]),
                [array(*native[i].shape)],
            )[0]
        hops[i].append(lax.ppermute(out, "row", hop_pairs(h)))

    def finish(i):
        while len(hops[i]) < chips - 1:
            hop(i)
        received[i].append(hops[i][-1])
        x_mine[i], x_send[i] = chain.whole(
            finish_kernel,
            "finish",
            place,
            (owner, me, native[i], *received[i]),
            [array(*native[i].shape)] * 2,
        )

    def exchange(i):
        x_other[i] = lax.ppermute(x_send[i], "row", swap)

    def side(own, down, axis_pairs=side_pairs):
        out = chain.whole(side_kernel, "side", place, (own, down), [array(*own.shape)])[0]
        return lax.ppermute(out, "col", side_pairs)

    def from_two(own):
        zero = jnp.zeros_like(own)
        return lax.psum(jnp.stack([jnp.where(col == b, own, zero) for b in range(2)]), "col")

    theirs0 = lax.ppermute(other, "row", swap)
    if few_cols:
        down_a = lax.ppermute(raw_a, "col", down_pairs)
        down_b = lax.ppermute(raw_b, "col", down_pairs)
    native[1], others[1] = gather(1, counts[1])
    theirs1 = lax.ppermute(others[1], "row", swap)
    native[0] = meet(mine, theirs0)
    hop(0)
    native[1] = meet(native[1], theirs1)
    hop(1)
    rest_mine, rest_other = gather(2, counts[2] + counts[3])
    rest_theirs = lax.ppermute(rest_other, "row", swap)
    hop(0)
    if few_cols:
        side_a = side(raw_a, down_a)
    rest = meet(rest_mine, rest_theirs)
    cut = counts[2]
    native[2], native[3] = rest[:cut], rest[cut:]
    others[2], others[3] = rest_other[:cut], rest_other[cut:]
    hop(2)
    if few_cols:
        side_b = side(raw_b, down_b)
    hop(0)
    hop(1)
    put, keep = chain.whole(
        placement_kernel,
        "placement",
        place,
        (lands,),
        [array(cycles, size, STEPS * size), array(cycles, size, size)],
    )
    if few_cols:
        chain.need(side_a)
    finish(0)
    lead = jnp.stack([x_mine[0][0], x_send[0][0]])
    if few_cols:
        down_lead = lax.ppermute(lead, "col", down_pairs)
    else:
        leads = from_two(lead)
        raws = from_two(jnp.concatenate([raw_a, raw_b], 0))
    hop(3)
    hop(2)
    if few_cols:
        chain.need(side_b)
    hop(1)
    exchange(0)
    if few_cols:
        side_lead = side(lead, down_lead)
        (firsts,) = chain.whole(
            pair_kernel, "pair", place, (raw_a, down_a, side_a), [array(2, size, size)]
        )
        pieces = [raw_a, raw_b, down_a, down_b, side_a, side_b]
    else:
        firsts = raws[:, 0]
        pieces = [raws[0], raws[1]]
    chain.need(x_other[0])
    tops = lax.ppermute(firsts, "row", first_swap)
    hop(3)
    if few_cols:
        panel_mine, panel_send = chain.whole(
            pair_kernel, "pair", place, (lead, down_lead, side_lead), [array(2, size, size)] * 2
        )
    else:
        panel_mine, panel_send = leads[:, 0], leads[:, 1]
    panel_other = lax.ppermute(panel_send, "row", swap)
    top = lax.ppermute(plain[0], "row", first_swap)
    hop(2)
    finish(1)
    exchange(1)
    side_rows, lower1, corner = factor_panels(
        chain, place, me, (panel_mine, panel_other), tops, onehot, put, keep, pieces
    )
    factors = (side_rows, keep, lower1, corner)

    def update(i, result):
        return update_columns(
            chain, place, me, matrix, (native[i], others[i], x_mine[i], x_other[i]), top,
            factors, starts[i], counts[i], width, result,
        )

    hop(3)
    result = update(0, None)
    result = update(1, result)
    finish(2)
    exchange(2)
    chain.need(x_other[2])
    finish(3)
    exchange(3)
    result = update(2, result)
    result = update(3, result)
    return result.transpose(0, 2, 1, 3)


def solution(mesh):
    return jax.shard_map(
        body,
        mesh=mesh,
        in_specs=(P(None, "row", None, "col"), P()),
        out_specs=P(None, "row", None, "col"),
        check_vma=False,
    )
```

time: 473 us -> 137 us (0.29); the launches traced: 465 us -> 136 us
  waiting for transfers between devices: 276 us -> 20.5 us
  local copies, waits for them, and re-layouts: 120 us -> 2.46 us
  Pallas kernels: 0 us -> 68.3 us
  starting transfers between devices: 0.81 us -> 43.9 us
  matrix products: 33.8 us -> 0 us
  other arithmetic: 20.3 us -> 0.1 us
  between operations: 13.8 us -> 0.48 us
    psum x4 -> x0, waiting for transfers between devices: 276 us -> none  [broadcast(): return lax.psum(jnp.where(mine, shard, jnp.zeros_like(shard)), axis)]
    pallas_call x0 -> x29, Pallas kernels: none -> 68.3 us  [the longest x28 64.3 us: run(): pl.pallas_call(body, in_specs=in_specs + [ANY] * len(waits), out_specs=li...]
    ppermute x0 -> x28, starting transfers between devices: none -> 43.9 us  [the longest x12 22.5 us: hop(): hops[i].append(lax.ppermute(out, 'row', hop_pairs(h)))]
    dot_general x16 -> x0, matrix products: 33.8 us -> none  [the longest x2 23 us: body(): jnp.dot(lower_panel, upper_rows, preferred_element_type=jnp.float32)]
    reshape x2 -> x0, local copies, waits for them, and re-layouts: 33.4 us -> none  [body(): return current.reshape(row_cycles, block_size, col_cycles, block_size)]
    scatter x2 -> x0, local copies, waits for them, and re-layouts: 33 us -> none  [body(): current = current.at[target].set(old_top, mode='drop')]
    unnamed x13 -> x2, local copies, waits for them, and re-layouts: 31.6 us -> 0.68 us
    ppermute x0 -> x28, waiting for transfers between devices: none -> 20.5 us  [the longest x12 11.2 us: hop(): hops[i].append(lax.ppermute(out, 'row', hop_pairs(h)))]
  transfers between devices with their start and end apart: 4 -> 28, of which waited for: 4 -> 11; matrix products, arithmetic and copies ran while one was open for 0% -> 1% of each run, Pallas kernels for 0% -> 33%
where the time goes in v2:
time: 137 us; the launch traced here: 136 us
  Pallas kernels  68.3 us (50%)
  starting transfers between devices  43.9 us (32%)
  waiting for transfers between devices  20.5 us (15%)
  local copies, waits for them, and re-layouts  2.46 us (2%)
    pallas_call x28, Pallas kernels, run(): pl.pallas_call(body, in_specs=in_specs + [ANY] * len(waits), out_specs=li...  64.3 us
    ppermute x12, starting transfers between devices, hop(): hops[i].append(lax.ppermute(out, 'row', hop_pairs(h)))  22.5 us
    ppermute x12, waiting for transfers between devices, hop(): hops[i].append(lax.ppermute(out, 'row', hop_pairs(h)))  11.2 us
    ppermute x3, starting transfers between devices, side(): return lax.ppermute(out, 'col', side_pairs)  4.67 us
    ppermute x1, starting transfers between devices, body(): down_a = lax.ppermute(raw_a, 'col', down_pairs)  4.59 us
    ppermute x1, starting transfers between devices, body(): down_lead = lax.ppermute(lead, 'col', down_pairs)  4.4 us
    pallas_call x1, Pallas kernels, start(): pl.pallas_call(functools.partial(start_kernel, rows), grid=(count // widt...  3.97 us
    ppermute x3, waiting for transfers between devices, side(): return lax.ppermute(out, 'col', side_pairs)  2.94 us
  transfers between devices with their start and end apart: 28, of which 11 were waited for; matrix products, arithmetic and copies ran while one was open for 1% of the time, Pallas kernels for 33%

profile of v2, /device:TPU:0, one launch (start us, length us, event | category | flops | bytes accessed | tf_op | source)
XLA Modules:
  0.0 135.8 jit_solution(8164950808609145667)
XLA Ops:
  0.8 4.0 %start.1 = (bf16[512,1792]{1,0:T(8,128)(2,1)S(1)}, s32[2,256,1]{2,1,0:T(8,128)S(1)}, s32[2,256,1]{2,1,0:T(8,128)S(1)}, s32[2,256]{1,0:T(2,128)S(1)}, bf16[4,256,...) custom-call(s32[3]{0:T(128)S(1)} %pad_add_fusion.place.refs_0_, ...), custom_call_target="tpu_custom_call" | custom-call | flops 1024 | bytes 1024 | tf_op jit(solution)/shard_map/start/pallas_call | solution.py:161
  4.7 3.8 %gather_rows.2 = (bf16[4,256,256]{2,1,0:T(8,128)(2,1)S(1)}, bf16[4,256,256]{2,1,0:T(8,128)(2,1)S(1)}, f32[8,128]{1,0:T(8,128)S(1)}) custom-call(bf16[512,1792]{1,0:T(8,128)(2,1)S(1)} %get-tuple-element.80.refs_0_.refs_5_, bf16[7,14,256,256]{3,2,1,0:T(8,128)(2,1)} %bitcast.8, f32[8,128]{1,0:T(8,128)S(1)} %get-tuple-element.81.refs_2_), custom_call_target="tpu_custom_call" | custom-call | flops 1024 | bytes 1024 | tf_op jit(solution)/shard_map/gather_rows/pallas_call | solution.py:194
  9.1 1.8 %collective-permute-done.1.refs_2_ = bf16[2,256,256]{2,1,0:T(8,128)(2,1)S(1)} collective-permute-done((bf16[2,256,256]{2,1,0:T(8,128)(2,1)S(1)}, bf16[2,256,256]{2,1,0:T(8,128)(2,1)S(1)}, u32[]{:S(2)}, u32[]{:S(2)}) %collective-permute-start.1) | collective-permute-done | bytes 262176 | tf_op jit(solution)/shard_map/ppermute | solution.py:586
  12.1 6.5 %gather_rows.3 = (bf16[8,256,256]{2,1,0:T(8,128)(2,1)S(1)}, bf16[8,256,256]{2,1,0:T(8,128)(2,1)S(1)}, f32[8,128]{1,0:T(8,128)S(1)}) custom-call(bf16[512,1792]{1,0:T(8,128)(2,1)S(1)} %get-tuple-element.80.refs_0_.refs_5_, bf16[7,14,256,256]{3,2,1,0:T(8,128)(2,1)} %bitcast.9, f32[8,128]{1,0:T(8,128)S(1)} %get-tuple-element.88.refs_2_), custom_call_target="tpu_custom_call" | custom-call | flops 1024 | bytes 1024 | tf_op jit(solution)/shard_map/gather_rows/pallas_call | solution.py:194
  19.1 4.6 %collective-permute-start.3 = (bf16[4,256,256]{2,1,0:T(8,128)(2,1)S(1)}, bf16[4,256,256]{2,1,0:T(8,128)(2,1)S(1)}, u32[]{:S(2)}, u32[]{:S(2)}) collective-permute-start(bf16[4,256,256]{2,1,0:T(8,128)(2,1)S(1)} %get-tuple-element.91.refs_1_.refs_8_), channel_id=1, source_target_pairs={{0,2},{1,3},{4,6},{5,7},{8,10},{9,11},{12,14},{13,15},{16,18},{17,... | collective-permute-start | bytes 1572872 | tf_op jit(solution)/shard_map/ppermute | solution.py:588
  23.7 3.5 %collective-permute-start.4 = (bf16[2,256,256]{2,1,0:T(8,128)(2,1)S(1)}, bf16[2,256,256]{2,1,0:T(8,128)(2,1)S(1)}, u32[]{:S(2)}, u32[]{:S(2)}) collective-permute-start(bf16[2,256,256]{2,1,0:T(8,128)(2,1)S(1)} %get-tuple-element.93.refs_2_.refs_3_), channel_id=1, source_target_pairs={{0,8},{4,12},{24,16},{28,20},{1,9},{5,13},{25,17},{29,21},{2,10},{... | collective-permute-start | bytes 786440 | tf_op jit(solution)/shard_map/ppermute | solution.py:561
  27.2 1.3 collective-permute-start.8
  28.5 1.3 collective-permute-start.10
  29.9 4.0 %collective-permute-done.4.refs_3_.refs_4_ = bf16[2,256,256]{2,1,0:T(8,128)(2,1)S(1)} collective-permute-done((bf16[2,256,256]{2,1,0:T(8,128)(2,1)S(1)}, bf16[2,256,256]{2,1,0:T(8,128)(2,1)S(1)}, u32[]{:S(2)}, u32[]{:S(2)}) %collective-permute-start.4) | collective-permute-done | bytes 262176 | tf_op jit(solution)/shard_map/ppermute | solution.py:561
  36.5 1.6 %collective-permute-start.6 = (bf16[4,256,256]{2,1,0:T(8,128)(2,1)S(1)}, bf16[4,256,256]{2,1,0:T(8,128)(2,1)S(1)}, u32[]{:S(2)}, u32[]{:S(2)}) collective-permute-start(bf16[4,256,256]{2,1,0:T(8,128)(2,1)S(1)} %get-tuple-element.98), channel_id=1, source_target_pairs={{0,1},{1,0},{2,3},{3,2},{4,5},{5,4},{6,7},{7,6},{8,9},{9,8},{10,11... | collective-permute-start | bytes 1572872 | tf_op jit(solution)/shard_map/ppermute | solution.py:580
  38.1 1.6 %slice_bitcast_fusion = bf16[14,256,256]{2,1,0:T(8,128)(2,1)S(1)} fusion(bf16[7,14,256,256]{3,2,1,0:T(8,128)(2,1)} %bitcast.10), kind=kLoop, calls=%fused_computation | loop fusion | bytes 3670016 | tf_op jit(solution)/shard_map/squeeze | solution.py:651
  39.7 1.9 %collective-permute-start.25 = (bf16[14,256,256]{2,1,0:T(8,128)(2,1)S(1)}, bf16[14,256,256]{2,1,0:T(8,128)(2,1)S(1)}, u32[]{:S(2)}, u32[]{:S(2)}) collective-permute-start(bf16[14,256,256]{2,1,0:T(8,128)(2,1)S(1)} %slice_bitcast_fusion), channel_id=1, source_target_pairs={{0,4},{4,0},{1,5},{5,1},{2,6},{6,2},{3,7},{7,3}} | collective-permute-start | bytes 5505032 | tf_op jit(solution)/shard_map/ppermute | solution.py:651
  42.3 1.5 %collective-permute-done.8.refs_2_.refs_11_ = bf16[3,256,256]{2,1,0:T(8,128)(2,1)S(1)} collective-permute-done((bf16[3,256,256]{2,1,0:T(8,128)(2,1)S(1)}, bf16[3,256,256]{2,1,0:T(8,128)(2,1)S(1)}, u32[]{:S(2)}, u32[]{:S(2)}) %collective-permute-start.8) | collective-permute-done | bytes 393248 | tf_op jit(solution)/shard_map/ppermute | solution.py:589
  45.0 1.3 collective-permute-start.9
  46.4 4.6 %collective-permute-start.13 = (bf16[4,256,256]{2,1,0:T(8,128)(2,1)S(1)}, bf16[4,256,256]{2,1,0:T(8,128)(2,1)S(1)}, u32[]{:S(2)}, u32[]{:S(2)}) collective-permute-start(bf16[4,256,256]{2,1,0:T(8,128)(2,1)S(1)} %get-tuple-element.155.refs_2_.refs_3_), channel_id=1, source_target_pairs={{0,8},{4,12},{24,16},{28,20},{1,9},{5,13},{25,17},{29,21},{2,10},{... | collective-permute-start | bytes 1572872 | tf_op jit(solution)/shard_map/ppermute | solution.py:561
  52.4 1.6 %collective-permute-start.14 = (bf16[3,256,256]{2,1,0:T(8,128)(2,1)S(1)}, bf16[3,256,256]{2,1,0:T(8,128)(2,1)S(1)}, u32[]{:S(2)}, u32[]{:S(2)}) collective-permute-start(bf16[3,256,256]{2,1,0:T(8,128)(2,1)S(1)} %get-tuple-element.114), channel_id=1, source_target_pairs={{0,1},{1,0},{2,3},{3,2},{4,5},{5,4},{6,7},{7,6},{8,9},{9,8},{10,11... | collective-permute-start | bytes 1179656 | tf_op jit(solution)/shard_map/ppermute | solution.py:580
  56.0 4.4 %collective-permute-start.11 = (bf16[2,256,256]{2,1,0:T(8,128)(2,1)S(1)}, bf16[2,256,256]{2,1,0:T(8,128)(2,1)S(1)}, u32[]{:S(2)}, u32[]{:S(2)}) collective-permute-start(bf16[2,256,256]{2,1,0:T(8,128)(2,1)S(1)} %pad_maximum_fusion.refs_1_), channel_id=1, source_target_pairs={{0,2},{1,3},{4,6},{5,7},{8,10},{9,11},{12,14},{13,15},{16,18},{17,... | collective-permute-start | bytes 786440 | tf_op jit(solution)/shard_map/ppermute | solution.py:622
  60.4 2.1 %collective-permute-done.14.refs_5_.refs_13_ = bf16[3,256,256]{2,1,0:T(8,128)(2,1)S(1)} collective-permute-done((bf16[3,256,256]{2,1,0:T(8,128)(2,1)S(1)}, bf16[3,256,256]{2,1,0:T(8,128)(2,1)S(1)}, u32[]{:S(2)}, u32[]{:S(2)}) %collective-permute-start.14) | collective-permute-done | bytes 393248 | tf_op jit(solution)/shard_map/ppermute | solution.py:580
  62.5 5.2 %collective-permute-start.5 = (bf16[4,256,256]{2,1,0:T(8,128)(2,1)S(1)}, bf16[4,256,256]{2,1,0:T(8,128)(2,1)S(1)}, u32[]{:S(2)}, u32[]{:S(2)}) collective-permute-start(bf16[4,256,256]{2,1,0:T(8,128)(2,1)S(1)} %get-tuple-element.156.refs_2_.refs_3_), channel_id=1, source_target_pairs={{0,8},{4,12},{24,16},{28,20},{1,9},{5,13},{25,17},{29,21},{2,10},{... | collective-permute-start | bytes 1572872 | tf_op jit(solution)/shard_map/ppermute | solution.py:561
  69.9 1.3 collective-permute-start.20
  71.8 1.6 %collective-permute-start.17 = (bf16[2,256,256]{2,1,0:T(8,128)(2,1)S(1)}, bf16[2,256,256]{2,1,0:T(8,128)(2,1)S(1)}, u32[]{:S(2)}, u32[]{:S(2)}) collective-permute-start(bf16[2,256,256]{2,1,0:T(8,128)(2,1)S(1)} %get-tuple-element.119), channel_id=1, source_target_pairs={{0,1},{1,0},{2,3},{3,2},{4,5},{5,4},{6,7},{7,6},{8,9},{9,8},{10,11... | collective-permute-start | bytes 786440 | tf_op jit(solution)/shard_map/ppermute | solution.py:580
  73.9 3.2 %collective-permute-done.5.refs_3_.refs_4_ = bf16[4,256,256]{2,1,0:T(8,128)(2,1)S(1)} collective-permute-done((bf16[4,256,256]{2,1,0:T(8,128)(2,1)S(1)}, bf16[4,256,256]{2,1,0:T(8,128)(2,1)S(1)}, u32[]{:S(2)}, u32[]{:S(2)}) %collective-permute-start.5) | collective-permute-done | bytes 524320 | tf_op jit(solution)/shard_map/ppermute | solution.py:561
  77.1 1.9 %collective-permute-start.19 = (bf16[2,256,256]{2,1,0:T(8,128)(2,1)S(1)}, bf16[2,256,256]{2,1,0:T(8,128)(2,1)S(1)}, u32[]{:S(2)}, u32[]{:S(2)}) collective-permute-start(bf16[2,256,256]{2,1,0:T(8,128)(2,1)S(1)} %get-tuple-element.123), channel_id=1, source_target_pairs={{0,4},{4,0},{1,5},{5,1},{2,6},{6,2},{3,7},{7,3}} | collective-permute-start | bytes 786440 | tf_op jit(solution)/shard_map/ppermute | solution.py:642
  82.5 3.6 %collective-permute-done.20.refs_6_ = bf16[4,256,256]{2,1,0:T(8,128)(2,1)S(1)} collective-permute-done((bf16[4,256,256]{2,1,0:T(8,128)(2,1)S(1)}, bf16[4,256,256]{2,1,0:T(8,128)(2,1)S(1)}, u32[]{:S(2)}, u32[]{:S(2)}) %collective-permute-start.20) | collective-permute-done | bytes 524320 | tf_op jit(solution)/shard_map/ppermute | solution.py:561
  87.2 1.3 collective-permute-start.23
  90.2 11.1 %factor_panels.1 = (bf16[7,256,768]{2,1,0:T(8,128)(2,1)S(1)}, bf16[7,256,256]{2,1,0:T(8,128)(2,1)S(1)}, bf16[256,256]{1,0:T(8,128)(2,1)S(1)}, f32[8,128]{1,0:T(8,128)S(1)}) custom-call(s32[3]{0:T(128)S(1)} %pad_add_fusion.place.refs_0_, s32[2,256,1]{2,1,0:T(8,128)S(1)} %get-tuple-element.79.refs_2_.refs_1_, ...), custom_call_target="tpu_custom_call" | custom-call | flops 1024 | bytes 1024 | tf_op jit(solution)/shard_map/factor_panels/pallas_call | solution.py:194
  102.0 1.3 collective-permute-start.22
  103.3 5.2 %update_columns.4 = (bf16[7,14,256,256]{3,2,1,0:T(8,128)(2,1)}, f32[8,128]{1,0:T(8,128)S(1)}) custom-call(s32[3]{0:T(128)S(1)} %pad_add_fusion.place.refs_0_, s32[2,256,1]{2,1,0:T(8,128)S(1)} %get-tuple-element.79.refs_2_.refs_1_, bf16[7,14,256,256]{3,2,1,0:T(8,128)(2,1)} %bitcast.11, bf16[2,256,256]{2,1,0:T(8,128)(2,1)S(1)} %get-tuple-element.93.refs_2_.refs_3_, ...), custom_call_target="tpu_custom_call" | custom-call | flops 1024 | bytes 1024 | tf_op jit(solution)/shard_map/update_columns/pallas_call | solution.py:194
  108.5 7.5 %update_columns.5 = (bf16[7,14,256,256]{3,2,1,0:T(8,128)(2,1)}, f32[8,128]{1,0:T(8,128)S(1)}) custom-call(s32[3]{0:T(128)S(1)} %pad_add_fusion.place.refs_0_, s32[2,256,1]{2,1,0:T(8,128)S(1)} %get-tuple-element.79.refs_2_.refs_1_, bf16[7,14,256,256]{3,2,1,0:T(8,128)(2,1)} %bitcast.12, ...), custom_call_target="tpu_custom_call", output_to_operand_aliasing={{0}: (12, {})} | custom-call | flops 1024 | bytes 1024 | tf_op jit(solution)/shard_map/update_columns/pallas_call | solution.py:194
  116.0 1.2 finish.6
  120.7 7.5 %update_columns.6 = (bf16[7,14,256,256]{3,2,1,0:T(8,128)(2,1)}, f32[8,128]{1,0:T(8,128)S(1)}) custom-call(s32[3]{0:T(128)S(1)} %pad_add_fusion.place.refs_0_, s32[2,256,1]{2,1,0:T(8,128)S(1)} %get-tuple-element.79.refs_2_.refs_1_, bf16[7,14,256,256]{3,2,1,0:T(8,128)(2,1)} %bitcast.13, ...), custom_call_target="tpu_custom_call", output_to_operand_aliasing={{0}: (12, {})} | custom-call | flops 1024 | bytes 1024 | tf_op jit(solution)/shard_map/update_columns/pallas_call | solution.py:194
  128.2 7.5 %update_columns.7 = (bf16[7,14,256,256]{3,2,1,0:T(8,128)(2,1)}, f32[8,128]{1,0:T(8,128)}) custom-call(s32[3]{0:T(128)S(1)} %pad_add_fusion.place.refs_0_, s32[2,256,1]{2,1,0:T(8,128)S(1)} %get-tuple-element.79.refs_2_.refs_1_, bf16[7,14,256,256]{3,2,1,0:T(8,128)(2,1)} %bitcast.14, ...), custom_call_target="tpu_custom_call", output_to_operand_aliasing={{0}: (12, {})} | custom-call | flops 1024 | bytes 1024 | tf_op jit(solution)/shard_map/update_columns/pallas_call | solution.py:194
  (62 shorter events, 24.6 us)
Async XLA Ops:
  0.1 0.7 copy-start
  8.5 3.0 %collective-permute-start = (bf16[4,256,256]{2,1,0:T(8,128)(2,1)S(1)}, bf16[4,256,256]{2,1,0:T(8,128)(2,1)S(1)}, u32[]{:S(2)}, u32[]{:S(2)}) collective-permute-start(bf16[4,256,256]{2,1,0:T(8,128)(2,1)S(1)} %get-tuple-element.83.refs_4_), channel_id=1, source_target_pairs={{0,4},{4,0},{8,12},{12,8},{16,20},{20,16},{24,28},{28,24},{1,5},{5... | collective-permute-start | bytes 1572872 | tf_op jit(solution)/shard_map/ppermute | solution.py:591
  9.0 1.9 %collective-permute-start.1 = (bf16[2,256,256]{2,1,0:T(8,128)(2,1)S(1)}, bf16[2,256,256]{2,1,0:T(8,128)(2,1)S(1)}, u32[]{:S(2)}, u32[]{:S(2)}) collective-permute-start(bf16[2,256,256]{2,1,0:T(8,128)(2,1)S(1)} %get-tuple-element.85.refs_4_), channel_id=1, source_target_pairs={{0,4},{4,0},{8,12},{12,8},{16,20},{20,16},{24,28},{28,24},{1,5},{5... | collective-permute-start | bytes 786440 | tf_op jit(solution)/shard_map/ppermute | solution.py:586
  18.7 21.0 %collective-permute-start.2 = (bf16[8,256,256]{2,1,0:T(8,128)(2,1)S(1)}, bf16[8,256,256]{2,1,0:T(8,128)(2,1)S(1)}, u32[]{:S(2)}, u32[]{:S(2)}) collective-permute-start(bf16[8,256,256]{2,1,0:T(8,128)(2,1)S(1)} %get-tuple-element.90), channel_id=1, source_target_pairs={{0,4},{4,0},{8,12},{12,8},{16,20},{20,16},{24,28},{28,24},{1,5},{5... | collective-permute-start | bytes 3145736 | tf_op jit(solution)/shard_map/ppermute | solution.py:597
  19.1 16.8 %collective-permute-start.3 = (bf16[4,256,256]{2,1,0:T(8,128)(2,1)S(1)}, bf16[4,256,256]{2,1,0:T(8,128)(2,1)S(1)}, u32[]{:S(2)}, u32[]{:S(2)}) collective-permute-start(bf16[4,256,256]{2,1,0:T(8,128)(2,1)S(1)} %get-tuple-element.91.refs_1_.refs_8_), channel_id=1, source_target_pairs={{0,2},{1,3},{4,6},{5,7},{8,10},{9,11},{12,14},{13,15},{16,18},{17,... | collective-permute-start | bytes 1572872 | tf_op jit(solution)/shard_map/ppermute | solution.py:588
  23.7 10.2 %collective-permute-start.4 = (bf16[2,256,256]{2,1,0:T(8,128)(2,1)S(1)}, bf16[2,256,256]{2,1,0:T(8,128)(2,1)S(1)}, u32[]{:S(2)}, u32[]{:S(2)}) collective-permute-start(bf16[2,256,256]{2,1,0:T(8,128)(2,1)S(1)} %get-tuple-element.93.refs_2_.refs_3_), channel_id=1, source_target_pairs={{0,8},{4,12},{24,16},{28,20},{1,9},{5,13},{25,17},{29,21},{2,10},{... | collective-permute-start | bytes 786440 | tf_op jit(solution)/shard_map/ppermute | solution.py:561
  27.2 16.6 %collective-permute-start.8 = (bf16[3,256,256]{2,1,0:T(8,128)(2,1)S(1)}, bf16[3,256,256]{2,1,0:T(8,128)(2,1)S(1)}, u32[]{:S(2)}, u32[]{:S(2)}) collective-permute-start(bf16[3,256,256]{2,1,0:T(8,128)(2,1)S(1)} %get-tuple-element.100.refs_1_.refs_9_), channel_id=1, source_target_pairs={{0,2},{1,3},{4,6},{5,7},{8,10},{9,11},{12,14},{13,15},{16,18},{17,... | collective-permute-start | bytes 1179656 | tf_op jit(solution)/shard_map/ppermute | solution.py:589
  28.5 22.5 %collective-permute-start.10 = (bf16[4,256,256]{2,1,0:T(8,128)(2,1)S(1)}, bf16[4,256,256]{2,1,0:T(8,128)(2,1)S(1)}, u32[]{:S(2)}, u32[]{:S(2)}) collective-permute-start(bf16[4,256,256]{2,1,0:T(8,128)(2,1)S(1)} %get-tuple-element.105.refs_2_.refs_3_), channel_id=1, source_target_pairs={{0,8},{4,12},{24,16},{28,20},{1,9},{5,13},{25,17},{29,21},{2,10},{... | collective-permute-start | bytes 1572872 | tf_op jit(solution)/shard_map/ppermute | solution.py:561
  34.5 9.9 %collective-permute-start.7 = (bf16[2,256,256]{2,1,0:T(8,128)(2,1)S(1)}, bf16[2,256,256]{2,1,0:T(8,128)(2,1)S(1)}, u32[]{:S(2)}, u32[]{:S(2)}) collective-permute-start(bf16[2,256,256]{2,1,0:T(8,128)(2,1)S(1)} %get-tuple-element.99), channel_id=1, source_target_pairs={{8,16},{12,20},{16,8},{20,12},{9,17},{13,21},{17,9},{21,13},{10,18... | collective-permute-start | bytes 786440 | tf_op jit(solution)/shard_map/ppermute | solution.py:561
  36.5 15.9 %collective-permute-start.6 = (bf16[4,256,256]{2,1,0:T(8,128)(2,1)S(1)}, bf16[4,256,256]{2,1,0:T(8,128)(2,1)S(1)}, u32[]{:S(2)}, u32[]{:S(2)}) collective-permute-start(bf16[4,256,256]{2,1,0:T(8,128)(2,1)S(1)} %get-tuple-element.98), channel_id=1, source_target_pairs={{0,1},{1,0},{2,3},{3,2},{4,5},{5,4},{6,7},{7,6},{8,9},{9,8},{10,11... | collective-permute-start | bytes 1572872 | tf_op jit(solution)/shard_map/ppermute | solution.py:580
  39.7 63.6 %collective-permute-start.25 = (bf16[14,256,256]{2,1,0:T(8,128)(2,1)S(1)}, bf16[14,256,256]{2,1,0:T(8,128)(2,1)S(1)}, u32[]{:S(2)}, u32[]{:S(2)}) collective-permute-start(bf16[14,256,256]{2,1,0:T(8,128)(2,1)S(1)} %slice_bitcast_fusion), channel_id=1, source_target_pairs={{0,4},{4,0},{1,5},{5,1},{2,6},{6,2},{3,7},{7,3}} | collective-permute-start | bytes 5505032 | tf_op jit(solution)/shard_map/ppermute | solution.py:651
  45.0 10.0 %collective-permute-start.9 = (bf16[2,256,256]{2,1,0:T(8,128)(2,1)S(1)}, bf16[2,256,256]{2,1,0:T(8,128)(2,1)S(1)}, u32[]{:S(2)}, u32[]{:S(2)}) collective-permute-start(bf16[2,256,256]{2,1,0:T(8,128)(2,1)S(1)} %get-tuple-element.103), channel_id=1, source_target_pairs={{16,24},{20,28},{8,0},{12,4},{17,25},{21,29},{9,1},{13,5},{18,26},... | collective-permute-start | bytes 786440 | tf_op jit(solution)/shard_map/ppermute | solution.py:561
  46.4 21.3 %collective-permute-start.13 = (bf16[4,256,256]{2,1,0:T(8,128)(2,1)S(1)}, bf16[4,256,256]{2,1,0:T(8,128)(2,1)S(1)}, u32[]{:S(2)}, u32[]{:S(2)}) collective-permute-start(bf16[4,256,256]{2,1,0:T(8,128)(2,1)S(1)} %get-tuple-element.155.refs_2_.refs_3_), channel_id=1, source_target_pairs={{0,8},{4,12},{24,16},{28,20},{1,9},{5,13},{25,17},{29,21},{2,10},{... | collective-permute-start | bytes 1572872 | tf_op jit(solution)/shard_map/ppermute | solution.py:561
  51.7 16.8 %collective-permute-start.12 = (bf16[4,256,256]{2,1,0:T(8,128)(2,1)S(1)}, bf16[4,256,256]{2,1,0:T(8,128)(2,1)S(1)}, u32[]{:S(2)}, u32[]{:S(2)}) collective-permute-start(bf16[4,256,256]{2,1,0:T(8,128)(2,1)S(1)} %get-tuple-element.111), channel_id=1, source_target_pairs={{8,16},{12,20},{16,8},{20,12},{9,17},{13,21},{17,9},{21,13},{10,18... | collective-permute-start | bytes 1572872 | tf_op jit(solution)/shard_map/ppermute | solution.py:561
  52.4 10.1 %collective-permute-start.14 = (bf16[3,256,256]{2,1,0:T(8,128)(2,1)S(1)}, bf16[3,256,256]{2,1,0:T(8,128)(2,1)S(1)}, u32[]{:S(2)}, u32[]{:S(2)}) collective-permute-start(bf16[3,256,256]{2,1,0:T(8,128)(2,1)S(1)} %get-tuple-element.114), channel_id=1, source_target_pairs={{0,1},{1,0},{2,3},{3,2},{4,5},{5,4},{6,7},{7,6},{8,9},{9,8},{10,11... | collective-permute-start | bytes 1179656 | tf_op jit(solution)/shard_map/ppermute | solution.py:580
  56.0 13.9 %collective-permute-start.11 = (bf16[2,256,256]{2,1,0:T(8,128)(2,1)S(1)}, bf16[2,256,256]{2,1,0:T(8,128)(2,1)S(1)}, u32[]{:S(2)}, u32[]{:S(2)}) collective-permute-start(bf16[2,256,256]{2,1,0:T(8,128)(2,1)S(1)} %pad_maximum_fusion.refs_1_), channel_id=1, source_target_pairs={{0,2},{1,3},{4,6},{5,7},{8,10},{9,11},{12,14},{13,15},{16,18},{17,... | collective-permute-start | bytes 786440 | tf_op jit(solution)/shard_map/ppermute | solution.py:622
  62.5 14.6 %collective-permute-start.5 = (bf16[4,256,256]{2,1,0:T(8,128)(2,1)S(1)}, bf16[4,256,256]{2,1,0:T(8,128)(2,1)S(1)}, u32[]{:S(2)}, u32[]{:S(2)}) collective-permute-start(bf16[4,256,256]{2,1,0:T(8,128)(2,1)S(1)} %get-tuple-element.156.refs_2_.refs_3_), channel_id=1, source_target_pairs={{0,8},{4,12},{24,16},{28,20},{1,9},{5,13},{25,17},{29,21},{2,10},{... | collective-permute-start | bytes 1572872 | tf_op jit(solution)/shard_map/ppermute | solution.py:561
  67.7 4.0 %collective-permute-start.15 = (bf16[2,256,256]{2,1,0:T(8,128)(2,1)S(1)}, bf16[2,256,256]{2,1,0:T(8,128)(2,1)S(1)}, u32[]{:S(2)}, u32[]{:S(2)}) collective-permute-start(bf16[2,256,256]{2,1,0:T(8,128)(2,1)S(1)} %get-tuple-element.110), channel_id=1, source_target_pairs={{0,4},{4,0},{8,12},{12,8},{16,20},{20,16},{24,28},{28,24},{1,5},{5... | collective-permute-start | bytes 786440 | tf_op jit(solution)/shard_map/ppermute | solution.py:576
  68.5 13.3 %collective-permute-start.21 = (bf16[4,256,256]{2,1,0:T(8,128)(2,1)S(1)}, bf16[4,256,256]{2,1,0:T(8,128)(2,1)S(1)}, u32[]{:S(2)}, u32[]{:S(2)}) collective-permute-start(bf16[4,256,256]{2,1,0:T(8,128)(2,1)S(1)} %get-tuple-element.127), channel_id=1, source_target_pairs={{8,16},{12,20},{16,8},{20,12},{9,17},{13,21},{17,9},{21,13},{10,18... | collective-permute-start | bytes 1572872 | tf_op jit(solution)/shard_map/ppermute | solution.py:561
  69.9 16.2 %collective-permute-start.20 = (bf16[4,256,256]{2,1,0:T(8,128)(2,1)S(1)}, bf16[4,256,256]{2,1,0:T(8,128)(2,1)S(1)}, u32[]{:S(2)}, u32[]{:S(2)}) collective-permute-start(bf16[4,256,256]{2,1,0:T(8,128)(2,1)S(1)} %get-tuple-element.126), channel_id=1, source_target_pairs={{16,24},{20,28},{8,0},{12,4},{17,25},{21,29},{9,1},{13,5},{18,26},... | collective-permute-start | bytes 1572872 | tf_op jit(solution)/shard_map/ppermute | solution.py:561
  71.8 8.8 %collective-permute-start.17 = (bf16[2,256,256]{2,1,0:T(8,128)(2,1)S(1)}, bf16[2,256,256]{2,1,0:T(8,128)(2,1)S(1)}, u32[]{:S(2)}, u32[]{:S(2)}) collective-permute-start(bf16[2,256,256]{2,1,0:T(8,128)(2,1)S(1)} %get-tuple-element.119), channel_id=1, source_target_pairs={{0,1},{1,0},{2,3},{3,2},{4,5},{5,4},{6,7},{7,6},{8,9},{9,8},{10,11... | collective-permute-start | bytes 786440 | tf_op jit(solution)/shard_map/ppermute | solution.py:580
  77.1 11.4 %collective-permute-start.19 = (bf16[2,256,256]{2,1,0:T(8,128)(2,1)S(1)}, bf16[2,256,256]{2,1,0:T(8,128)(2,1)S(1)}, u32[]{:S(2)}, u32[]{:S(2)}) collective-permute-start(bf16[2,256,256]{2,1,0:T(8,128)(2,1)S(1)} %get-tuple-element.123), channel_id=1, source_target_pairs={{0,4},{4,0},{1,5},{5,1},{2,6},{6,2},{3,7},{7,3}} | collective-permute-start | bytes 786440 | tf_op jit(solution)/shard_map/ppermute | solution.py:642
  80.5 20.7 %collective-permute-start.16 = (bf16[4,256,256]{2,1,0:T(8,128)(2,1)S(1)}, bf16[4,256,256]{2,1,0:T(8,128)(2,1)S(1)}, u32[]{:S(2)}, u32[]{:S(2)}) collective-permute-start(bf16[4,256,256]{2,1,0:T(8,128)(2,1)S(1)} %get-tuple-element.118), channel_id=1, source_target_pairs={{8,16},{12,20},{16,8},{20,12},{9,17},{13,21},{17,9},{21,13},{10,18... | collective-permute-start | bytes 1572872 | tf_op jit(solution)/shard_map/ppermute | solution.py:561
  87.1 21.4 %collective-permute-start.24 = (bf16[4,256,256]{2,1,0:T(8,128)(2,1)S(1)}, bf16[4,256,256]{2,1,0:T(8,128)(2,1)S(1)}, u32[]{:S(2)}, u32[]{:S(2)}) collective-permute-start(bf16[4,256,256]{2,1,0:T(8,128)(2,1)S(1)} %get-tuple-element.135), channel_id=1, source_target_pairs={{0,4},{4,0},{8,12},{12,8},{16,20},{20,16},{24,28},{28,24},{1,5},{5... | collective-permute-start | bytes 1572872 | tf_op jit(solution)/shard_map/ppermute | solution.py:576
  87.2 28.8 %collective-permute-start.23 = (bf16[4,256,256]{2,1,0:T(8,128)(2,1)S(1)}, bf16[4,256,256]{2,1,0:T(8,128)(2,1)S(1)}, u32[]{:S(2)}, u32[]{:S(2)}) collective-permute-start(bf16[4,256,256]{2,1,0:T(8,128)(2,1)S(1)} %get-tuple-element.133), channel_id=1, source_target_pairs={{16,24},{20,28},{8,0},{12,4},{17,25},{21,29},{9,1},{13,5},{18,26},... | collective-permute-start | bytes 1572872 | tf_op jit(solution)/shard_map/ppermute | solution.py:561
  88.5 1.7 %collective-permute-start.18 = (bf16[2,256,256]{2,1,0:T(8,128)(2,1)S(1)}, bf16[2,256,256]{2,1,0:T(8,128)(2,1)S(1)}, u32[]{:S(2)}, u32[]{:S(2)}) collective-permute-start(bf16[2,256,256]{2,1,0:T(8,128)(2,1)S(1)} %get-tuple-element.122), channel_id=1, source_target_pairs={{0,4},{4,0},{8,12},{12,8},{16,20},{20,16},{24,28},{28,24},{1,5},{5... | collective-permute-start | bytes 786440 | tf_op jit(solution)/shard_map/ppermute | solution.py:650
  102.0 16.1 %collective-permute-start.22 = (bf16[4,256,256]{2,1,0:T(8,128)(2,1)S(1)}, bf16[4,256,256]{2,1,0:T(8,128)(2,1)S(1)}, u32[]{:S(2)}, u32[]{:S(2)}) collective-permute-start(bf16[4,256,256]{2,1,0:T(8,128)(2,1)S(1)} %get-tuple-element.132), channel_id=1, source_target_pairs={{16,24},{20,28},{8,0},{12,4},{17,25},{21,29},{9,1},{13,5},{18,26},... | collective-permute-start | bytes 1572872 | tf_op jit(solution)/shard_map/ppermute | solution.py:561
  117.2 2.0 %collective-permute-start.26 = (bf16[4,256,256]{2,1,0:T(8,128)(2,1)S(1)}, bf16[4,256,256]{2,1,0:T(8,128)(2,1)S(1)}, u32[]{:S(2)}, u32[]{:S(2)}) collective-permute-start(bf16[4,256,256]{2,1,0:T(8,128)(2,1)S(1)} %get-tuple-element.144), channel_id=1, source_target_pairs={{0,4},{4,0},{8,12},{12,8},{16,20},{20,16},{24,28},{28,24},{1,5},{5... | collective-permute-start | bytes 1572872 | tf_op jit(solution)/shard_map/ppermute | solution.py:576
  120.2 8.1 %collective-permute-start.27 = (bf16[4,256,256]{2,1,0:T(8,128)(2,1)S(1)}, bf16[4,256,256]{2,1,0:T(8,128)(2,1)S(1)}, u32[]{:S(2)}, u32[]{:S(2)}) collective-permute-start(bf16[4,256,256]{2,1,0:T(8,128)(2,1)S(1)} %get-tuple-element.146), channel_id=1, source_target_pairs={{0,4},{4,0},{8,12},{12,8},{16,20},{20,16},{24,28},{28,24},{1,5},{5... | collective-permute-start | bytes 1572872 | tf_op jit(solution)/shard_map/ppermute | solution.py:576

commit v3 on v2

--- a/solution.py
+++ b/solution.py
@@ -52,9 +52,11 @@
 
 
 def start_kernel(
-    rows, place, pivot_ref, block_ref,
-    onehot_ref, owner_ref, me_ref, lands_ref, raw_a_ref, raw_b_ref, mine_ref, other_ref, token_ref,
+    rows, place, pivot_ref, matrix_ref, block_ref,
+    onehot_ref, owner_ref, me_ref, lands_ref, raw_ref, mine_ref, other_ref, top_ref, token_ref, sem,
 ):
+    copy = pltpu.make_async_copy(matrix_ref.at[0], top_ref, sem)
+    copy.start()
     cycles, width, size, _ = block_ref.shape
     chip, core = place[0], place[1]
     row = 2 * chip + core
@@ -112,11 +114,10 @@
         lands = [jnp.where(chip == 0, a, b) for a, b in zip(by_top, lands)]
         lands_ref[0:1] = jnp.where(swapped, lands[1], lands[0])
         lands_ref[1:2] = jnp.where(swapped, lands[0], lands[1])
-        half = raw_a_ref.shape[0]
-        raw_a_ref[...] = block_ref[:half, 0]
-        raw_b_ref[...] = block_ref[half:, 0]
+        raw_ref[...] = block_ref[:, 0]
 
     gather_step(onehot_ref, block_ref, mine_ref, other_ref)
+    copy.wait()
 
 
 def gather_step(onehot_ref, block_ref, mine_ref, other_ref):
@@ -144,40 +145,45 @@
 TOKEN = array(8, 128, dtype=F32)
 
 
-def start(place, pivots, matrix, count, width, rows):
-    cycles, _, size, _ = matrix.shape
+def start(place, pivots, matrix, width, rows):
+    cycles, blocks, size, _ = matrix.shape
     slots = STEPS * size
-    half = (cycles + 1) // 2
-    part = array(count, size, size)
-    part_spec = pl.BlockSpec((width, size, size), lambda j: (j, 0, 0))
+    part = array(width, size, size)
     outs = [
         array(slots, cycles * size),
         array(2, size, 1, dtype=I32),
         array(2, size, 1, dtype=I32),
         array(2, size, dtype=I32),
-        array(half, size, size),
-        array(cycles - half, size, size),
+        array(cycles, size, size),
+        part,
+        part,
     ]
     return pl.pallas_call(
         functools.partial(start_kernel, rows),
-        grid=(count // width,),
+        grid=(1,),
         in_specs=[
             SMEM,
             constant(pivots.shape),
-            pl.BlockSpec((cycles, width, size, size), lambda j: (0, j, 0, 0)),
+            ANY,
+            pl.BlockSpec((cycles, width, size, size), lambda j: (0, 0, 0, 0)),
         ],
-        out_specs=[constant(o.shape) for o in outs] + [part_spec, part_spec, ANY],
-        out_shape=outs + [part, part, TOKEN],
+        out_specs=[constant(o.shape) for o in outs] + [ANY, ANY],
+        out_shape=outs + [array(blocks, size, size), TOKEN],
+        scratch_shapes=[pltpu.SemaphoreType.DMA],
         compiler_params=params(),
         cost_estimate=CHEAP,
         name="start",
-    )(place, pivots, matrix)
+    )(place, pivots, matrix, matrix)
 
 
 class Chain:
     def __init__(self, token):
         self.token = token
         self.due = []
+        self.held = []
+
+    def hold(self, *arrays):
+        self.held = list(arrays)
 
     def need(self, *arrays):
         self.due += arrays
@@ -185,23 +191,30 @@
     def run(self, kernel, name, operands, in_specs, out_shape, out_specs, **options):
         operands, in_specs = list(operands), list(in_specs)
         given, made = len(operands), len(out_shape)
-        waits = [self.token, *self.due]
-        self.due = []
-
-        def body(*refs):
-            kernel(*refs[:given], *refs[given + len(waits) : given + len(waits) + made], *refs[given + len(waits) + made + 1 :])
-
-        *outs, self.token = pl.pallas_call(
-            body,
-            in_specs=in_specs + [ANY] * len(waits),
-            out_specs=list(out_specs) + [ANY],
-            out_shape=list(out_shape) + [TOKEN],
+        held, waits = self.held, [self.token, *self.due]
+        self.due, self.held = [], []
+        aliases = dict(options.pop("input_output_aliases", {}))
+        for i in range(len(held)):
+            aliases[given + len(waits) + i] = made + 1 + i
+        passed = len(held)
+
+        def inner(*refs):
+            outs = given + len(waits) + passed
+            kernel(*refs[:given], *refs[outs : outs + made], *refs[outs + made + 1 + passed :])
+
+        outs = pl.pallas_call(
+            inner,
+            in_specs=in_specs + [ANY] * (len(waits) + passed),
+            out_specs=list(out_specs) + [ANY] * (1 + passed),
+            out_shape=list(out_shape) + [TOKEN] + [array(*a.shape) for a in held],
+            input_output_aliases=aliases,
             compiler_params=params(),
             cost_estimate=CHEAP,
             name=name,
             **options,
-        )(*operands, *waits)
-        return outs
+        )(*operands, *waits, *held)
+        self.token, self.passed = outs[made], outs[made + 1 :]
+        return outs[:made]
 
     def whole(self, kernel, name, place, operands, out_shape, **options):
         return self.run(
@@ -224,7 +237,7 @@
         "gather_rows",
         (onehot, matrix),
         [
-            constant(onehot.shape),
+            VMEM,
             pl.BlockSpec((cycles, width, size, size), lambda j: (0, j + first // width, 0, 0)),
         ],
         [part, part],
@@ -233,14 +246,37 @@
     )
 
 
-def meet_kernel(place, mine_ref, theirs_ref, out_ref):
-    out_ref[...] = mine_ref[...] + theirs_ref[...]
+def meet_kernel(place, mine_ref, theirs_ref, *out_refs):
+    at = 0
+    for out_ref in out_refs:
+        count = out_ref.shape[0]
+        out_ref[...] = mine_ref[at : at + count] + theirs_ref[at : at + count]
+        at += count
+
+
+def meet_more_kernel(place, mine_ref, theirs_ref, extra_ref, out_ref):
+    count = mine_ref.shape[0]
+    out_ref[:count] = mine_ref[...] + theirs_ref[...]
+    out_ref[count:] = extra_ref[...]
+
+
+def lead_kernel(place, mine_ref, other_ref, out_ref):
+    out_ref[0] = mine_ref[0]
+    out_ref[1] = other_ref[0]
 
 
 def merge_kernel(place, owner_ref, native_ref, received_ref, out_ref):
     own = jnp.logical_or(place[0] == 0, owner_ref[0] == place[0])
     for b in range(out_ref.shape[0]):
         out_ref[b] = jnp.where(own, native_ref[b], received_ref[b])
+
+
+def merge_or_send_kernel(place, owner_ref, native_ref, received_ref, fresh_ref, out_ref, *, chips):
+    own = jnp.logical_or(place[0] == 0, owner_ref[0] == place[0])
+    end = jnp.logical_or(place[0] == 0, place[0] == chips - 1)
+    for b in range(out_ref.shape[0]):
+        merged = jnp.where(own, native_ref[b], received_ref[b])
+        out_ref[b] = jnp.where(end, fresh_ref[b], merged)
 
 
 def finish_kernel(place, owner_ref, me_ref, native_ref, *refs):
@@ -292,20 +328,37 @@
         keep_ref[cycle] = jnp.broadcast_to(1.0 - filled, (size, size)).astype(BF16)
 
 
+def placement(chain, place, lands, cycles):
+    size = lands.shape[1]
+    return chain.whole(
+        placement_kernel,
+        "placement",
+        place,
+        (lands,),
+        [array(cycles, size, STEPS * size), array(cycles, size, size)],
+    )
+
+
+def three_parts(a):
+    high = a.astype(BF16)
+    rest = a - high.astype(F32)
+    mid = rest.astype(BF16)
+    low = (rest - mid.astype(F32)).astype(BF16)
+    return jnp.concatenate([low, mid, high], 1)
+
+
+def sum_parts(a):
+    size = a.shape[1] // 3
+    return (a[:, :size] + a[:, size : 2 * size]) + a[:, 2 * size :]
+
+
 def newton_inverse(diag, identity):
     third = 1.0 / 3.0
-    approx = (2.0 * identity - diag * third) * third
+    approx = (2.0 * identity - diag.astype(F32) * third) * third
     for _ in range(NEWTON - 1):
-        approx = dot_full(approx, 2.0 * identity - dot_full(diag, approx))
+        product = sum_parts(dot(diag, three_parts(approx)))
+        approx = dot_full(approx, 2.0 * identity - product)
     return approx
-
-
-def split_dot(a, b):
-    high = b.astype(BF16)
-    rest = b - high.astype(F32)
-    mid = rest.astype(BF16)
-    low = (rest - mid.astype(F32)).astype(BF16)
-    return dot(a, low) + dot(a, mid) + dot(a, high)
 
 
 def whole_rows(place, me_ref, own_mine, own_other, x_mine, x_other):
@@ -350,45 +403,49 @@
     if len(pieces) == 2:
         fetch(((pieces[0],), (pieces[1],)))
     else:
-        own, down, over = pieces[:2], pieces[2:4], pieces[4:]
+        own, down, over = ((piece,) for piece in pieces)
         for col, pairs in enumerate(((own, over), (over, own), (down, over), (over, down))):
 
             @pl.when(place[2] == col)
             def _(pairs=pairs):
                 fetch(pairs)
 
+    flat = [raw.reshape(cycles * size, size)[...] for raw in (raw0, raw1)]
+    own = dot(onehot_ref[...], jnp.concatenate(flat, 1)).astype(BF16)
     new0, new1, old = [], [], []
     for b, raw in enumerate((raw0, raw1)):
-        own = dot(onehot_ref[...], raw.reshape(cycles * size, size)[...]).astype(BF16)
-        upper, below = whole_rows(place, me_ref, own[:size], own[size:], xm_ref[b], xo_ref[b])
+        mine, other = own[:size, b * size : (b + 1) * size], own[size:, b * size : (b + 1) * size]
+        upper, below = whole_rows(place, me_ref, mine, other, xm_ref[b], xo_ref[b])
         new0.append(upper)
         new1.append(below)
         old.append(old_rows(place, xm_ref[b], xo_ref[b], raw[0], top_ref[b]))
+    old = jnp.concatenate(old, 1)
     identity = jnp.where(iota((size, size), 0) == iota((size, size), 1), 1.0, 0.0).astype(F32)
-    inverse0 = newton_inverse(new0[0].astype(F32), identity)
-    corner = split_dot(new1[0], inverse0).astype(BF16)
+    inverse0 = three_parts(newton_inverse(new0[0], identity))
+    corner = sum_parts(dot(new1[0], inverse0)).astype(BF16)
     corner_ref[...] = corner
-    inverse1 = newton_inverse(
-        (new1[1].astype(F32) - dot(corner, new0[1])).astype(BF16).astype(F32), identity
+    inverse1 = three_parts(
+        newton_inverse((new1[1].astype(F32) - dot(corner, new0[1])).astype(BF16), identity)
     )
     for cycle in range(cycles):
         put = put_ref[cycle]
         keep = keep_ref[cycle]
-        left = (dot(put, old[0]) + (keep * raw0[cycle]).astype(F32)).astype(BF16)
-        right = dot(put, old[1]) + (keep * raw1[cycle]).astype(F32)
+        both = dot(put, old)
+        left = (both[:, :size] + (keep * raw0[cycle]).astype(F32)).astype(BF16)
+        right = both[:, size:] + (keep * raw1[cycle]).astype(F32)
         if cycle == 0:
             left = jnp.where(row == 0, new0[0], jnp.where(row == 1, new1[0], left))
             right = jnp.where(
                 row == 0, new0[1].astype(F32), jnp.where(row == 1, new1[1].astype(F32), right)
             )
-        lower = split_dot(left, inverse0)
+        lower = sum_parts(dot(left, inverse0))
         if cycle == 0:
             lower = jnp.where(row == 0, 0.0, lower)
         lower = lower.astype(BF16)
         side_ref[cycle, :, :slots] = put
         side_ref[cycle, :, slots:] = -lower
         right = (right - dot(lower, new0[1])).astype(BF16)
-        lower = split_dot(right, inverse1)
+        lower = sum_parts(dot(right, inverse1))
         if cycle == 0:
             lower = jnp.where(row <= 1, 0.0, lower)
         lower1_ref[cycle] = lower.astype(BF16)
@@ -396,12 +453,11 @@
 
 def factor_panels(chain, place, me, rows, tops, onehot, put, keep, pieces):
     cycles, size, _ = keep.shape
-    operands = (place, me, *rows, tops, onehot, put, keep)
     return chain.run(
         panel_kernel,
         "factor_panels",
-        (*operands, *pieces),
-        [SMEM] + [VMEM] * (len(operands) - 1) + [ANY] * len(pieces),
+        (place, me, *rows, tops, onehot, put, keep, *pieces),
+        [SMEM] + [VMEM] * 7 + [ANY] * len(pieces),
         [
             array(cycles, size, (STEPS + 1) * size),
             array(cycles, size, size),
@@ -411,29 +467,42 @@
         scratch_shapes=[
             pltpu.VMEM((cycles, size, size), BF16),
             pltpu.VMEM((cycles, size, size), BF16),
-            pltpu.SemaphoreType.DMA((len(pieces),)),
+            pltpu.SemaphoreType.DMA((4,)),
         ],
     )
 
 
-def update_kernel(
-    first, place, me_ref, block_ref, native_ref, own_ref, xm_ref, xo_ref, top_ref,
-    side_ref, keep_ref, lower1_ref, corner_ref, *rest,
-):
-    out_ref = rest[-1]
+def update_kernel(first, counts, place, me_ref, block_ref, top_ref, *rest):
+    sets = [rest[4 * i : 4 * i + 4] for i in range(len(counts))]
+    side_ref, keep_ref, lower1_ref, corner_ref = rest[4 * len(counts) : 4 * len(counts) + 4]
+    out_ref, both_ref, below_ref = rest[-3:]
     cycles, width, size, _ = block_ref.shape
+    at = pl.program_id(0) * width
     row = 2 * place[0] + place[1]
     slots = STEPS * size
-    upper, below, old = [], [], []
-    for b in range(width):
-        u, n = whole_rows(place, me_ref, native_ref[b], own_ref[b], xm_ref[b], xo_ref[b])
-        upper.append(u)
-        below.append(n)
-        old.append(old_rows(place, xm_ref[b], xo_ref[b], block_ref[0, b], top_ref[b]))
+    start = 0
+    for (native_ref, own_ref, xm_ref, xo_ref), count in zip(sets, counts):
+
+        def prepare(start=start, native_ref=native_ref, own_ref=own_ref, xm_ref=xm_ref, xo_ref=xo_ref):
+            for b in range(width):
+                i = at + (b - start)
+                xm, xo = xm_ref[i], xo_ref[i]
+                upper, below = whole_rows(place, me_ref, native_ref[i], own_ref[i], xm, xo)
+                old = old_rows(place, xm, xo, block_ref[0, b], top_ref[b])
+                part = slice(b * size, (b + 1) * size)
+                both_ref[:slots, part] = old
+                both_ref[slots:, part] = upper
+                below_ref[:, part] = below
+
+        if len(counts) == 1:
+            prepare()
+        else:
+            pl.when(jnp.logical_and(at >= start, at < start + count))(prepare)
+        start += count
     join = lambda parts: parts[0] if width == 1 else jnp.concatenate(parts, 1)
-    upper, below, old = join(upper), join(below), join(old)
-    upper1 = (below.astype(F32) - dot(corner_ref[...], upper)).astype(BF16)
-    both = jnp.concatenate([old, upper], 0)
+    both = both_ref[...]
+    upper = both[slots:]
+    upper1 = (below_ref[...].astype(F32) - dot(corner_ref[...], upper)).astype(BF16)
     for cycle in range(cycles):
         keep = keep_ref[cycle]
         kept = join([block_ref[cycle, b] * keep for b in range(width)])
@@ -464,30 +533,33 @@
                 out_ref[cycle, 0] = block
 
 
-def update_columns(chain, place, me, matrix, rows, top, factors, first, count, width, result):
+def update_columns(chain, place, me, matrix, sets, top, factors, first, width, result):
     cycles, blocks, size, _ = matrix.shape
-    column = pl.BlockSpec((width, size, size), lambda j: (j, 0, 0))
-    blocks_spec = pl.BlockSpec(
-        (cycles, width, size, size), lambda j: (0, j + first // width, 0, 0)
-    )
-    operands = [place, me, matrix, *rows, top, *factors]
-    in_specs = [SMEM, constant(me.shape), blocks_spec]
-    in_specs += [column] * 4
-    in_specs += [pl.BlockSpec((width, size, size), lambda j: (j + first // width, 0, 0))]
-    in_specs += [constant(f.shape) for f in factors]
+    counts = [s[0].shape[0] for s in sets]
+    rows = [r for s in sets for r in s]
+    at = lambda j: j + first // width
+    blocks_spec = pl.BlockSpec((cycles, width, size, size), lambda j: (0, at(j), 0, 0))
+    top_spec = pl.BlockSpec((width, size, size), lambda j: (at(j), 0, 0))
+    operands = [place, me, matrix, top, *rows, *factors]
+    in_specs = [SMEM, VMEM, blocks_spec, top_spec]
+    in_specs += [VMEM] * (len(rows) + len(factors))
     aliases = {}
     if result is not None:
         aliases = {len(operands): 0}
         operands.append(result)
         in_specs.append(ANY)
     return chain.run(
-        functools.partial(update_kernel, first),
+        functools.partial(update_kernel, first, counts),
         "update_columns",
         operands,
         in_specs,
         [array(*matrix.shape)],
         [blocks_spec],
-        grid=(count // width,),
+        grid=(sum(counts) // width,),
+        scratch_shapes=[
+            pltpu.VMEM(((STEPS + 1) * size, width * size), BF16),
+            pltpu.VMEM((size, width * size), BF16),
+        ],
         input_output_aliases=aliases,
     )[0]
 
@@ -495,8 +567,8 @@
 def split_blocks(blocks):
     width = 2 if blocks % 2 == 0 else 1
     base, extra = divmod(blocks // width - 1, 3)
-    counts = [1] + [base + (1 if i < extra else 0) for i in range(3)]
-    return width, [width * c for c in counts]
+    counts = [width] + [width * (base + (1 if i < extra else 0)) for i in range(3)]
+    return width, [(sum(counts[:i]), c) for i, c in enumerate(counts)]
 
 
 def body(matrix, pivots):
@@ -509,10 +581,9 @@
     plain = matrix.transpose(0, 2, 1, 3)
     matrix = pltpu.with_memory_space_constraint(plain, pltpu.HBM)
     place = jnp.stack([row // 2, row % 2, col]).astype(I32)
-    width, counts = split_blocks(blocks)
-    starts = [sum(counts[:i]) for i in range(len(counts))]
+    width, chunks = split_blocks(blocks)
+    count = len(chunks)
     few_cols = cols == 4
-    half = (cycles + 1) // 2
 
     swap = [(r, r ^ 1) for r in range(rows)]
     first_swap = [(0, 1), (1, 0)]
@@ -525,154 +596,156 @@
             pairs += [(2 * a, 2 * b), (2 * a + 1, 2 * b + 1)]
         return pairs
 
-    onehot, owner, me, lands, raw_a, raw_b, mine, other, token = start(
-        place, pivots, matrix, counts[0], width, rows
+    onehot, owner, me, lands, raw, mine, other, top, token = start(
+        place, pivots, matrix, width, rows
     )
     chain = Chain(token)
-    native, others, theirs, x_mine, x_send, x_other = {0: mine}, {0: other}, {}, {}, {}, {}
-    hops = {i: [] for i in range(len(counts))}
-    received = {i: [] for i in range(len(counts))}
-
-    def swap_others(*chunks):
-        own = [others[i] for i in chunks]
-        own = own[0] if len(own) == 1 else jnp.concatenate(own, 0)
-        theirs[chunks] = lax.ppermute(own, "row", swap)
-
-    def gather(i, count):
-        a, b = gather_rows(chain, matrix, onehot, starts[i], count, width)
-        return a, b
-
-    def meet(mine, theirs):
-        return chain.whole(meet_kernel, "meet", place, (mine, theirs), [array(*mine.shape)])[0]
+    native, others, x_mine, x_send, x_other = {}, {}, {}, {}, {}
+    hops = {i: [] for i in range(count)}
+
+    def exchange(own):
+        return lax.ppermute(own, "row", swap)
+
+    def gather(i, blocks):
+        return gather_rows(chain, matrix, onehot, chunks[i][0], blocks, width)
+
+    def meet(mine, theirs, *counts):
+        return chain.whole(
+            meet_kernel, "meet", place, (mine, theirs), [array(c, size, size) for c in counts]
+        )
 
     def hop(i):
         h = len(hops[i])
-        if h == 0:
-            out = native[i]
-        else:
-            received[i].append(hops[i][h - 1])
-            out = chain.whole(
+        out = native[i]
+        if h:
+            (out,) = chain.whole(
                 merge_kernel,
                 "merge",
                 place,
-                (owner, native[i], received[i][h - 1]),
+                (owner, native[i], hops[i][-1]),
                 [array(*native[i].shape)],
-            )[0]
+            )
         hops[i].append(lax.ppermute(out, "row", hop_pairs(h)))
 
     def finish(i):
         while len(hops[i]) < chips - 1:
             hop(i)
-        received[i].append(hops[i][-1])
         x_mine[i], x_send[i] = chain.whole(
             finish_kernel,
             "finish",
             place,
-            (owner, me, native[i], *received[i]),
+            (owner, me, native[i], *hops[i]),
             [array(*native[i].shape)] * 2,
         )
-
-    def exchange(i):
-        x_other[i] = lax.ppermute(x_send[i], "row", swap)
-
-    def side(own, down, axis_pairs=side_pairs):
-        out = chain.whole(side_kernel, "side", place, (own, down), [array(*own.shape)])[0]
+        x_other[i] = exchange(x_send[i])
+
+    def side(own, down):
+        (out,) = chain.whole(side_kernel, "side", place, (own, down), [array(*own.shape)])
         return lax.ppermute(out, "col", side_pairs)
+
+    def down(own):
+        return lax.ppermute(own, "col", down_pairs)
+
+    def pair(own, down, side, made):
+        return chain.whole(
+            pair_kernel, "pair", place, (own, down, side), [array(2, size, size)] * made
+        )
 
     def from_two(own):
         zero = jnp.zeros_like(own)
         return lax.psum(jnp.stack([jnp.where(col == b, own, zero) for b in range(2)]), "col")
 
-    theirs0 = lax.ppermute(other, "row", swap)
+    def hop_both(i, j):
+        if chips != 4 or native[i].shape != native[j].shape:
+            hop(i)
+            hop(j)
+            return
+        (out,) = chain.whole(
+            functools.partial(merge_or_send_kernel, chips=chips),
+            "merge",
+            place,
+            (owner, native[i], hops[i][-1], native[j]),
+            [array(*native[i].shape)],
+        )
+        arrived = lax.ppermute(out, "row", hop_pairs(0) + hop_pairs(2))
+        hops[i].append(arrived)
+        hops[j].append(arrived)
+
+    native[0], others[0] = mine, other
+    theirs0 = exchange(other)
     if few_cols:
-        down_a = lax.ppermute(raw_a, "col", down_pairs)
-        down_b = lax.ppermute(raw_b, "col", down_pairs)
-    native[1], others[1] = gather(1, counts[1])
-    theirs1 = lax.ppermute(others[1], "row", swap)
-    native[0] = meet(mine, theirs0)
+        down_raw = down(raw)
+    sizes = [c for _, c in chunks]
+    cut = sizes[1]
+    some_mine, some_other = gather(1, sizes[1] + sizes[2])
+    chain.hold(some_other)
+    (native[0],) = meet(mine, theirs0, width)
+    (some_other,) = chain.passed
     hop(0)
-    native[1] = meet(native[1], theirs1)
+    some_theirs = exchange(some_other)
+    others[1], others[2] = some_other[:cut], some_other[cut:]
+    mine3, others[3] = gather(3, sizes[3])
+    chain.hold(others[3])
+    native[1], native[2] = meet(some_mine, some_theirs, sizes[1], sizes[2])
+    (others[3],) = chain.passed
     hop(1)
-    rest_mine, rest_other = gather(2, counts[2] + counts[3])
-    rest_theirs = lax.ppermute(rest_other, "row", swap)
+    theirs3 = exchange(others[3])
+    chain.hold(native[2])
     hop(0)
+    (native[2],) = chain.passed
+    hop(2)
+    put, keep = placement(chain, place, lands, cycles)
     if few_cols:
-        side_a = side(raw_a, down_a)
-    rest = meet(rest_mine, rest_theirs)
-    cut = counts[2]
-    native[2], native[3] = rest[:cut], rest[cut:]
-    others[2], others[3] = rest_other[:cut], rest_other[cut:]
-    hop(2)
+        side_raw = side(raw, down_raw)
+    hop(0)
+    (native[3],) = meet(mine3, theirs3, sizes[3])
+    hop(1)
+    finish(0)
+    (lead,) = chain.whole(
+        lead_kernel, "lead", place, (x_mine[0], x_other[0]), [array(2, size, size)]
+    )
     if few_cols:
-        side_b = side(raw_b, down_b)
-    hop(0)
-    hop(1)
-    put, keep = chain.whole(
-        placement_kernel,
-        "placement",
-        place,
-        (lands,),
-        [array(cycles, size, STEPS * size), array(cycles, size, size)],
-    )
-    if few_cols:
-        chain.need(side_a)
-    finish(0)
-    lead = jnp.stack([x_mine[0][0], x_send[0][0]])
-    if few_cols:
-        down_lead = lax.ppermute(lead, "col", down_pairs)
+        down_lead = down(lead)
     else:
         leads = from_two(lead)
-        raws = from_two(jnp.concatenate([raw_a, raw_b], 0))
-    hop(3)
     hop(2)
-    if few_cols:
-        chain.need(side_b)
-    hop(1)
-    exchange(0)
+    hop_both(1, 3)
     if few_cols:
         side_lead = side(lead, down_lead)
-        (firsts,) = chain.whole(
-            pair_kernel, "pair", place, (raw_a, down_a, side_a), [array(2, size, size)]
-        )
-        pieces = [raw_a, raw_b, down_a, down_b, side_a, side_b]
+    if few_cols:
+        (firsts,) = pair(raw, down_raw, side_raw, 1)
     else:
+        raws = from_two(raw)
         firsts = raws[:, 0]
+    tops = lax.ppermute(firsts, "row", first_swap)
+    if few_cols:
+        panel_mine, panel_other = pair(lead, down_lead, side_lead, 2)
+        pieces = [raw, down_raw, side_raw]
+    else:
+        panel_mine, panel_other = leads[:, 0], leads[:, 1]
         pieces = [raws[0], raws[1]]
-    chain.need(x_other[0])
-    tops = lax.ppermute(firsts, "row", first_swap)
+    hop(2)
     hop(3)
-    if few_cols:
-        panel_mine, panel_send = chain.whole(
-            pair_kernel, "pair", place, (lead, down_lead, side_lead), [array(2, size, size)] * 2
-        )
-    else:
-        panel_mine, panel_send = leads[:, 0], leads[:, 1]
-    panel_other = lax.ppermute(panel_send, "row", swap)
-    top = lax.ppermute(plain[0], "row", first_swap)
-    hop(2)
     finish(1)
-    exchange(1)
     side_rows, lower1, corner = factor_panels(
         chain, place, me, (panel_mine, panel_other), tops, onehot, put, keep, pieces
     )
     factors = (side_rows, keep, lower1, corner)
 
-    def update(i, result):
+    def update(which, result):
+        sets = [(native[i], others[i], x_mine[i], x_other[i]) for i in which]
         return update_columns(
-            chain, place, me, matrix, (native[i], others[i], x_mine[i], x_other[i]), top,
-            factors, starts[i], counts[i], width, result,
+            chain, place, me, matrix, sets, top, factors, chunks[which[0]][0], width, result
         )
 
+    finish(2)
+    chain.hold(top)
     hop(3)
-    result = update(0, None)
-    result = update(1, result)
-    finish(2)
-    exchange(2)
-    chain.need(x_other[2])
+    (top,) = chain.passed
+    top = lax.ppermute(top, "row", first_swap)
+    result = update((0, 1, 2), None)
     finish(3)
-    exchange(3)
-    result = update(2, result)
-    result = update(3, result)
+    result = update((3,), result)
     return result.transpose(0, 2, 1, 3)
 
 

time: 137 us -> 126 us (0.920)
  Pallas kernels: 68.3 us -> 62.9 us
  starting transfers between devices: 43.9 us -> 39.6 us
  local copies, waits for them, and re-layouts: 2.46 us -> 0.75 us
  waiting for transfers between devices: 20.5 us -> 22 us
    ppermute x12 -> x10, waiting for transfers between devices: 11.2 us -> 0.03 us  [hop(): hops[i].append(lax.ppermute(out, 'row', hop_pairs(h)))]
    ppermute x12 -> x11, waiting for transfers between devices: 6.31 us -> 14.4 us  [the longest x2 7.91 us: down(): return lax.ppermute(own, 'col', down_pairs)]
    ppermute x12 -> x10, starting transfers between devices: 22.5 us -> 16 us  [hop(): hops[i].append(lax.ppermute(out, 'row', hop_pairs(h)))]
    pallas_call x29 -> x27, Pallas kernels: 68.3 us -> 62.9 us  [the longest x26 58.7 us: run(): pl.pallas_call(inner, in_specs=in_specs + [ANY] * (len(waits) + passed),...]
    ppermute x3 -> x2, waiting for transfers between devices: 2.94 us -> 7.11 us  [side(): return lax.ppermute(out, 'col', side_pairs)]
    ppermute x12 -> x11, starting transfers between devices: 14.8 us -> 18.5 us  [the longest x2 9.32 us: down(): return lax.ppermute(own, 'col', down_pairs)]
    squeeze x1 -> x0, local copies, waits for them, and re-layouts: 1.62 us -> none  [body(): top = lax.ppermute(plain[0], 'row', first_swap)]
    ppermute x3 -> x2, starting transfers between devices: 4.67 us -> 3.11 us  [side(): return lax.ppermute(out, 'col', side_pairs)]
  transfers between devices with their start and end apart: 28 -> 24, of which waited for: 11 -> 8; matrix products, arithmetic and copies ran while one was open for 1% -> 0% of each run, Pallas kernels for 33% -> 39%
where the time goes in v3:
time: 126 us
  Pallas kernels  62.9 us (50%)
  starting transfers between devices  39.6 us (31%)
  waiting for transfers between devices  22 us (17%)
    pallas_call x26, Pallas kernels, run(): pl.pallas_call(inner, in_specs=in_specs + [ANY] * (len(waits) + passed),...  58.7 us
    ppermute x10, starting transfers between devices, hop(): hops[i].append(lax.ppermute(out, 'row', hop_pairs(h)))  16 us
    ppermute x2, starting transfers between devices, down(): return lax.ppermute(own, 'col', down_pairs)  9.32 us
    ppermute x2, waiting for transfers between devices, down(): return lax.ppermute(own, 'col', down_pairs)  7.91 us
    ppermute x2, waiting for transfers between devices, side(): return lax.ppermute(out, 'col', side_pairs)  7.11 us
    ppermute x7, waiting for transfers between devices, exchange(): return lax.ppermute(own, 'row', swap)  6.49 us
    ppermute x1, starting transfers between devices, hop_both(): arrived = lax.ppermute(out, 'row', hop_pairs(0) + hop_pairs(2))  5.63 us
    pallas_call x1, Pallas kernels, start(): pl.pallas_call(functools.partial(start_kernel, rows), grid=(1,), in_specs...  4.2 us
  transfers between devices with their start and end apart: 24, of which 8 were waited for; matrix products, arithmetic and copies ran while one was open for 0% of the time, Pallas kernels for 39%

profile of v3, /device:TPU:0, one launch (start us, length us, event | category | flops | bytes accessed | tf_op | source)
XLA Modules:
  0.0 125.7 jit_solution(15683767569783919457)
XLA Ops:
  0.8 4.2 %start.1 = (bf16[512,1792]{1,0:T(8,128)(2,1)S(1)}, s32[2,256,1]{2,1,0:T(8,128)S(1)}, s32[2,256,1]{2,1,0:T(8,128)S(1)}, s32[2,256]{1,0:T(2,128)S(1)}, bf16[7,256,...) custom-call(s32[3]{0:T(128)S(1)} %pad_add_fusion.place.refs_0_, ...), custom_call_target="tpu_custom_call" | custom-call | flops 1024 | bytes 1024 | tf_op jit(solution)/shard_map/start/pallas_call | solution.py:161
  5.5 6.5 %gather_rows.2 = (bf16[8,256,256]{2,1,0:T(8,128)(2,1)S(1)}, bf16[8,256,256]{2,1,0:T(8,128)(2,1)S(1)}, f32[8,128]{1,0:T(8,128)S(1)}) custom-call(bf16[512,1792]{1,0:T(8,128)(2,1)S(1)} %get-tuple-element.82.refs_0_.refs_5_, bf16[7,14,256,256]{3,2,1,0:T(8,128)(2,1)} %bitcast.7, f32[8,128]{1,0:T(8,128)S(1)} %get-tuple-element.85.refs_2_), custom_call_target="tpu_custom_call" | custom-call | flops 1024 | bytes 1024 | tf_op jit(solution)/shard_map/gather_rows/pallas_call | solution.py:205
  12.7 4.9 %collective-permute-start.5 = (bf16[7,256,256]{2,1,0:T(8,128)(2,1)S(1)}, bf16[7,256,256]{2,1,0:T(8,128)(2,1)S(1)}, u32[]{:S(2)}, u32[]{:S(2)}) collective-permute-start(bf16[7,256,256]{2,1,0:T(8,128)(2,1)S(1)} %get-tuple-element.99.refs_1_.refs_8_), channel_id=1, source_target_pairs={{0,2},{1,3},{4,6},{5,7},{8,10},{9,11},{12,14},{13,15},{16,18},{17,... | collective-permute-start | bytes 2752520 | tf_op jit(solution)/shard_map/ppermute | solution.py:647
  17.6 3.5 %collective-permute-start.3 = (bf16[2,256,256]{2,1,0:T(8,128)(2,1)S(1)}, bf16[2,256,256]{2,1,0:T(8,128)(2,1)S(1)}, u32[]{:S(2)}, u32[]{:S(2)}) collective-permute-start(bf16[2,256,256]{2,1,0:T(8,128)(2,1)S(1)} %get-tuple-element.95.refs_2_.refs_3_.refs_4_), channel_id=1, source_target_pairs={{0,8},{4,12},{24,16},{28,20},{1,9},{5,13},{25,17},{29,21},{2,10},{... | collective-permute-start | bytes 786440 | tf_op jit(solution)/shard_map/ppermute | solution.py:628
  21.1 3.8 %gather_rows.3 = (bf16[4,256,256]{2,1,0:T(8,128)(2,1)S(1)}, bf16[4,256,256]{2,1,0:T(8,128)(2,1)S(1)}, f32[8,128]{1,0:T(8,128)S(1)}) custom-call(bf16[512,1792]{1,0:T(8,128)(2,1)S(1)} %get-tuple-element.82.refs_0_.refs_5_, bf16[7,14,256,256]{3,2,1,0:T(8,128)(2,1)} %bitcast.8, f32[8,128]{1,0:T(8,128)S(1)} %get-tuple-element.88.refs_2_), custom_call_target="tpu_custom_call" | custom-call | flops 1024 | bytes 1024 | tf_op jit(solution)/shard_map/gather_rows/pallas_call | solution.py:205
  25.7 1.3 %collective-permute-start.6 = (bf16[4,256,256]{2,1,0:T(8,128)(2,1)S(1)}, bf16[4,256,256]{2,1,0:T(8,128)(2,1)S(1)}, u32[]{:S(2)}, u32[]{:S(2)}) collective-permute-start(bf16[4,256,256]{2,1,0:T(8,128)(2,1)S(1)} %get-tuple-element.106.refs_2_.refs_3_.refs_8_), channel_id=1, source_target_pairs={{0,8},{4,12},{24,16},{28,20},{1,9},{5,13},{25,17},{29,21},{2,10},{... | collective-permute-start | bytes 1572872 | tf_op jit(solution)/shard_map/ppermute | solution.py:628
  28.4 1.1 placement.1
  29.4 7.9 %collective-permute-done.5.refs_2_.refs_9_ = bf16[7,256,256]{2,1,0:T(8,128)(2,1)S(1)} collective-permute-done((bf16[7,256,256]{2,1,0:T(8,128)(2,1)S(1)}, bf16[7,256,256]{2,1,0:T(8,128)(2,1)S(1)}, u32[]{:S(2)}, u32[]{:S(2)}) %collective-permute-start.5) | collective-permute-done | bytes 917536 | tf_op jit(solution)/shard_map/ppermute | solution.py:647
  38.7 1.3 %collective-permute-start.9 = (bf16[2,256,256]{2,1,0:T(8,128)(2,1)S(1)}, bf16[2,256,256]{2,1,0:T(8,128)(2,1)S(1)}, u32[]{:S(2)}, u32[]{:S(2)}) collective-permute-start(bf16[2,256,256]{2,1,0:T(8,128)(2,1)S(1)} %get-tuple-element.110), channel_id=1, source_target_pairs={{16,24},{20,28},{8,0},{12,4},{17,25},{21,29},{9,1},{13,5},{18,26},... | collective-permute-start | bytes 786440 | tf_op jit(solution)/shard_map/ppermute | solution.py:628
  40.0 4.6 %collective-permute-start.8 = (bf16[4,256,256]{2,1,0:T(8,128)(2,1)S(1)}, bf16[4,256,256]{2,1,0:T(8,128)(2,1)S(1)}, u32[]{:S(2)}, u32[]{:S(2)}) collective-permute-start(bf16[4,256,256]{2,1,0:T(8,128)(2,1)S(1)} %get-tuple-element.109.refs_2_.refs_3_.refs_12_), channel_id=1, source_target_pairs={{0,8},{4,12},{24,16},{28,20},{1,9},{5,13},{25,17},{29,21},{2,10},{... | collective-permute-start | bytes 1572872 | tf_op jit(solution)/shard_map/ppermute | solution.py:628
  46.6 1.6 %collective-permute-start.15 = (bf16[7,256,256]{2,1,0:T(8,128)(2,1)S(1)}, bf16[7,256,256]{2,1,0:T(8,128)(2,1)S(1)}, u32[]{:S(2)}, u32[]{:S(2)}) collective-permute-start(bf16[7,256,256]{2,1,0:T(8,128)(2,1)S(1)} %get-tuple-element.122), channel_id=1, source_target_pairs={{0,1},{1,0},{2,3},{3,2},{4,5},{5,4},{6,7},{7,6},{8,9},{9,8},{10,11... | collective-permute-start | bytes 2752520 | tf_op jit(solution)/shard_map/ppermute | solution.py:644
  48.1 0.9 finish.4
  49.1 1.5 %collective-permute-done.10.refs_2_.refs_7_ = bf16[2,256,256]{2,1,0:T(8,128)(2,1)S(1)} collective-permute-done((bf16[2,256,256]{2,1,0:T(8,128)(2,1)S(1)}, bf16[2,256,256]{2,1,0:T(8,128)(2,1)S(1)}, u32[]{:S(2)}, u32[]{:S(2)}) %collective-permute-start.10) | collective-permute-done | bytes 262176 | tf_op jit(solution)/shard_map/ppermute | solution.py:607
  51.2 4.4 %collective-permute-start.13 = (bf16[2,256,256]{2,1,0:T(8,128)(2,1)S(1)}, bf16[2,256,256]{2,1,0:T(8,128)(2,1)S(1)}, u32[]{:S(2)}, u32[]{:S(2)}) collective-permute-start(bf16[2,256,256]{2,1,0:T(8,128)(2,1)S(1)} %get-tuple-element.119.refs_1_), channel_id=1, source_target_pairs={{0,2},{1,3},{4,6},{5,7},{8,10},{9,11},{12,14},{13,15},{16,18},{17,... | collective-permute-start | bytes 786440 | tf_op jit(solution)/shard_map/ppermute | solution.py:647
  57.0 0.7 merge.12
  57.7 5.6 %collective-permute-start.11 = (bf16[4,256,256]{2,1,0:T(8,128)(2,1)S(1)}, bf16[4,256,256]{2,1,0:T(8,128)(2,1)S(1)}, u32[]{:S(2)}, u32[]{:S(2)}) collective-permute-start(bf16[4,256,256]{2,1,0:T(8,128)(2,1)S(1)} %get-tuple-element.117), channel_id=1, source_target_pairs={{0,8},{4,12},{24,16},{28,20},{16,24},{20,28},{8,0},{12,4},{1,9},{5... | collective-permute-start | bytes 1572872 | tf_op jit(solution)/shard_map/ppermute | solution.py:670
  63.9 1.6 %collective-permute-start.14 = (bf16[2,256,256]{2,1,0:T(8,128)(2,1)S(1)}, bf16[2,256,256]{2,1,0:T(8,128)(2,1)S(1)}, u32[]{:S(2)}, u32[]{:S(2)}) collective-permute-start(bf16[2,256,256]{2,1,0:T(8,128)(2,1)S(1)} %get-tuple-element.121), channel_id=1, source_target_pairs={{0,1},{1,0},{2,3},{3,2},{4,5},{5,4},{6,7},{7,6},{8,9},{9,8},{10,11... | collective-permute-start | bytes 786440 | tf_op jit(solution)/shard_map/ppermute | solution.py:644
  65.5 4.5 %collective-permute-done.15.refs_3_.refs_10_ = bf16[7,256,256]{2,1,0:T(8,128)(2,1)S(1)} collective-permute-done((bf16[7,256,256]{2,1,0:T(8,128)(2,1)S(1)}, bf16[7,256,256]{2,1,0:T(8,128)(2,1)S(1)}, u32[]{:S(2)}, u32[]{:S(2)}) %collective-permute-start.15) | collective-permute-done | bytes 917536 | tf_op jit(solution)/shard_map/ppermute | solution.py:644
  70.5 2.6 %collective-permute-done.14.refs_3_ = bf16[2,256,256]{2,1,0:T(8,128)(2,1)S(1)} collective-permute-done((bf16[2,256,256]{2,1,0:T(8,128)(2,1)S(1)}, bf16[2,256,256]{2,1,0:T(8,128)(2,1)S(1)}, u32[]{:S(2)}, u32[]{:S(2)}) %collective-permute-start.14) | collective-permute-done | bytes 262176 | tf_op jit(solution)/shard_map/ppermute | solution.py:644
  74.4 1.3 %collective-permute-start.17 = (bf16[4,256,256]{2,1,0:T(8,128)(2,1)S(1)}, bf16[4,256,256]{2,1,0:T(8,128)(2,1)S(1)}, u32[]{:S(2)}, u32[]{:S(2)}) collective-permute-start(bf16[4,256,256]{2,1,0:T(8,128)(2,1)S(1)} %get-tuple-element.128), channel_id=1, source_target_pairs={{16,24},{20,28},{8,0},{12,4},{17,25},{21,29},{9,1},{13,5},{18,26},... | collective-permute-start | bytes 1572872 | tf_op jit(solution)/shard_map/ppermute | solution.py:628
  77.1 1.9 %collective-permute-start.18 = (bf16[2,256,256]{2,1,0:T(8,128)(2,1)S(1)}, bf16[2,256,256]{2,1,0:T(8,128)(2,1)S(1)}, u32[]{:S(2)}, u32[]{:S(2)}) collective-permute-start(bf16[2,256,256]{2,1,0:T(8,128)(2,1)S(1)} %get-tuple-element.131), channel_id=1, source_target_pairs={{0,4},{4,0},{1,5},{5,1},{2,6},{6,2},{3,7},{7,3}} | collective-permute-start | bytes 786440 | tf_op jit(solution)/shard_map/ppermute | solution.py:720
  79.0 1.0 finish.5
  80.5 10.0 %factor_panels.1 = (bf16[7,256,768]{2,1,0:T(8,128)(2,1)S(1)}, bf16[7,256,256]{2,1,0:T(8,128)(2,1)S(1)}, bf16[256,256]{1,0:T(8,128)(2,1)S(1)}, f32[8,128]{1,0:T(8,128)S(1)}) custom-call(s32[3]{0:T(128)S(1)} %pad_add_fusion.place.refs_0_, s32[2,256,1]{2,1,0:T(8,128)S(1)} %get-tuple-element.80.refs_2_.refs_1_, ...), custom_call_target="tpu_custom_call" | custom-call | flops 1024 | bytes 1024 | tf_op jit(solution)/shard_map/factor_panels/pallas_call | solution.py:205
  90.6 1.0 finish.6
  92.3 2.0 %collective-permute-start.19 = (bf16[14,256,256]{2,1,0:T(8,128)(2,1)S(1)}, bf16[14,256,256]{2,1,0:T(8,128)(2,1)S(1)}, u32[]{:S(2)}, u32[]{:S(2)}) collective-permute-start(bf16[14,256,256]{2,1,0:T(8,128)(2,1)S(1)} %get-tuple-element.139), channel_id=1, source_target_pairs={{0,4},{4,0},{1,5},{5,1},{2,6},{6,2},{3,7},{7,3}} | collective-permute-start | bytes 5505032 | tf_op jit(solution)/shard_map/ppermute | solution.py:745
  94.9 1.3 %collective-permute-start.20 = (bf16[4,256,256]{2,1,0:T(8,128)(2,1)S(1)}, bf16[4,256,256]{2,1,0:T(8,128)(2,1)S(1)}, u32[]{:S(2)}, u32[]{:S(2)}) collective-permute-start(bf16[4,256,256]{2,1,0:T(8,128)(2,1)S(1)} %get-tuple-element.140), channel_id=1, source_target_pairs={{16,24},{20,28},{8,0},{12,4},{17,25},{21,29},{9,1},{13,5},{18,26},... | collective-permute-start | bytes 1572872 | tf_op jit(solution)/shard_map/ppermute | solution.py:628
  96.3 2.4 %collective-permute-done.21.refs_11_ = bf16[4,256,256]{2,1,0:T(8,128)(2,1)S(1)} collective-permute-done((bf16[4,256,256]{2,1,0:T(8,128)(2,1)S(1)}, bf16[4,256,256]{2,1,0:T(8,128)(2,1)S(1)}, u32[]{:S(2)}, u32[]{:S(2)}) %collective-permute-start.21) | collective-permute-done | bytes 524320 | tf_op jit(solution)/shard_map/ppermute | solution.py:607
  98.7 0.7 collective-permute-done.22.refs_15_
  99.5 15.5 %update_columns.2 = (bf16[7,14,256,256]{3,2,1,0:T(8,128)(2,1)}, f32[8,128]{1,0:T(8,128)S(1)}) custom-call(s32[3]{0:T(128)S(1)} %pad_add_fusion.place.refs_0_, s32[2,256,1]{2,1,0:T(8,128)S(1)} %get-tuple-element.80.refs_2_.refs_1_, bf16[7,14,256,256]{3,2,1,0:T(8,128)(2,1)} %bitcast.9, bf16[14,256,256]{2,1,0:T(8,128)(2,1)S(1)} %collective-permute-done.19.refs_3_, ...), custom_call_target="tpu_custom_call" | custom-call | flops 1024 | bytes 1024 | tf_op jit(solution)/shard_map/update_columns/pallas_call | solution.py:205
  114.9 1.2 finish.7
  116.4 1.8 %collective-permute-done.23.refs_7_ = bf16[4,256,256]{2,1,0:T(8,128)(2,1)S(1)} collective-permute-done((bf16[4,256,256]{2,1,0:T(8,128)(2,1)S(1)}, bf16[4,256,256]{2,1,0:T(8,128)(2,1)S(1)}, u32[]{:S(2)}, u32[]{:S(2)}) %collective-permute-start.23) | collective-permute-done | bytes 524320 | tf_op jit(solution)/shard_map/ppermute | solution.py:607
  118.2 7.6 %update_columns.3 = (bf16[7,14,256,256]{3,2,1,0:T(8,128)(2,1)}, f32[8,128]{1,0:T(8,128)}) custom-call(s32[3]{0:T(128)S(1)} %pad_add_fusion.place.refs_0_, s32[2,256,1]{2,1,0:T(8,128)S(1)} %get-tuple-element.80.refs_2_.refs_1_, bf16[7,14,256,256]{3,2,1,0:T(8,128)(2,1)} %bitcast.10, ...), custom_call_target="tpu_custom_call", output_to_operand_aliasing={{0}: (12, {})} | custom-call | flops 1024 | bytes 1024 | tf_op jit(solution)/shard_map/update_columns/pallas_call | solution.py:205
  (47 shorter events, 15.1 us)
Async XLA Ops:
  0.1 0.7 copy-start
  5.0 7.0 %collective-permute-start = (bf16[2,256,256]{2,1,0:T(8,128)(2,1)S(1)}, bf16[2,256,256]{2,1,0:T(8,128)(2,1)S(1)}, u32[]{:S(2)}, u32[]{:S(2)}) collective-permute-start(bf16[2,256,256]{2,1,0:T(8,128)(2,1)S(1)} %get-tuple-element.84.refs_5_), channel_id=1, source_target_pairs={{0,4},{4,0},{8,12},{12,8},{16,20},{20,16},{24,28},{28,24},{1,5},{5... | collective-permute-start | bytes 786440 | tf_op jit(solution)/shard_map/ppermute | solution.py:607
  12.6 12.3 %collective-permute-start.1 = (bf16[8,256,256]{2,1,0:T(8,128)(2,1)S(1)}, bf16[8,256,256]{2,1,0:T(8,128)(2,1)S(1)}, u32[]{:S(2)}, u32[]{:S(2)}) collective-permute-start(bf16[8,256,256]{2,1,0:T(8,128)(2,1)S(1)} %get-tuple-element.91), channel_id=1, source_target_pairs={{0,4},{4,0},{8,12},{12,8},{16,20},{20,16},{24,28},{28,24},{1,5},{5... | collective-permute-start | bytes 3145736 | tf_op jit(solution)/shard_map/ppermute | solution.py:607
  12.7 24.7 %collective-permute-start.5 = (bf16[7,256,256]{2,1,0:T(8,128)(2,1)S(1)}, bf16[7,256,256]{2,1,0:T(8,128)(2,1)S(1)}, u32[]{:S(2)}, u32[]{:S(2)}) collective-permute-start(bf16[7,256,256]{2,1,0:T(8,128)(2,1)S(1)} %get-tuple-element.99.refs_1_.refs_8_), channel_id=1, source_target_pairs={{0,2},{1,3},{4,6},{5,7},{8,10},{9,11},{12,14},{13,15},{16,18},{17,... | collective-permute-start | bytes 2752520 | tf_op jit(solution)/shard_map/ppermute | solution.py:647
  17.6 9.4 %collective-permute-start.3 = (bf16[2,256,256]{2,1,0:T(8,128)(2,1)S(1)}, bf16[2,256,256]{2,1,0:T(8,128)(2,1)S(1)}, u32[]{:S(2)}, u32[]{:S(2)}) collective-permute-start(bf16[2,256,256]{2,1,0:T(8,128)(2,1)S(1)} %get-tuple-element.95.refs_2_.refs_3_.refs_4_), channel_id=1, source_target_pairs={{0,8},{4,12},{24,16},{28,20},{1,9},{5,13},{25,17},{29,21},{2,10},{... | collective-permute-start | bytes 786440 | tf_op jit(solution)/shard_map/ppermute | solution.py:628
  25.6 19.0 %collective-permute-start.2 = (bf16[4,256,256]{2,1,0:T(8,128)(2,1)S(1)}, bf16[4,256,256]{2,1,0:T(8,128)(2,1)S(1)}, u32[]{:S(2)}, u32[]{:S(2)}) collective-permute-start(bf16[4,256,256]{2,1,0:T(8,128)(2,1)S(1)} %get-tuple-element.94.refs_5_), channel_id=1, source_target_pairs={{0,4},{4,0},{8,12},{12,8},{16,20},{20,16},{24,28},{28,24},{1,5},{5... | collective-permute-start | bytes 1572872 | tf_op jit(solution)/shard_map/ppermute | solution.py:607
  25.7 19.5 %collective-permute-start.6 = (bf16[4,256,256]{2,1,0:T(8,128)(2,1)S(1)}, bf16[4,256,256]{2,1,0:T(8,128)(2,1)S(1)}, u32[]{:S(2)}, u32[]{:S(2)}) collective-permute-start(bf16[4,256,256]{2,1,0:T(8,128)(2,1)S(1)} %get-tuple-element.106.refs_2_.refs_3_.refs_8_), channel_id=1, source_target_pairs={{0,8},{4,12},{24,16},{28,20},{1,9},{5,13},{25,17},{29,21},{2,10},{... | collective-permute-start | bytes 1572872 | tf_op jit(solution)/shard_map/ppermute | solution.py:628
  27.7 10.3 %collective-permute-start.4 = (bf16[2,256,256]{2,1,0:T(8,128)(2,1)S(1)}, bf16[2,256,256]{2,1,0:T(8,128)(2,1)S(1)}, u32[]{:S(2)}, u32[]{:S(2)}) collective-permute-start(bf16[2,256,256]{2,1,0:T(8,128)(2,1)S(1)} %get-tuple-element.98), channel_id=1, source_target_pairs={{8,16},{12,20},{16,8},{20,12},{9,17},{13,21},{17,9},{21,13},{10,18... | collective-permute-start | bytes 786440 | tf_op jit(solution)/shard_map/ppermute | solution.py:628
  38.7 9.5 %collective-permute-start.9 = (bf16[2,256,256]{2,1,0:T(8,128)(2,1)S(1)}, bf16[2,256,256]{2,1,0:T(8,128)(2,1)S(1)}, u32[]{:S(2)}, u32[]{:S(2)}) collective-permute-start(bf16[2,256,256]{2,1,0:T(8,128)(2,1)S(1)} %get-tuple-element.110), channel_id=1, source_target_pairs={{16,24},{20,28},{8,0},{12,4},{17,25},{21,29},{9,1},{13,5},{18,26},... | collective-permute-start | bytes 786440 | tf_op jit(solution)/shard_map/ppermute | solution.py:628
  40.0 15.6 %collective-permute-start.8 = (bf16[4,256,256]{2,1,0:T(8,128)(2,1)S(1)}, bf16[4,256,256]{2,1,0:T(8,128)(2,1)S(1)}, u32[]{:S(2)}, u32[]{:S(2)}) collective-permute-start(bf16[4,256,256]{2,1,0:T(8,128)(2,1)S(1)} %get-tuple-element.109.refs_2_.refs_3_.refs_12_), channel_id=1, source_target_pairs={{0,8},{4,12},{24,16},{28,20},{1,9},{5,13},{25,17},{29,21},{2,10},{... | collective-permute-start | bytes 1572872 | tf_op jit(solution)/shard_map/ppermute | solution.py:628
  45.9 11.1 %collective-permute-start.7 = (bf16[4,256,256]{2,1,0:T(8,128)(2,1)S(1)}, bf16[4,256,256]{2,1,0:T(8,128)(2,1)S(1)}, u32[]{:S(2)}, u32[]{:S(2)}) collective-permute-start(bf16[4,256,256]{2,1,0:T(8,128)(2,1)S(1)} %get-tuple-element.108), channel_id=1, source_target_pairs={{8,16},{12,20},{16,8},{20,12},{9,17},{13,21},{17,9},{21,13},{10,18... | collective-permute-start | bytes 1572872 | tf_op jit(solution)/shard_map/ppermute | solution.py:628
  46.6 23.4 %collective-permute-start.15 = (bf16[7,256,256]{2,1,0:T(8,128)(2,1)S(1)}, bf16[7,256,256]{2,1,0:T(8,128)(2,1)S(1)}, u32[]{:S(2)}, u32[]{:S(2)}) collective-permute-start(bf16[7,256,256]{2,1,0:T(8,128)(2,1)S(1)} %get-tuple-element.122), channel_id=1, source_target_pairs={{0,1},{1,0},{2,3},{3,2},{4,5},{5,4},{6,7},{7,6},{8,9},{9,8},{10,11... | collective-permute-start | bytes 2752520 | tf_op jit(solution)/shard_map/ppermute | solution.py:644
  49.0 1.6 %collective-permute-start.10 = (bf16[2,256,256]{2,1,0:T(8,128)(2,1)S(1)}, bf16[2,256,256]{2,1,0:T(8,128)(2,1)S(1)}, u32[]{:S(2)}, u32[]{:S(2)}) collective-permute-start(bf16[2,256,256]{2,1,0:T(8,128)(2,1)S(1)} %get-tuple-element.113), channel_id=1, source_target_pairs={{0,4},{4,0},{8,12},{12,8},{16,20},{20,16},{24,28},{28,24},{1,5},{5... | collective-permute-start | bytes 786440 | tf_op jit(solution)/shard_map/ppermute | solution.py:607
  51.2 12.1 %collective-permute-start.13 = (bf16[2,256,256]{2,1,0:T(8,128)(2,1)S(1)}, bf16[2,256,256]{2,1,0:T(8,128)(2,1)S(1)}, u32[]{:S(2)}, u32[]{:S(2)}) collective-permute-start(bf16[2,256,256]{2,1,0:T(8,128)(2,1)S(1)} %get-tuple-element.119.refs_1_), channel_id=1, source_target_pairs={{0,2},{1,3},{4,6},{5,7},{8,10},{9,11},{12,14},{13,15},{16,18},{17,... | collective-permute-start | bytes 786440 | tf_op jit(solution)/shard_map/ppermute | solution.py:647
  56.3 17.5 %collective-permute-start.12 = (bf16[4,256,256]{2,1,0:T(8,128)(2,1)S(1)}, bf16[4,256,256]{2,1,0:T(8,128)(2,1)S(1)}, u32[]{:S(2)}, u32[]{:S(2)}) collective-permute-start(bf16[4,256,256]{2,1,0:T(8,128)(2,1)S(1)} %get-tuple-element.118), channel_id=1, source_target_pairs={{8,16},{12,20},{16,8},{20,12},{9,17},{13,21},{17,9},{21,13},{10,18... | collective-permute-start | bytes 1572872 | tf_op jit(solution)/shard_map/ppermute | solution.py:628
  57.7 18.0 %collective-permute-start.11 = (bf16[4,256,256]{2,1,0:T(8,128)(2,1)S(1)}, bf16[4,256,256]{2,1,0:T(8,128)(2,1)S(1)}, u32[]{:S(2)}, u32[]{:S(2)}) collective-permute-start(bf16[4,256,256]{2,1,0:T(8,128)(2,1)S(1)} %get-tuple-element.117), channel_id=1, source_target_pairs={{0,8},{4,12},{24,16},{28,20},{16,24},{20,28},{8,0},{12,4},{1,9},{5... | collective-permute-start | bytes 1572872 | tf_op jit(solution)/shard_map/ppermute | solution.py:670
  63.9 9.2 %collective-permute-start.14 = (bf16[2,256,256]{2,1,0:T(8,128)(2,1)S(1)}, bf16[2,256,256]{2,1,0:T(8,128)(2,1)S(1)}, u32[]{:S(2)}, u32[]{:S(2)}) collective-permute-start(bf16[2,256,256]{2,1,0:T(8,128)(2,1)S(1)} %get-tuple-element.121), channel_id=1, source_target_pairs={{0,1},{1,0},{2,3},{3,2},{4,5},{5,4},{6,7},{7,6},{8,9},{9,8},{10,11... | collective-permute-start | bytes 786440 | tf_op jit(solution)/shard_map/ppermute | solution.py:644
  74.4 16.1 %collective-permute-start.17 = (bf16[4,256,256]{2,1,0:T(8,128)(2,1)S(1)}, bf16[4,256,256]{2,1,0:T(8,128)(2,1)S(1)}, u32[]{:S(2)}, u32[]{:S(2)}) collective-permute-start(bf16[4,256,256]{2,1,0:T(8,128)(2,1)S(1)} %get-tuple-element.128), channel_id=1, source_target_pairs={{16,24},{20,28},{8,0},{12,4},{17,25},{21,29},{9,1},{13,5},{18,26},... | collective-permute-start | bytes 1572872 | tf_op jit(solution)/shard_map/ppermute | solution.py:628
  76.4 15.2 %collective-permute-start.16 = (bf16[4,256,256]{2,1,0:T(8,128)(2,1)S(1)}, bf16[4,256,256]{2,1,0:T(8,128)(2,1)S(1)}, u32[]{:S(2)}, u32[]{:S(2)}) collective-permute-start(bf16[4,256,256]{2,1,0:T(8,128)(2,1)S(1)} %get-tuple-element.127), channel_id=1, source_target_pairs={{8,16},{12,20},{16,8},{20,12},{9,17},{13,21},{17,9},{21,13},{10,18... | collective-permute-start | bytes 1572872 | tf_op jit(solution)/shard_map/ppermute | solution.py:628
  77.1 3.4 %collective-permute-start.18 = (bf16[2,256,256]{2,1,0:T(8,128)(2,1)S(1)}, bf16[2,256,256]{2,1,0:T(8,128)(2,1)S(1)}, u32[]{:S(2)}, u32[]{:S(2)}) collective-permute-start(bf16[2,256,256]{2,1,0:T(8,128)(2,1)S(1)} %get-tuple-element.131), channel_id=1, source_target_pairs={{0,4},{4,0},{1,5},{5,1},{2,6},{6,2},{3,7},{7,3}} | collective-permute-start | bytes 786440 | tf_op jit(solution)/shard_map/ppermute | solution.py:720
  92.3 7.2 %collective-permute-start.19 = (bf16[14,256,256]{2,1,0:T(8,128)(2,1)S(1)}, bf16[14,256,256]{2,1,0:T(8,128)(2,1)S(1)}, u32[]{:S(2)}, u32[]{:S(2)}) collective-permute-start(bf16[14,256,256]{2,1,0:T(8,128)(2,1)S(1)} %get-tuple-element.139), channel_id=1, source_target_pairs={{0,4},{4,0},{1,5},{5,1},{2,6},{6,2},{3,7},{7,3}} | collective-permute-start | bytes 5505032 | tf_op jit(solution)/shard_map/ppermute | solution.py:745
  94.3 4.4 %collective-permute-start.21 = (bf16[4,256,256]{2,1,0:T(8,128)(2,1)S(1)}, bf16[4,256,256]{2,1,0:T(8,128)(2,1)S(1)}, u32[]{:S(2)}, u32[]{:S(2)}) collective-permute-start(bf16[4,256,256]{2,1,0:T(8,128)(2,1)S(1)} %get-tuple-element.142), channel_id=1, source_target_pairs={{0,4},{4,0},{8,12},{12,8},{16,20},{20,16},{24,28},{28,24},{1,5},{5... | collective-permute-start | bytes 1572872 | tf_op jit(solution)/shard_map/ppermute | solution.py:607
  94.8 4.7 %collective-permute-start.22 = (bf16[4,256,256]{2,1,0:T(8,128)(2,1)S(1)}, bf16[4,256,256]{2,1,0:T(8,128)(2,1)S(1)}, u32[]{:S(2)}, u32[]{:S(2)}) collective-permute-start(bf16[4,256,256]{2,1,0:T(8,128)(2,1)S(1)} %get-tuple-element.144), channel_id=1, source_target_pairs={{0,4},{4,0},{8,12},{12,8},{16,20},{20,16},{24,28},{28,24},{1,5},{5... | collective-permute-start | bytes 1572872 | tf_op jit(solution)/shard_map/ppermute | solution.py:607
  94.9 20.0 %collective-permute-start.20 = (bf16[4,256,256]{2,1,0:T(8,128)(2,1)S(1)}, bf16[4,256,256]{2,1,0:T(8,128)(2,1)S(1)}, u32[]{:S(2)}, u32[]{:S(2)}) collective-permute-start(bf16[4,256,256]{2,1,0:T(8,128)(2,1)S(1)} %get-tuple-element.140), channel_id=1, source_target_pairs={{16,24},{20,28},{8,0},{12,4},{17,25},{21,29},{9,1},{13,5},{18,26},... | collective-permute-start | bytes 1572872 | tf_op jit(solution)/shard_map/ppermute | solution.py:628
  116.2 2.0 %collective-permute-start.23 = (bf16[4,256,256]{2,1,0:T(8,128)(2,1)S(1)}, bf16[4,256,256]{2,1,0:T(8,128)(2,1)S(1)}, u32[]{:S(2)}, u32[]{:S(2)}) collective-permute-start(bf16[4,256,256]{2,1,0:T(8,128)(2,1)S(1)} %get-tuple-element.151), channel_id=1, source_target_pairs={{0,4},{4,0},{8,12},{12,8},{16,20},{20,16},{24,28},{28,24},{1,5},{5... | collective-permute-start | bytes 1572872 | tf_op jit(solution)/shard_map/ppermute | solution.py:607

commit v4 on v3

--- a/solution.py
+++ b/solution.py
@@ -228,6 +228,29 @@
         )
 
 
+    def together(self, place, parts):
+        def kernel(place_ref, *refs):
+            at, made = 0, sum(len(part[1]) for part in parts)
+            for part, operands, shapes in parts:
+                part(place_ref, *refs[at : at + len(operands)], *refs[made : made + len(shapes)])
+                at += len(operands)
+                made += len(shapes)
+
+        name = "_".join(getattr(part[0], "func", part[0]).__name__[:-7] for part in parts)
+        outs = self.whole(
+            kernel,
+            name,
+            place,
+            [operand for part in parts for operand in part[1]],
+            [shape for part in parts for shape in part[2]],
+        )
+        split, at = [], 0
+        for part in parts:
+            split.append(outs[at : at + len(part[2])])
+            at += len(part[2])
+        return split
+
+
 def gather_rows(chain, matrix, onehot, first, count, width):
     cycles, _, size, _ = matrix.shape
     part = array(count, size, size)
@@ -379,46 +402,69 @@
     )
 
 
-def panel_kernel(place, me_ref, xm_ref, xo_ref, top_ref, onehot_ref, put_ref, keep_ref, *rest):
-    *pieces, side_ref, lower1_ref, corner_ref, raw0, raw1, sems = rest
-    cycles, size, _ = raw0.shape
-    row = 2 * place[0] + place[1]
-    slots = STEPS * size
-
-    def fetch(pairs):
-        copies = []
-        for target, sources in zip((raw0, raw1), pairs):
-            at = 0
-            for source in sources:
-                count = source.shape[0]
-                copies.append(
-                    pltpu.make_async_copy(source, target.at[at : at + count], sems.at[len(copies)])
-                )
-                at += count
+def panel_rows_kernel(place, onehot_ref, *rest):
+    *pieces, raw_ref, own_ref, first_ref, sems = rest
+    _, cycles, size, _ = raw_ref.shape
+
+    def fetch(first, second):
+        copies = [
+            pltpu.make_async_copy(source, raw_ref.at[b], sems.at[b])
+            for b, source in enumerate((first, second))
+        ]
         for copy in copies:
             copy.start()
         for copy in copies:
             copy.wait()
 
     if len(pieces) == 2:
-        fetch(((pieces[0],), (pieces[1],)))
+        fetch(*pieces)
     else:
-        own, down, over = ((piece,) for piece in pieces)
-        for col, pairs in enumerate(((own, over), (over, own), (down, over), (over, down))):
+        own, down, over = pieces
+        for col, pair in enumerate(((own, over), (over, own), (down, over), (over, down))):
 
             @pl.when(place[2] == col)
-            def _(pairs=pairs):
-                fetch(pairs)
-
-    flat = [raw.reshape(cycles * size, size)[...] for raw in (raw0, raw1)]
-    own = dot(onehot_ref[...], jnp.concatenate(flat, 1)).astype(BF16)
+            def _(pair=pair):
+                fetch(*pair)
+
+    flat = [raw_ref[b].reshape(cycles * size, size) for b in range(2)]
+    total = dot(onehot_ref[...], jnp.concatenate(flat, 1)).astype(BF16)
+    for b in range(2):
+        own_ref[b] = total[:, b * size : (b + 1) * size]
+        first_ref[b] = raw_ref[b, 0]
+
+
+def panel_rows(chain, place, onehot, pieces):
+    cycles, size, _ = pieces[0].shape
+    return chain.run(
+        panel_rows_kernel,
+        "panel_rows",
+        (place, onehot, *pieces),
+        [SMEM, VMEM] + [ANY] * len(pieces),
+        [
+            array(2, cycles, size, size),
+            array(2, STEPS * size, size),
+            array(2, size, size),
+        ],
+        [VMEM] * 3,
+        scratch_shapes=[pltpu.SemaphoreType.DMA((2,))],
+    )
+
+
+def panel_kernel(
+    place, me_ref, xm_ref, xo_ref, top_ref, raw_ref, own_ref, put_ref, keep_ref,
+    side_ref, lower1_ref, corner_ref,
+):
+    _, cycles, size, _ = raw_ref.shape
+    row = 2 * place[0] + place[1]
+    slots = STEPS * size
+    raw0, raw1 = raw_ref.at[0], raw_ref.at[1]
     new0, new1, old = [], [], []
-    for b, raw in enumerate((raw0, raw1)):
-        mine, other = own[:size, b * size : (b + 1) * size], own[size:, b * size : (b + 1) * size]
+    for b in range(2):
+        mine, other = own_ref[b, :size], own_ref[b, size:]
         upper, below = whole_rows(place, me_ref, mine, other, xm_ref[b], xo_ref[b])
         new0.append(upper)
         new1.append(below)
-        old.append(old_rows(place, xm_ref[b], xo_ref[b], raw[0], top_ref[b]))
+        old.append(old_rows(place, xm_ref[b], xo_ref[b], raw_ref[b, 0], top_ref[b]))
     old = jnp.concatenate(old, 1)
     identity = jnp.where(iota((size, size), 0) == iota((size, size), 1), 1.0, 0.0).astype(F32)
     inverse0 = three_parts(newton_inverse(new0[0], identity))
@@ -451,24 +497,19 @@
         lower1_ref[cycle] = lower.astype(BF16)
 
 
-def factor_panels(chain, place, me, rows, tops, onehot, put, keep, pieces):
+def factor_panels(chain, place, me, rows, tops, raw, own, put, keep):
     cycles, size, _ = keep.shape
     return chain.run(
         panel_kernel,
         "factor_panels",
-        (place, me, *rows, tops, onehot, put, keep, *pieces),
-        [SMEM] + [VMEM] * 7 + [ANY] * len(pieces),
+        (place, me, *rows, tops, raw, own, put, keep),
+        [SMEM] + [VMEM] * 8,
         [
             array(cycles, size, (STEPS + 1) * size),
             array(cycles, size, size),
             array(size, size),
         ],
         [VMEM] * 3,
-        scratch_shapes=[
-            pltpu.VMEM((cycles, size, size), BF16),
-            pltpu.VMEM((cycles, size, size), BF16),
-            pltpu.SemaphoreType.DMA((4,)),
-        ],
     )
 
 
@@ -614,30 +655,59 @@
             meet_kernel, "meet", place, (mine, theirs), [array(c, size, size) for c in counts]
         )
 
-    def hop(i):
+    def hop_part(i):
         h = len(hops[i])
-        out = native[i]
-        if h:
-            (out,) = chain.whole(
-                merge_kernel,
-                "merge",
-                place,
-                (owner, native[i], hops[i][-1]),
-                [array(*native[i].shape)],
-            )
-        hops[i].append(lax.ppermute(out, "row", hop_pairs(h)))
-
-    def finish(i):
+        shape = array(*native[i].shape)
+
+        def go(out):
+            hops[i].append(lax.ppermute(out[0], "row", hop_pairs(h)))
+
+        return merge_kernel, (owner, native[i], hops[i][-1]), [shape], go
+
+    def both_part(i, j):
+        if chips != 4 or native[i].shape != native[j].shape:
+            hop(j)
+            return hop_part(i)
+
+        def go(out):
+            arrived = lax.ppermute(out[0], "row", hop_pairs(0) + hop_pairs(2))
+            hops[i].append(arrived)
+            hops[j].append(arrived)
+
+        kernel = functools.partial(merge_or_send_kernel, chips=chips)
+        operands = (owner, native[i], hops[i][-1], native[j])
+        return kernel, operands, [array(*native[i].shape)], go
+
+    def finish_part(i):
         while len(hops[i]) < chips - 1:
             hop(i)
-        x_mine[i], x_send[i] = chain.whole(
-            finish_kernel,
-            "finish",
-            place,
-            (owner, me, native[i], *hops[i]),
-            [array(*native[i].shape)] * 2,
-        )
-        x_other[i] = exchange(x_send[i])
+
+        def go(out):
+            x_mine[i], x_send[i] = out
+            x_other[i] = exchange(x_send[i])
+
+        operands = (owner, me, native[i], *hops[i])
+        return finish_kernel, operands, [array(*native[i].shape)] * 2, go
+
+    def meet_part(i, mine, theirs):
+        def go(out):
+            (native[i],) = out
+
+        return meet_kernel, (mine, theirs), [array(*mine.shape)], go
+
+    def group(*parts):
+        outs = chain.together(place, [part[:3] for part in parts])
+        for part, out in zip(parts, outs):
+            part[3](out)
+
+    def hop(i):
+        if hops[i]:
+            group(hop_part(i))
+        else:
+            hops[i].append(lax.ppermute(native[i], "row", hop_pairs(0)))
+
+    def finish(i):
+        group(finish_part(i))
 
     def side(own, down):
         (out,) = chain.whole(side_kernel, "side", place, (own, down), [array(*own.shape)])
@@ -654,22 +724,6 @@
     def from_two(own):
         zero = jnp.zeros_like(own)
         return lax.psum(jnp.stack([jnp.where(col == b, own, zero) for b in range(2)]), "col")
-
-    def hop_both(i, j):
-        if chips != 4 or native[i].shape != native[j].shape:
-            hop(i)
-            hop(j)
-            return
-        (out,) = chain.whole(
-            functools.partial(merge_or_send_kernel, chips=chips),
-            "merge",
-            place,
-            (owner, native[i], hops[i][-1], native[j]),
-            [array(*native[i].shape)],
-        )
-        arrived = lax.ppermute(out, "row", hop_pairs(0) + hop_pairs(2))
-        hops[i].append(arrived)
-        hops[j].append(arrived)
 
     native[0], others[0] = mine, other
     theirs0 = exchange(other)
@@ -697,9 +751,10 @@
     put, keep = placement(chain, place, lands, cycles)
     if few_cols:
         side_raw = side(raw, down_raw)
-    hop(0)
-    (native[3],) = meet(mine3, theirs3, sizes[3])
-    hop(1)
+    chain.hold(top)
+    group(hop_part(0), hop_part(1), meet_part(3, mine3, theirs3))
+    (top,) = chain.passed
+    top = lax.ppermute(top, "row", first_swap)
     finish(0)
     (lead,) = chain.whole(
         lead_kernel, "lead", place, (x_mine[0], x_other[0]), [array(2, size, size)]
@@ -708,27 +763,23 @@
         down_lead = down(lead)
     else:
         leads = from_two(lead)
-    hop(2)
-    hop_both(1, 3)
+    group(hop_part(2), both_part(1, 3))
+    if few_cols:
+        pieces = [raw, down_raw, side_raw]
+    else:
+        raws = from_two(raw)
+        pieces = [raws[0], raws[1]]
+    panels, panel_own, firsts = panel_rows(chain, place, onehot, pieces)
+    tops = lax.ppermute(firsts, "row", first_swap)
     if few_cols:
         side_lead = side(lead, down_lead)
     if few_cols:
-        (firsts,) = pair(raw, down_raw, side_raw, 1)
-    else:
-        raws = from_two(raw)
-        firsts = raws[:, 0]
-    tops = lax.ppermute(firsts, "row", first_swap)
-    if few_cols:
         panel_mine, panel_other = pair(lead, down_lead, side_lead, 2)
-        pieces = [raw, down_raw, side_raw]
     else:
         panel_mine, panel_other = leads[:, 0], leads[:, 1]
-        pieces = [raws[0], raws[1]]
-    hop(2)
-    hop(3)
-    finish(1)
+    group(hop_part(2), hop_part(3), finish_part(1))
     side_rows, lower1, corner = factor_panels(
-        chain, place, me, (panel_mine, panel_other), tops, onehot, put, keep, pieces
+        chain, place, me, (panel_mine, panel_other), tops, panels, panel_own, put, keep
     )
     factors = (side_rows, keep, lower1, corner)
 
@@ -738,11 +789,7 @@
             chain, place, me, matrix, sets, top, factors, chunks[which[0]][0], width, result
         )
 
-    finish(2)
-    chain.hold(top)
-    hop(3)
-    (top,) = chain.passed
-    top = lax.ppermute(top, "row", first_swap)
+    group(hop_part(3), finish_part(2))
     result = update((0, 1, 2), None)
     finish(3)
     result = update((3,), result)

time: 126 us -> 121 us (0.960)
  Pallas kernels: 62.9 us -> 59.3 us
  starting transfers between devices: 39.6 us -> 36.9 us
    ppermute x11, waiting for transfers between devices: 0.03 us -> 7.05 us  [the longest x7 7.04 us: go(): hops[i].append(lax.ppermute(out[0], 'row', hop_pairs(h)))]
    ppermute x7, waiting for transfers between devices: 6.49 us -> 2.29 us  [exchange(): return lax.ppermute(own, 'row', swap)]
    pallas_call x26 -> x20, Pallas kernels: 58.7 us -> 55.1 us  [run(): pl.pallas_call(inner, in_specs=in_specs + [ANY] * (len(waits) + passed),...]
    ppermute x11, starting transfers between devices: 21.7 us -> 19.3 us  [the longest x3 9.41 us: hop(): hops[i].append(lax.ppermute(native[i], 'row', hop_pairs(0)))]
    ppermute x2, waiting for transfers between devices: 7.11 us -> 5.21 us  [side(): return lax.ppermute(out, 'col', side_pairs)]
  transfers between devices with their start and end apart: 24 -> 24, of which waited for: 8 -> 7; matrix products, arithmetic and copies ran while one was open for 0% -> 0% of each run, Pallas kernels for 39% -> 38%
where the time goes in v4:
time: 121 us
  Pallas kernels  59.3 us (49%)
  starting transfers between devices  36.9 us (30%)
  waiting for transfers between devices  23.2 us (19%)
    pallas_call x20, Pallas kernels, run(): pl.pallas_call(inner, in_specs=in_specs + [ANY] * (len(waits) + passed),...  55.1 us
    ppermute x3, starting transfers between devices, hop(): hops[i].append(lax.ppermute(native[i], 'row', hop_pairs(0)))  9.41 us
    ppermute x2, starting transfers between devices, down(): return lax.ppermute(own, 'col', down_pairs)  8.68 us
    ppermute x2, waiting for transfers between devices, down(): return lax.ppermute(own, 'col', down_pairs)  7.89 us
    ppermute x7, waiting for transfers between devices, go(): hops[i].append(lax.ppermute(out[0], 'row', hop_pairs(h)))  7.04 us
    ppermute x7, starting transfers between devices, go(): hops[i].append(lax.ppermute(out[0], 'row', hop_pairs(h)))  6.62 us
    ppermute x2, waiting for transfers between devices, side(): return lax.ppermute(out, 'col', side_pairs)  5.21 us
    pallas_call x1, Pallas kernels, start(): pl.pallas_call(functools.partial(start_kernel, rows), grid=(1,), in_specs...  4.2 us
  transfers between devices with their start and end apart: 24, of which 7 were waited for; matrix products, arithmetic and copies ran while one was open for 0% of the time, Pallas kernels for 38%

profile of v4, /device:TPU:0, one launch (start us, length us, event | category | flops | bytes accessed | tf_op | source)
XLA Modules:
  0.0 120.6 jit_solution(16823953033862600826)
XLA Ops:
  0.8 4.2 %start.1 = (bf16[512,1792]{1,0:T(8,128)(2,1)S(1)}, s32[2,256,1]{2,1,0:T(8,128)S(1)}, s32[2,256,1]{2,1,0:T(8,128)S(1)}, s32[2,256]{1,0:T(2,128)S(1)}, bf16[7,256,...) custom-call(s32[3]{0:T(128)S(1)} %pad_add_fusion.place.refs_0_, ...), custom_call_target="tpu_custom_call" | custom-call | flops 1024 | bytes 1024 | tf_op jit(solution)/shard_map/start/pallas_call | solution.py:161
  5.5 6.5 %gather_rows.2 = (bf16[8,256,256]{2,1,0:T(8,128)(2,1)S(1)}, bf16[8,256,256]{2,1,0:T(8,128)(2,1)S(1)}, f32[8,128]{1,0:T(8,128)S(1)}) custom-call(bf16[512,1792]{1,0:T(8,128)(2,1)S(1)} %get-tuple-element.80.refs_0_.refs_1_, bf16[7,14,256,256]{3,2,1,0:T(8,128)(2,1)} %bitcast.7, f32[8,128]{1,0:T(8,128)S(1)} %get-tuple-element.81.refs_2_), custom_call_target="tpu_custom_call" | custom-call | flops 1024 | bytes 1024 | tf_op jit(solution)/shard_map/gather_rows/pallas_call | solution.py:205
  12.7 4.9 %collective-permute-start.6 = (bf16[7,256,256]{2,1,0:T(8,128)(2,1)S(1)}, bf16[7,256,256]{2,1,0:T(8,128)(2,1)S(1)}, u32[]{:S(2)}, u32[]{:S(2)}) collective-permute-start(bf16[7,256,256]{2,1,0:T(8,128)(2,1)S(1)} %get-tuple-element.96.refs_1_.refs_2_), channel_id=1, source_target_pairs={{0,2},{1,3},{4,6},{5,7},{8,10},{9,11},{12,14},{13,15},{16,18},{17,... | collective-permute-start | bytes 2752520 | tf_op jit(solution)/shard_map/ppermute | solution.py:717
  17.6 3.5 %collective-permute-start.1 = (bf16[2,256,256]{2,1,0:T(8,128)(2,1)S(1)}, bf16[2,256,256]{2,1,0:T(8,128)(2,1)S(1)}, u32[]{:S(2)}, u32[]{:S(2)}) collective-permute-start(bf16[2,256,256]{2,1,0:T(8,128)(2,1)S(1)} %get-tuple-element.84.refs_2_.refs_3_.refs_4_), channel_id=1, source_target_pairs={{0,8},{4,12},{24,16},{28,20},{1,9},{5,13},{25,17},{29,21},{2,10},{... | collective-permute-start | bytes 786440 | tf_op jit(solution)/shard_map/ppermute | solution.py:707
  21.1 3.8 %gather_rows.3 = (bf16[4,256,256]{2,1,0:T(8,128)(2,1)S(1)}, bf16[4,256,256]{2,1,0:T(8,128)(2,1)S(1)}, f32[8,128]{1,0:T(8,128)S(1)}) custom-call(bf16[512,1792]{1,0:T(8,128)(2,1)S(1)} %get-tuple-element.80.refs_0_.refs_1_, bf16[7,14,256,256]{3,2,1,0:T(8,128)(2,1)} %bitcast.8, f32[8,128]{1,0:T(8,128)S(1)} %get-tuple-element.87.refs_2_), custom_call_target="tpu_custom_call" | custom-call | flops 1024 | bytes 1024 | tf_op jit(solution)/shard_map/gather_rows/pallas_call | solution.py:205
  25.7 1.3 %collective-permute-start.4 = (bf16[4,256,256]{2,1,0:T(8,128)(2,1)S(1)}, bf16[4,256,256]{2,1,0:T(8,128)(2,1)S(1)}, u32[]{:S(2)}, u32[]{:S(2)}) collective-permute-start(bf16[4,256,256]{2,1,0:T(8,128)(2,1)S(1)} %get-tuple-element.93.refs_5_.refs_9_.refs_8_), channel_id=1, source_target_pairs={{0,8},{4,12},{24,16},{28,20},{1,9},{5,13},{25,17},{29,21},{2,10},{... | collective-permute-start | bytes 1572872 | tf_op jit(solution)/shard_map/ppermute | solution.py:707
  28.4 1.1 placement.1
  29.5 7.9 %collective-permute-done.6.refs_2_.refs_3_ = bf16[7,256,256]{2,1,0:T(8,128)(2,1)S(1)} collective-permute-done((bf16[7,256,256]{2,1,0:T(8,128)(2,1)S(1)}, bf16[7,256,256]{2,1,0:T(8,128)(2,1)S(1)}, u32[]{:S(2)}, u32[]{:S(2)}) %collective-permute-start.6) | collective-permute-done | bytes 917536 | tf_op jit(solution)/shard_map/ppermute | solution.py:717
  38.0 1.6 %collective-permute-start.15 = (bf16[7,256,256]{2,1,0:T(8,128)(2,1)S(1)}, bf16[7,256,256]{2,1,0:T(8,128)(2,1)S(1)}, u32[]{:S(2)}, u32[]{:S(2)}) collective-permute-start(bf16[7,256,256]{2,1,0:T(8,128)(2,1)S(1)} %get-tuple-element.115), channel_id=1, source_target_pairs={{0,1},{1,0},{2,3},{3,2},{4,5},{5,4},{6,7},{7,6},{8,9},{9,8},{10,11... | collective-permute-start | bytes 2752520 | tf_op jit(solution)/shard_map/ppermute | solution.py:714
  39.6 0.8 merge_merge_meet.1
  40.4 1.3 %collective-permute-start.10 = (bf16[2,256,256]{2,1,0:T(8,128)(2,1)S(1)}, bf16[2,256,256]{2,1,0:T(8,128)(2,1)S(1)}, u32[]{:S(2)}, u32[]{:S(2)}) collective-permute-start(bf16[2,256,256]{2,1,0:T(8,128)(2,1)S(1)} %get-tuple-element.106), channel_id=1, source_target_pairs={{16,24},{20,28},{8,0},{12,4},{17,25},{21,29},{9,1},{13,5},{18,26},... | collective-permute-start | bytes 786440 | tf_op jit(solution)/shard_map/ppermute | solution.py:663
  41.7 4.6 %collective-permute-start.8 = (bf16[4,256,256]{2,1,0:T(8,128)(2,1)S(1)}, bf16[4,256,256]{2,1,0:T(8,128)(2,1)S(1)}, u32[]{:S(2)}, u32[]{:S(2)}) collective-permute-start(bf16[4,256,256]{2,1,0:T(8,128)(2,1)S(1)} %get-tuple-element.104.refs_2_.refs_6_.refs_12_), channel_id=1, source_target_pairs={{0,8},{4,12},{24,16},{28,20},{1,9},{5,13},{25,17},{29,21},{2,10},{... | collective-permute-start | bytes 1572872 | tf_op jit(solution)/shard_map/ppermute | solution.py:707
  47.0 3.0 %collective-permute-done.10.refs_6_ = bf16[2,256,256]{2,1,0:T(8,128)(2,1)S(1)} collective-permute-done((bf16[2,256,256]{2,1,0:T(8,128)(2,1)S(1)}, bf16[2,256,256]{2,1,0:T(8,128)(2,1)S(1)}, u32[]{:S(2)}, u32[]{:S(2)}) %collective-permute-start.10) | collective-permute-done | bytes 262176 | tf_op jit(solution)/shard_map/ppermute | solution.py:663
  50.0 0.9 finish.2
  50.9 2.4 %collective-permute-start.7 = (bf16[14,256,256]{2,1,0:T(8,128)(2,1)S(1)}, bf16[14,256,256]{2,1,0:T(8,128)(2,1)S(1)}, u32[]{:S(2)}, u32[]{:S(2)}) collective-permute-start(bf16[14,256,256]{2,1,0:T(8,128)(2,1)S(1)} %get-tuple-element.102), channel_id=1, source_target_pairs={{0,4},{4,0},{1,5},{5,1},{2,6},{6,2},{3,7},{7,3}} | collective-permute-start | bytes 5505032 | tf_op jit(solution)/shard_map/ppermute | solution.py:757
  53.9 3.8 %collective-permute-start.14 = (bf16[2,256,256]{2,1,0:T(8,128)(2,1)S(1)}, bf16[2,256,256]{2,1,0:T(8,128)(2,1)S(1)}, u32[]{:S(2)}, u32[]{:S(2)}) collective-permute-start(bf16[2,256,256]{2,1,0:T(8,128)(2,1)S(1)} %get-tuple-element.114.refs_1_), channel_id=1, source_target_pairs={{0,2},{1,3},{4,6},{5,7},{8,10},{9,11},{12,14},{13,15},{16,18},{17,... | collective-permute-start | bytes 786440 | tf_op jit(solution)/shard_map/ppermute | solution.py:717
  58.5 3.3 %collective-permute-start.12 = (bf16[4,256,256]{2,1,0:T(8,128)(2,1)S(1)}, bf16[4,256,256]{2,1,0:T(8,128)(2,1)S(1)}, u32[]{:S(2)}, u32[]{:S(2)}) collective-permute-start(bf16[4,256,256]{2,1,0:T(8,128)(2,1)S(1)} %get-tuple-element.112), channel_id=1, source_target_pairs={{0,8},{4,12},{24,16},{28,20},{16,24},{20,28},{8,0},{12,4},{1,9},{5... | collective-permute-start | bytes 1572872 | tf_op jit(solution)/shard_map/ppermute | solution.py:673
  62.4 2.2 %panel_rows.1 = (bf16[2,7,256,256]{3,2,1,0:T(8,128)(2,1)S(1)}, bf16[2,512,256]{2,1,0:T(8,128)(2,1)S(1)}, bf16[2,256,256]{2,1,0:T(8,128)(2,1)S(1)}, f32[8,128]{1,0:T(8,128)S(1)}) custom-call(s32[3]{0:T(128)S(1)} %pad_add_fusion.place.refs_0_, bf16[512,1792]{1,0:T(8,128)(2,1)S(1)} %get-tuple-element.80.refs_0_.refs_1_, ...), custom_call_target="tpu_custom_call" | custom-call | flops 1024 | bytes 1024 | tf_op jit(solution)/shard_map/panel_rows/pallas_call | solution.py:205
  65.2 1.2 %collective-permute-start.16 = (bf16[2,256,256]{2,1,0:T(8,128)(2,1)S(1)}, bf16[2,256,256]{2,1,0:T(8,128)(2,1)S(1)}, u32[]{:S(2)}, u32[]{:S(2)}) collective-permute-start(bf16[2,256,256]{2,1,0:T(8,128)(2,1)S(1)} %get-tuple-element.118), channel_id=1, source_target_pairs={{0,1},{1,0},{2,3},{3,2},{4,5},{5,4},{6,7},{7,6},{8,9},{9,8},{10,11... | collective-permute-start | bytes 786440 | tf_op jit(solution)/shard_map/ppermute | solution.py:714
  66.4 5.2 %collective-permute-done.16.refs_3_ = bf16[2,256,256]{2,1,0:T(8,128)(2,1)S(1)} collective-permute-done((bf16[2,256,256]{2,1,0:T(8,128)(2,1)S(1)}, bf16[2,256,256]{2,1,0:T(8,128)(2,1)S(1)}, u32[]{:S(2)}, u32[]{:S(2)}) %collective-permute-start.16) | collective-permute-done | bytes 262176 | tf_op jit(solution)/shard_map/ppermute | solution.py:714
  72.2 1.2 merge_merge_finish.1
  74.1 1.3 %collective-permute-start.18 = (bf16[4,256,256]{2,1,0:T(8,128)(2,1)S(1)}, bf16[4,256,256]{2,1,0:T(8,128)(2,1)S(1)}, u32[]{:S(2)}, u32[]{:S(2)}) collective-permute-start(bf16[4,256,256]{2,1,0:T(8,128)(2,1)S(1)} %get-tuple-element.122), channel_id=1, source_target_pairs={{16,24},{20,28},{8,0},{12,4},{17,25},{21,29},{9,1},{13,5},{18,26},... | collective-permute-start | bytes 1572872 | tf_op jit(solution)/shard_map/ppermute | solution.py:663
  75.4 2.1 %collective-permute-start.19 = (bf16[2,256,256]{2,1,0:T(8,128)(2,1)S(1)}, bf16[2,256,256]{2,1,0:T(8,128)(2,1)S(1)}, u32[]{:S(2)}, u32[]{:S(2)}) collective-permute-start(bf16[2,256,256]{2,1,0:T(8,128)(2,1)S(1)} %get-tuple-element.125), channel_id=1, source_target_pairs={{0,4},{4,0},{1,5},{5,1},{2,6},{6,2},{3,7},{7,3}} | collective-permute-start | bytes 786440 | tf_op jit(solution)/shard_map/ppermute | solution.py:773
  78.1 0.8 collective-permute-done.19.refs_4_
  78.9 8.4 %factor_panels.1 = (bf16[7,256,768]{2,1,0:T(8,128)(2,1)S(1)}, bf16[7,256,256]{2,1,0:T(8,128)(2,1)S(1)}, bf16[256,256]{1,0:T(8,128)(2,1)S(1)}, f32[8,128]{1,0:T(8,128)S(1)}) custom-call(s32[3]{0:T(128)S(1)} %pad_add_fusion.place.refs_0_, s32[2,256,1]{2,1,0:T(8,128)S(1)} %get-tuple-element.76.refs_2_.refs_8_.refs_1_.refs_5_, ...), custom_call_target="tpu_custom_call" | custom-call | flops 1024 | bytes 1024 | tf_op jit(solution)/shard_map/factor_panels/pallas_call | solution.py:205
  87.3 4.0 %collective-permute-done.18.refs_9_ = bf16[4,256,256]{2,1,0:T(8,128)(2,1)S(1)} collective-permute-done((bf16[4,256,256]{2,1,0:T(8,128)(2,1)S(1)}, bf16[4,256,256]{2,1,0:T(8,128)(2,1)S(1)}, u32[]{:S(2)}, u32[]{:S(2)}) %collective-permute-start.18) | collective-permute-done | bytes 524320 | tf_op jit(solution)/shard_map/ppermute | solution.py:663
  91.3 1.1 merge_finish.1
  92.5 1.3 %collective-permute-start.20 = (bf16[4,256,256]{2,1,0:T(8,128)(2,1)S(1)}, bf16[4,256,256]{2,1,0:T(8,128)(2,1)S(1)}, u32[]{:S(2)}, u32[]{:S(2)}) collective-permute-start(bf16[4,256,256]{2,1,0:T(8,128)(2,1)S(1)} %get-tuple-element.132), channel_id=1, source_target_pairs={{16,24},{20,28},{8,0},{12,4},{17,25},{21,29},{9,1},{13,5},{18,26},... | collective-permute-start | bytes 1572872 | tf_op jit(solution)/shard_map/ppermute | solution.py:663
  94.4 15.5 %update_columns.2 = (bf16[7,14,256,256]{3,2,1,0:T(8,128)(2,1)}, f32[8,128]{1,0:T(8,128)S(1)}) custom-call(s32[3]{0:T(128)S(1)} %pad_add_fusion.place.refs_0_, s32[2,256,1]{2,1,0:T(8,128)S(1)} %get-tuple-element.76.refs_2_.refs_8_.refs_1_.refs_5_, bf16[7,14,256,256]{3,2,1,0:T(8,128)(2,1)} %bitcast.9, ...), custom_call_target="tpu_custom_call" | custom-call | flops 1024 | bytes 1024 | tf_op jit(solution)/shard_map/update_columns/pallas_call | solution.py:205
  110.0 1.0 finish.3
  111.2 1.8 %collective-permute-done.23.refs_7_ = bf16[4,256,256]{2,1,0:T(8,128)(2,1)S(1)} collective-permute-done((bf16[4,256,256]{2,1,0:T(8,128)(2,1)S(1)}, bf16[4,256,256]{2,1,0:T(8,128)(2,1)S(1)}, u32[]{:S(2)}, u32[]{:S(2)}) %collective-permute-start.23) | collective-permute-done | bytes 524320 | tf_op jit(solution)/shard_map/ppermute | solution.py:648
  112.9 7.6 %update_columns.3 = (bf16[7,14,256,256]{3,2,1,0:T(8,128)(2,1)}, f32[8,128]{1,0:T(8,128)}) custom-call(s32[3]{0:T(128)S(1)} %pad_add_fusion.place.refs_0_, s32[2,256,1]{2,1,0:T(8,128)S(1)} %get-tuple-element.76.refs_2_.refs_8_.refs_1_.refs_5_, bf16[7,14,256,256]{3,2,1,0:T(8,128)(2,1)} %bitcast.10, ...), custom_call_target="tpu_custom_call", output_to_operand_aliasing={{0}: (12, {})} | custom-call | flops 1024 | bytes 1024 | tf_op jit(solution)/shard_map/update_columns/pallas_call | solution.py:205
  (41 shorter events, 10.8 us)
Async XLA Ops:
  0.1 0.7 copy-start
  5.0 7.0 %collective-permute-start = (bf16[2,256,256]{2,1,0:T(8,128)(2,1)S(1)}, bf16[2,256,256]{2,1,0:T(8,128)(2,1)S(1)}, u32[]{:S(2)}, u32[]{:S(2)}) collective-permute-start(bf16[2,256,256]{2,1,0:T(8,128)(2,1)S(1)} %get-tuple-element.79.refs_5_), channel_id=1, source_target_pairs={{0,4},{4,0},{8,12},{12,8},{16,20},{20,16},{24,28},{28,24},{1,5},{5... | collective-permute-start | bytes 786440 | tf_op jit(solution)/shard_map/ppermute | solution.py:648
  12.6 12.3 %collective-permute-start.2 = (bf16[8,256,256]{2,1,0:T(8,128)(2,1)S(1)}, bf16[8,256,256]{2,1,0:T(8,128)(2,1)S(1)}, u32[]{:S(2)}, u32[]{:S(2)}) collective-permute-start(bf16[8,256,256]{2,1,0:T(8,128)(2,1)S(1)} %get-tuple-element.86), channel_id=1, source_target_pairs={{0,4},{4,0},{8,12},{12,8},{16,20},{20,16},{24,28},{28,24},{1,5},{5... | collective-permute-start | bytes 3145736 | tf_op jit(solution)/shard_map/ppermute | solution.py:648
  12.7 24.7 %collective-permute-start.6 = (bf16[7,256,256]{2,1,0:T(8,128)(2,1)S(1)}, bf16[7,256,256]{2,1,0:T(8,128)(2,1)S(1)}, u32[]{:S(2)}, u32[]{:S(2)}) collective-permute-start(bf16[7,256,256]{2,1,0:T(8,128)(2,1)S(1)} %get-tuple-element.96.refs_1_.refs_2_), channel_id=1, source_target_pairs={{0,2},{1,3},{4,6},{5,7},{8,10},{9,11},{12,14},{13,15},{16,18},{17,... | collective-permute-start | bytes 2752520 | tf_op jit(solution)/shard_map/ppermute | solution.py:717
  17.6 9.4 %collective-permute-start.1 = (bf16[2,256,256]{2,1,0:T(8,128)(2,1)S(1)}, bf16[2,256,256]{2,1,0:T(8,128)(2,1)S(1)}, u32[]{:S(2)}, u32[]{:S(2)}) collective-permute-start(bf16[2,256,256]{2,1,0:T(8,128)(2,1)S(1)} %get-tuple-element.84.refs_2_.refs_3_.refs_4_), channel_id=1, source_target_pairs={{0,8},{4,12},{24,16},{28,20},{1,9},{5,13},{25,17},{29,21},{2,10},{... | collective-permute-start | bytes 786440 | tf_op jit(solution)/shard_map/ppermute | solution.py:707
  25.6 13.9 %collective-permute-start.5 = (bf16[4,256,256]{2,1,0:T(8,128)(2,1)S(1)}, bf16[4,256,256]{2,1,0:T(8,128)(2,1)S(1)}, u32[]{:S(2)}, u32[]{:S(2)}) collective-permute-start(bf16[4,256,256]{2,1,0:T(8,128)(2,1)S(1)} %get-tuple-element.95.refs_5_), channel_id=1, source_target_pairs={{0,4},{4,0},{8,12},{12,8},{16,20},{20,16},{24,28},{28,24},{1,5},{5... | collective-permute-start | bytes 1572872 | tf_op jit(solution)/shard_map/ppermute | solution.py:648
  25.7 13.9 %collective-permute-start.4 = (bf16[4,256,256]{2,1,0:T(8,128)(2,1)S(1)}, bf16[4,256,256]{2,1,0:T(8,128)(2,1)S(1)}, u32[]{:S(2)}, u32[]{:S(2)}) collective-permute-start(bf16[4,256,256]{2,1,0:T(8,128)(2,1)S(1)} %get-tuple-element.93.refs_5_.refs_9_.refs_8_), channel_id=1, source_target_pairs={{0,8},{4,12},{24,16},{28,20},{1,9},{5,13},{25,17},{29,21},{2,10},{... | collective-permute-start | bytes 1572872 | tf_op jit(solution)/shard_map/ppermute | solution.py:707
  27.7 11.9 %collective-permute-start.3 = (bf16[2,256,256]{2,1,0:T(8,128)(2,1)S(1)}, bf16[2,256,256]{2,1,0:T(8,128)(2,1)S(1)}, u32[]{:S(2)}, u32[]{:S(2)}) collective-permute-start(bf16[2,256,256]{2,1,0:T(8,128)(2,1)S(1)} %get-tuple-element.92), channel_id=1, source_target_pairs={{8,16},{12,20},{16,8},{20,12},{9,17},{13,21},{17,9},{21,13},{10,18... | collective-permute-start | bytes 786440 | tf_op jit(solution)/shard_map/ppermute | solution.py:663
  38.0 24.4 %collective-permute-start.15 = (bf16[7,256,256]{2,1,0:T(8,128)(2,1)S(1)}, bf16[7,256,256]{2,1,0:T(8,128)(2,1)S(1)}, u32[]{:S(2)}, u32[]{:S(2)}) collective-permute-start(bf16[7,256,256]{2,1,0:T(8,128)(2,1)S(1)} %get-tuple-element.115), channel_id=1, source_target_pairs={{0,1},{1,0},{2,3},{3,2},{4,5},{5,4},{6,7},{7,6},{8,9},{9,8},{10,11... | collective-permute-start | bytes 2752520 | tf_op jit(solution)/shard_map/ppermute | solution.py:714
  40.4 9.6 %collective-permute-start.10 = (bf16[2,256,256]{2,1,0:T(8,128)(2,1)S(1)}, bf16[2,256,256]{2,1,0:T(8,128)(2,1)S(1)}, u32[]{:S(2)}, u32[]{:S(2)}) collective-permute-start(bf16[2,256,256]{2,1,0:T(8,128)(2,1)S(1)} %get-tuple-element.106), channel_id=1, source_target_pairs={{16,24},{20,28},{8,0},{12,4},{17,25},{21,29},{9,1},{13,5},{18,26},... | collective-permute-start | bytes 786440 | tf_op jit(solution)/shard_map/ppermute | solution.py:663
  41.7 16.0 %collective-permute-start.8 = (bf16[4,256,256]{2,1,0:T(8,128)(2,1)S(1)}, bf16[4,256,256]{2,1,0:T(8,128)(2,1)S(1)}, u32[]{:S(2)}, u32[]{:S(2)}) collective-permute-start(bf16[4,256,256]{2,1,0:T(8,128)(2,1)S(1)} %get-tuple-element.104.refs_2_.refs_6_.refs_12_), channel_id=1, source_target_pairs={{0,8},{4,12},{24,16},{28,20},{1,9},{5,13},{25,17},{29,21},{2,10},{... | collective-permute-start | bytes 1572872 | tf_op jit(solution)/shard_map/ppermute | solution.py:707
  46.3 11.5 %collective-permute-start.9 = (bf16[4,256,256]{2,1,0:T(8,128)(2,1)S(1)}, bf16[4,256,256]{2,1,0:T(8,128)(2,1)S(1)}, u32[]{:S(2)}, u32[]{:S(2)}) collective-permute-start(bf16[4,256,256]{2,1,0:T(8,128)(2,1)S(1)} %get-tuple-element.105), channel_id=1, source_target_pairs={{8,16},{12,20},{16,8},{20,12},{9,17},{13,21},{17,9},{21,13},{10,18... | collective-permute-start | bytes 1572872 | tf_op jit(solution)/shard_map/ppermute | solution.py:663
  50.9 2.5 %collective-permute-start.11 = (bf16[2,256,256]{2,1,0:T(8,128)(2,1)S(1)}, bf16[2,256,256]{2,1,0:T(8,128)(2,1)S(1)}, u32[]{:S(2)}, u32[]{:S(2)}) collective-permute-start(bf16[2,256,256]{2,1,0:T(8,128)(2,1)S(1)} %get-tuple-element.109), channel_id=1, source_target_pairs={{0,4},{4,0},{8,12},{12,8},{16,20},{20,16},{24,28},{28,24},{1,5},{5... | collective-permute-start | bytes 786440 | tf_op jit(solution)/shard_map/ppermute | solution.py:648
  50.9 43.0 %collective-permute-start.7 = (bf16[14,256,256]{2,1,0:T(8,128)(2,1)S(1)}, bf16[14,256,256]{2,1,0:T(8,128)(2,1)S(1)}, u32[]{:S(2)}, u32[]{:S(2)}) collective-permute-start(bf16[14,256,256]{2,1,0:T(8,128)(2,1)S(1)} %get-tuple-element.102), channel_id=1, source_target_pairs={{0,4},{4,0},{1,5},{5,1},{2,6},{6,2},{3,7},{7,3}} | collective-permute-start | bytes 5505032 | tf_op jit(solution)/shard_map/ppermute | solution.py:757
  53.9 10.7 %collective-permute-start.14 = (bf16[2,256,256]{2,1,0:T(8,128)(2,1)S(1)}, bf16[2,256,256]{2,1,0:T(8,128)(2,1)S(1)}, u32[]{:S(2)}, u32[]{:S(2)}) collective-permute-start(bf16[2,256,256]{2,1,0:T(8,128)(2,1)S(1)} %get-tuple-element.114.refs_1_), channel_id=1, source_target_pairs={{0,2},{1,3},{4,6},{5,7},{8,10},{9,11},{12,14},{13,15},{16,18},{17,... | collective-permute-start | bytes 786440 | tf_op jit(solution)/shard_map/ppermute | solution.py:717
  58.5 13.8 %collective-permute-start.12 = (bf16[4,256,256]{2,1,0:T(8,128)(2,1)S(1)}, bf16[4,256,256]{2,1,0:T(8,128)(2,1)S(1)}, u32[]{:S(2)}, u32[]{:S(2)}) collective-permute-start(bf16[4,256,256]{2,1,0:T(8,128)(2,1)S(1)} %get-tuple-element.112), channel_id=1, source_target_pairs={{0,8},{4,12},{24,16},{28,20},{16,24},{20,28},{8,0},{12,4},{1,9},{5... | collective-permute-start | bytes 1572872 | tf_op jit(solution)/shard_map/ppermute | solution.py:673
  61.7 10.5 %collective-permute-start.13 = (bf16[4,256,256]{2,1,0:T(8,128)(2,1)S(1)}, bf16[4,256,256]{2,1,0:T(8,128)(2,1)S(1)}, u32[]{:S(2)}, u32[]{:S(2)}) collective-permute-start(bf16[4,256,256]{2,1,0:T(8,128)(2,1)S(1)} %get-tuple-element.113), channel_id=1, source_target_pairs={{8,16},{12,20},{16,8},{20,12},{9,17},{13,21},{17,9},{21,13},{10,18... | collective-permute-start | bytes 1572872 | tf_op jit(solution)/shard_map/ppermute | solution.py:663
  65.2 6.4 %collective-permute-start.16 = (bf16[2,256,256]{2,1,0:T(8,128)(2,1)S(1)}, bf16[2,256,256]{2,1,0:T(8,128)(2,1)S(1)}, u32[]{:S(2)}, u32[]{:S(2)}) collective-permute-start(bf16[2,256,256]{2,1,0:T(8,128)(2,1)S(1)} %get-tuple-element.118), channel_id=1, source_target_pairs={{0,1},{1,0},{2,3},{3,2},{4,5},{5,4},{6,7},{7,6},{8,9},{9,8},{10,11... | collective-permute-start | bytes 786440 | tf_op jit(solution)/shard_map/ppermute | solution.py:714
  73.4 13.9 %collective-permute-start.17 = (bf16[4,256,256]{2,1,0:T(8,128)(2,1)S(1)}, bf16[4,256,256]{2,1,0:T(8,128)(2,1)S(1)}, u32[]{:S(2)}, u32[]{:S(2)}) collective-permute-start(bf16[4,256,256]{2,1,0:T(8,128)(2,1)S(1)} %get-tuple-element.121), channel_id=1, source_target_pairs={{8,16},{12,20},{16,8},{20,12},{9,17},{13,21},{17,9},{21,13},{10,18... | collective-permute-start | bytes 1572872 | tf_op jit(solution)/shard_map/ppermute | solution.py:663
  74.1 17.1 %collective-permute-start.18 = (bf16[4,256,256]{2,1,0:T(8,128)(2,1)S(1)}, bf16[4,256,256]{2,1,0:T(8,128)(2,1)S(1)}, u32[]{:S(2)}, u32[]{:S(2)}) collective-permute-start(bf16[4,256,256]{2,1,0:T(8,128)(2,1)S(1)} %get-tuple-element.122), channel_id=1, source_target_pairs={{16,24},{20,28},{8,0},{12,4},{17,25},{21,29},{9,1},{13,5},{18,26},... | collective-permute-start | bytes 1572872 | tf_op jit(solution)/shard_map/ppermute | solution.py:663
  75.4 3.4 %collective-permute-start.19 = (bf16[2,256,256]{2,1,0:T(8,128)(2,1)S(1)}, bf16[2,256,256]{2,1,0:T(8,128)(2,1)S(1)}, u32[]{:S(2)}, u32[]{:S(2)}) collective-permute-start(bf16[2,256,256]{2,1,0:T(8,128)(2,1)S(1)} %get-tuple-element.125), channel_id=1, source_target_pairs={{0,4},{4,0},{1,5},{5,1},{2,6},{6,2},{3,7},{7,3}} | collective-permute-start | bytes 786440 | tf_op jit(solution)/shard_map/ppermute | solution.py:773
  77.6 16.3 %collective-permute-start.21 = (bf16[4,256,256]{2,1,0:T(8,128)(2,1)S(1)}, bf16[4,256,256]{2,1,0:T(8,128)(2,1)S(1)}, u32[]{:S(2)}, u32[]{:S(2)}) collective-permute-start(bf16[4,256,256]{2,1,0:T(8,128)(2,1)S(1)} %get-tuple-element.134), channel_id=1, source_target_pairs={{0,4},{4,0},{8,12},{12,8},{16,20},{20,16},{24,28},{28,24},{1,5},{5... | collective-permute-start | bytes 1572872 | tf_op jit(solution)/shard_map/ppermute | solution.py:648
  92.4 2.0 %collective-permute-start.22 = (bf16[4,256,256]{2,1,0:T(8,128)(2,1)S(1)}, bf16[4,256,256]{2,1,0:T(8,128)(2,1)S(1)}, u32[]{:S(2)}, u32[]{:S(2)}) collective-permute-start(bf16[4,256,256]{2,1,0:T(8,128)(2,1)S(1)} %get-tuple-element.136), channel_id=1, source_target_pairs={{0,4},{4,0},{8,12},{12,8},{16,20},{20,16},{24,28},{28,24},{1,5},{5... | collective-permute-start | bytes 1572872 | tf_op jit(solution)/shard_map/ppermute | solution.py:648
  92.5 17.4 %collective-permute-start.20 = (bf16[4,256,256]{2,1,0:T(8,128)(2,1)S(1)}, bf16[4,256,256]{2,1,0:T(8,128)(2,1)S(1)}, u32[]{:S(2)}, u32[]{:S(2)}) collective-permute-start(bf16[4,256,256]{2,1,0:T(8,128)(2,1)S(1)} %get-tuple-element.132), channel_id=1, source_target_pairs={{16,24},{20,28},{8,0},{12,4},{17,25},{21,29},{9,1},{13,5},{18,26},... | collective-permute-start | bytes 1572872 | tf_op jit(solution)/shard_map/ppermute | solution.py:663
  111.0 2.0 %collective-permute-start.23 = (bf16[4,256,256]{2,1,0:T(8,128)(2,1)S(1)}, bf16[4,256,256]{2,1,0:T(8,128)(2,1)S(1)}, u32[]{:S(2)}, u32[]{:S(2)}) collective-permute-start(bf16[4,256,256]{2,1,0:T(8,128)(2,1)S(1)} %get-tuple-element.143), channel_id=1, source_target_pairs={{0,4},{4,0},{8,12},{12,8},{16,20},{20,16},{24,28},{28,24},{1,5},{5... | collective-permute-start | bytes 1572872 | tf_op jit(solution)/shard_map/ppermute | solution.py:648

commit v5 on v4

--- a/solution.py
+++ b/solution.py
@@ -731,30 +731,30 @@
         down_raw = down(raw)
     sizes = [c for _, c in chunks]
     cut = sizes[1]
-    some_mine, some_other = gather(1, sizes[1] + sizes[2])
-    chain.hold(some_other)
+    mine1, others[1] = gather(1, sizes[1])
+    chain.hold(others[1])
     (native[0],) = meet(mine, theirs0, width)
-    (some_other,) = chain.passed
+    (others[1],) = chain.passed
     hop(0)
-    some_theirs = exchange(some_other)
-    others[1], others[2] = some_other[:cut], some_other[cut:]
+    theirs1 = exchange(others[1])
+    mine2, others[2] = gather(2, sizes[2])
+    (native[1],) = meet(mine1, theirs1, sizes[1])
+    hop(1)
     mine3, others[3] = gather(3, sizes[3])
-    chain.hold(others[3])
-    native[1], native[2] = meet(some_mine, some_theirs, sizes[1], sizes[2])
-    (others[3],) = chain.passed
+    chain.hold(others[2], others[3])
+    hop(0)
+    others[2], others[3] = chain.passed
+    theirs2, theirs3 = exchange(others[2]), exchange(others[3])
+    put, keep = placement(chain, place, lands, cycles)
     hop(1)
-    theirs3 = exchange(others[3])
-    chain.hold(native[2])
-    hop(0)
-    (native[2],) = chain.passed
+    (native[2],) = meet(mine2, theirs2, sizes[2])
     hop(2)
-    put, keep = placement(chain, place, lands, cycles)
+    chain.hold(top)
+    group(hop_part(0), meet_part(3, mine3, theirs3))
+    (top,) = chain.passed
+    top = lax.ppermute(top, "row", first_swap)
     if few_cols:
         side_raw = side(raw, down_raw)
-    chain.hold(top)
-    group(hop_part(0), hop_part(1), meet_part(3, mine3, theirs3))
-    (top,) = chain.passed
-    top = lax.ppermute(top, "row", first_swap)
     finish(0)
     (lead,) = chain.whole(
         lead_kernel, "lead", place, (x_mine[0], x_other[0]), [array(2, size, size)]

time: 121 us -> 117 us (0.967)
  waiting for transfers between devices: 23.2 us -> 18.7 us
  Pallas kernels: 59.3 us -> 61.3 us
  starting transfers between devices: 36.9 us -> 35.5 us
    ppermute x2, waiting for transfers between devices: 7.89 us -> 0.01 us  [down(): return lax.ppermute(own, 'col', down_pairs)]
    ppermute x3, waiting for transfers between devices: 0.01 us -> 5.18 us  [hop(): hops[i].append(lax.ppermute(native[i], 'row', hop_pairs(0)))]
    ppermute x7, waiting for transfers between devices: 7.04 us -> 4.51 us  [go(): hops[i].append(lax.ppermute(out[0], 'row', hop_pairs(h)))]
    pallas_call x20 -> x23, Pallas kernels: 55.1 us -> 57.1 us  [run(): pl.pallas_call(inner, in_specs=in_specs + [ANY] * (len(waits) + passed),...]
    ppermute x2, starting transfers between devices: 8.68 us -> 6.86 us  [down(): return lax.ppermute(own, 'col', down_pairs)]
  transfers between devices with their start and end apart: 24 -> 25, of which waited for: 7 -> 8; matrix products, arithmetic and copies ran while one was open for 0% -> 0% of each run, Pallas kernels for 38% -> 41%
where the time goes in v5:
time: 117 us
  Pallas kernels  61.3 us (52%)
  starting transfers between devices  35.5 us (30%)
  waiting for transfers between devices  18.7 us (16%)
    pallas_call x23, Pallas kernels, run(): pl.pallas_call(inner, in_specs=in_specs + [ANY] * (len(waits) + passed),...  57.1 us
    ppermute x3, starting transfers between devices, hop(): hops[i].append(lax.ppermute(native[i], 'row', hop_pairs(0)))  9.41 us
    ppermute x2, starting transfers between devices, down(): return lax.ppermute(own, 'col', down_pairs)  6.86 us
    ppermute x7, starting transfers between devices, go(): hops[i].append(lax.ppermute(out[0], 'row', hop_pairs(h)))  6.6 us
    ppermute x2, waiting for transfers between devices, side(): return lax.ppermute(out, 'col', side_pairs)  5.84 us
    ppermute x3, waiting for transfers between devices, hop(): hops[i].append(lax.ppermute(native[i], 'row', hop_pairs(0)))  5.18 us
    ppermute x7, waiting for transfers between devices, go(): hops[i].append(lax.ppermute(out[0], 'row', hop_pairs(h)))  4.51 us
    pallas_call x1, Pallas kernels, start(): pl.pallas_call(functools.partial(start_kernel, rows), grid=(1,), in_specs...  4.2 us
  transfers between devices with their start and end apart: 25, of which 8 were waited for; matrix products, arithmetic and copies ran while one was open for 0% of the time, Pallas kernels for 41%

profile of v5, /device:TPU:0, one launch (start us, length us, event | category | flops | bytes accessed | tf_op | source)
XLA Modules:
  0.0 116.6 jit_solution(7785403504381594568)
XLA Ops:
  0.8 4.2 %start.1 = (bf16[512,1792]{1,0:T(8,128)(2,1)S(1)}, s32[2,256,1]{2,1,0:T(8,128)S(1)}, s32[2,256,1]{2,1,0:T(8,128)S(1)}, s32[2,256]{1,0:T(2,128)S(1)}, bf16[7,256,...) custom-call(s32[3]{0:T(128)S(1)} %pad_add_fusion.place.refs_0_, ...), custom_call_target="tpu_custom_call" | custom-call | flops 1024 | bytes 1024 | tf_op jit(solution)/shard_map/start/pallas_call | solution.py:161
  5.5 3.8 %gather_rows.3 = (bf16[4,256,256]{2,1,0:T(8,128)(2,1)S(1)}, bf16[4,256,256]{2,1,0:T(8,128)(2,1)S(1)}, f32[8,128]{1,0:T(8,128)S(1)}) custom-call(bf16[512,1792]{1,0:T(8,128)(2,1)S(1)} %get-tuple-element.85.refs_0_.refs_1_, bf16[7,14,256,256]{3,2,1,0:T(8,128)(2,1)} %bitcast.7, f32[8,128]{1,0:T(8,128)S(1)} %get-tuple-element.86.refs_2_), custom_call_target="tpu_custom_call" | custom-call | flops 1024 | bytes 1024 | tf_op jit(solution)/shard_map/gather_rows/pallas_call | solution.py:205
  10.0 4.9 %collective-permute-start.11 = (bf16[7,256,256]{2,1,0:T(8,128)(2,1)S(1)}, bf16[7,256,256]{2,1,0:T(8,128)(2,1)S(1)}, u32[]{:S(2)}, u32[]{:S(2)}) collective-permute-start(bf16[7,256,256]{2,1,0:T(8,128)(2,1)S(1)} %get-tuple-element.115.refs_1_.refs_2_), channel_id=1, source_target_pairs={{0,2},{1,3},{4,6},{5,7},{8,10},{9,11},{12,14},{13,15},{16,18},{17,... | collective-permute-start | bytes 2752520 | tf_op jit(solution)/shard_map/ppermute | solution.py:717
  14.9 3.5 %collective-permute-start.1 = (bf16[2,256,256]{2,1,0:T(8,128)(2,1)S(1)}, bf16[2,256,256]{2,1,0:T(8,128)(2,1)S(1)}, u32[]{:S(2)}, u32[]{:S(2)}) collective-permute-start(bf16[2,256,256]{2,1,0:T(8,128)(2,1)S(1)} %get-tuple-element.89.refs_2_.refs_3_.refs_4_), channel_id=1, source_target_pairs={{0,8},{4,12},{24,16},{28,20},{1,9},{5,13},{25,17},{29,21},{2,10},{... | collective-permute-start | bytes 786440 | tf_op jit(solution)/shard_map/ppermute | solution.py:707
  18.4 3.8 %gather_rows.4 = (bf16[4,256,256]{2,1,0:T(8,128)(2,1)S(1)}, bf16[4,256,256]{2,1,0:T(8,128)(2,1)S(1)}, f32[8,128]{1,0:T(8,128)S(1)}) custom-call(bf16[512,1792]{1,0:T(8,128)(2,1)S(1)} %get-tuple-element.85.refs_0_.refs_1_, bf16[7,14,256,256]{3,2,1,0:T(8,128)(2,1)} %bitcast.8, f32[8,128]{1,0:T(8,128)S(1)} %get-tuple-element.92.refs_2_), custom_call_target="tpu_custom_call" | custom-call | flops 1024 | bytes 1024 | tf_op jit(solution)/shard_map/gather_rows/pallas_call | solution.py:205
  22.8 1.3 %collective-permute-start.6 = (bf16[4,256,256]{2,1,0:T(8,128)(2,1)S(1)}, bf16[4,256,256]{2,1,0:T(8,128)(2,1)S(1)}, u32[]{:S(2)}, u32[]{:S(2)}) collective-permute-start(bf16[4,256,256]{2,1,0:T(8,128)(2,1)S(1)} %get-tuple-element.103.refs_2_.refs_5_.refs_9_.refs_8_), channel_id=1, source_target_pairs={{0,8},{4,12},{24,16},{28,20},{1,9},{5,13},{25,17},{29,21},{2,10},{... | collective-permute-start | bytes 1572872 | tf_op jit(solution)/shard_map/ppermute | solution.py:707
  24.1 3.8 %gather_rows.5 = (bf16[4,256,256]{2,1,0:T(8,128)(2,1)S(1)}, bf16[4,256,256]{2,1,0:T(8,128)(2,1)S(1)}, f32[8,128]{1,0:T(8,128)S(1)}) custom-call(bf16[512,1792]{1,0:T(8,128)(2,1)S(1)} %get-tuple-element.85.refs_0_.refs_1_, bf16[7,14,256,256]{3,2,1,0:T(8,128)(2,1)} %bitcast.9, f32[8,128]{1,0:T(8,128)S(1)} %get-tuple-element.94.refs_2_), custom_call_target="tpu_custom_call" | custom-call | flops 1024 | bytes 1024 | tf_op jit(solution)/shard_map/gather_rows/pallas_call | solution.py:205
  29.9 1.1 placement.1
  30.9 4.2 %collective-permute-done.6.refs_3_.refs_10_ = bf16[4,256,256]{2,1,0:T(8,128)(2,1)S(1)} collective-permute-done((bf16[4,256,256]{2,1,0:T(8,128)(2,1)S(1)}, bf16[4,256,256]{2,1,0:T(8,128)(2,1)S(1)}, u32[]{:S(2)}, u32[]{:S(2)}) %collective-permute-start.6) | collective-permute-done | bytes 524320 | tf_op jit(solution)/shard_map/ppermute | solution.py:707
  37.8 1.6 %collective-permute-start.16 = (bf16[7,256,256]{2,1,0:T(8,128)(2,1)S(1)}, bf16[7,256,256]{2,1,0:T(8,128)(2,1)S(1)}, u32[]{:S(2)}, u32[]{:S(2)}) collective-permute-start(bf16[7,256,256]{2,1,0:T(8,128)(2,1)S(1)} %get-tuple-element.125), channel_id=1, source_target_pairs={{0,1},{1,0},{2,3},{3,2},{4,5},{5,4},{6,7},{7,6},{8,9},{9,8},{10,11... | collective-permute-start | bytes 2752520 | tf_op jit(solution)/shard_map/ppermute | solution.py:714
  39.4 1.3 %collective-permute-start.10 = (bf16[2,256,256]{2,1,0:T(8,128)(2,1)S(1)}, bf16[2,256,256]{2,1,0:T(8,128)(2,1)S(1)}, u32[]{:S(2)}, u32[]{:S(2)}) collective-permute-start(bf16[2,256,256]{2,1,0:T(8,128)(2,1)S(1)} %get-tuple-element.114), channel_id=1, source_target_pairs={{16,24},{20,28},{8,0},{12,4},{17,25},{21,29},{9,1},{13,5},{18,26},... | collective-permute-start | bytes 786440 | tf_op jit(solution)/shard_map/ppermute | solution.py:663
  40.7 4.6 %collective-permute-start.8 = (bf16[4,256,256]{2,1,0:T(8,128)(2,1)S(1)}, bf16[4,256,256]{2,1,0:T(8,128)(2,1)S(1)}, u32[]{:S(2)}, u32[]{:S(2)}) collective-permute-start(bf16[4,256,256]{2,1,0:T(8,128)(2,1)S(1)} %get-tuple-element.112.refs_2_.refs_6_.refs_12_), channel_id=1, source_target_pairs={{0,8},{4,12},{24,16},{28,20},{1,9},{5,13},{25,17},{29,21},{2,10},{... | collective-permute-start | bytes 1572872 | tf_op jit(solution)/shard_map/ppermute | solution.py:707
  46.0 2.3 %collective-permute-done.10.refs_6_ = bf16[2,256,256]{2,1,0:T(8,128)(2,1)S(1)} collective-permute-done((bf16[2,256,256]{2,1,0:T(8,128)(2,1)S(1)}, bf16[2,256,256]{2,1,0:T(8,128)(2,1)S(1)}, u32[]{:S(2)}, u32[]{:S(2)}) %collective-permute-start.10) | collective-permute-done | bytes 262176 | tf_op jit(solution)/shard_map/ppermute | solution.py:663
  48.3 0.9 finish.2
  49.2 2.4 %collective-permute-start.7 = (bf16[14,256,256]{2,1,0:T(8,128)(2,1)S(1)}, bf16[14,256,256]{2,1,0:T(8,128)(2,1)S(1)}, u32[]{:S(2)}, u32[]{:S(2)}) collective-permute-start(bf16[14,256,256]{2,1,0:T(8,128)(2,1)S(1)} %get-tuple-element.110), channel_id=1, source_target_pairs={{0,4},{4,0},{1,5},{5,1},{2,6},{6,2},{3,7},{7,3}} | collective-permute-start | bytes 5505032 | tf_op jit(solution)/shard_map/ppermute | solution.py:755
  52.2 1.9 %collective-permute-start.15 = (bf16[2,256,256]{2,1,0:T(8,128)(2,1)S(1)}, bf16[2,256,256]{2,1,0:T(8,128)(2,1)S(1)}, u32[]{:S(2)}, u32[]{:S(2)}) collective-permute-start(bf16[2,256,256]{2,1,0:T(8,128)(2,1)S(1)} %get-tuple-element.124.refs_1_), channel_id=1, source_target_pairs={{0,2},{1,3},{4,6},{5,7},{8,10},{9,11},{12,14},{13,15},{16,18},{17,... | collective-permute-start | bytes 786440 | tf_op jit(solution)/shard_map/ppermute | solution.py:717
  54.2 0.9 collective-permute-done.8.refs_3_.refs_7_
  55.8 3.8 %collective-permute-start.13 = (bf16[4,256,256]{2,1,0:T(8,128)(2,1)S(1)}, bf16[4,256,256]{2,1,0:T(8,128)(2,1)S(1)}, u32[]{:S(2)}, u32[]{:S(2)}) collective-permute-start(bf16[4,256,256]{2,1,0:T(8,128)(2,1)S(1)} %get-tuple-element.122), channel_id=1, source_target_pairs={{0,8},{4,12},{24,16},{28,20},{16,24},{20,28},{8,0},{12,4},{1,9},{5... | collective-permute-start | bytes 1572872 | tf_op jit(solution)/shard_map/ppermute | solution.py:673
  60.4 2.2 %panel_rows.1 = (bf16[2,7,256,256]{3,2,1,0:T(8,128)(2,1)S(1)}, bf16[2,512,256]{2,1,0:T(8,128)(2,1)S(1)}, bf16[2,256,256]{2,1,0:T(8,128)(2,1)S(1)}, f32[8,128]{1,0:T(8,128)S(1)}) custom-call(s32[3]{0:T(128)S(1)} %pad_add_fusion.place.refs_0_, bf16[512,1792]{1,0:T(8,128)(2,1)S(1)} %get-tuple-element.85.refs_0_.refs_1_, ...), custom_call_target="tpu_custom_call" | custom-call | flops 1024 | bytes 1024 | tf_op jit(solution)/shard_map/panel_rows/pallas_call | solution.py:205
  63.7 5.8 %collective-permute-done.17.refs_3_ = bf16[2,256,256]{2,1,0:T(8,128)(2,1)S(1)} collective-permute-done((bf16[2,256,256]{2,1,0:T(8,128)(2,1)S(1)}, bf16[2,256,256]{2,1,0:T(8,128)(2,1)S(1)}, u32[]{:S(2)}, u32[]{:S(2)}) %collective-permute-start.17) | collective-permute-done | bytes 262176 | tf_op jit(solution)/shard_map/ppermute | solution.py:714
  70.2 1.2 %merge_merge_finish.1 = (bf16[4,256,256]{2,1,0:T(8,128)(2,1)S(1)}, bf16[4,256,256]{2,1,0:T(8,128)(2,1)S(1)}, bf16[4,256,256]{2,1,0:T(8,128)(2,1)S(1)}, bf16[4,256,256]{2,1,0:T(8,128)(2,1)S(1)}, f32[8,128]{1,0:T(8,128)S(1)}) custom-call(s32[3]{0:T(128)S(1)} %pad_add_fusion.place.refs_0_, s32[2,256,1]{2,1,0:T(8,128)S(1)} %get-tuple-element.82.refs_1_.refs_4_.refs_7_, ...), custom_call_target="tpu_custom_call" | custom-call | flops 1024 | bytes 1024 | tf_op jit(solution)/shard_map/merge_merge_finish/pallas_call | solution.py:205
  72.1 1.3 %collective-permute-start.19 = (bf16[4,256,256]{2,1,0:T(8,128)(2,1)S(1)}, bf16[4,256,256]{2,1,0:T(8,128)(2,1)S(1)}, u32[]{:S(2)}, u32[]{:S(2)}) collective-permute-start(bf16[4,256,256]{2,1,0:T(8,128)(2,1)S(1)} %get-tuple-element.132), channel_id=1, source_target_pairs={{16,24},{20,28},{8,0},{12,4},{17,25},{21,29},{9,1},{13,5},{18,26},... | collective-permute-start | bytes 1572872 | tf_op jit(solution)/shard_map/ppermute | solution.py:663
  73.4 2.1 %collective-permute-start.20 = (bf16[2,256,256]{2,1,0:T(8,128)(2,1)S(1)}, bf16[2,256,256]{2,1,0:T(8,128)(2,1)S(1)}, u32[]{:S(2)}, u32[]{:S(2)}) collective-permute-start(bf16[2,256,256]{2,1,0:T(8,128)(2,1)S(1)} %get-tuple-element.135), channel_id=1, source_target_pairs={{0,4},{4,0},{1,5},{5,1},{2,6},{6,2},{3,7},{7,3}} | collective-permute-start | bytes 786440 | tf_op jit(solution)/shard_map/ppermute | solution.py:773
  76.1 0.8 collective-permute-done.20.refs_4_
  76.8 8.4 %factor_panels.1 = (bf16[7,256,768]{2,1,0:T(8,128)(2,1)S(1)}, bf16[7,256,256]{2,1,0:T(8,128)(2,1)S(1)}, bf16[256,256]{1,0:T(8,128)(2,1)S(1)}, f32[8,128]{1,0:T(8,128)S(1)}) custom-call(s32[3]{0:T(128)S(1)} %pad_add_fusion.place.refs_0_, s32[2,256,1]{2,1,0:T(8,128)S(1)} %get-tuple-element.81.refs_2_.refs_8_.refs_1_.refs_5_, ...), custom_call_target="tpu_custom_call" | custom-call | flops 1024 | bytes 1024 | tf_op jit(solution)/shard_map/factor_panels/pallas_call | solution.py:205
  85.3 2.2 %collective-permute-done.19.refs_9_ = bf16[4,256,256]{2,1,0:T(8,128)(2,1)S(1)} collective-permute-done((bf16[4,256,256]{2,1,0:T(8,128)(2,1)S(1)}, bf16[4,256,256]{2,1,0:T(8,128)(2,1)S(1)}, u32[]{:S(2)}, u32[]{:S(2)}) %collective-permute-start.19) | collective-permute-done | bytes 524320 | tf_op jit(solution)/shard_map/ppermute | solution.py:663
  87.5 1.1 merge_finish.1
  88.7 1.3 %collective-permute-start.21 = (bf16[4,256,256]{2,1,0:T(8,128)(2,1)S(1)}, bf16[4,256,256]{2,1,0:T(8,128)(2,1)S(1)}, u32[]{:S(2)}, u32[]{:S(2)}) collective-permute-start(bf16[4,256,256]{2,1,0:T(8,128)(2,1)S(1)} %get-tuple-element.142), channel_id=1, source_target_pairs={{16,24},{20,28},{8,0},{12,4},{17,25},{21,29},{9,1},{13,5},{18,26},... | collective-permute-start | bytes 1572872 | tf_op jit(solution)/shard_map/ppermute | solution.py:663
  90.6 15.4 %update_columns.2 = (bf16[7,14,256,256]{3,2,1,0:T(8,128)(2,1)}, f32[8,128]{1,0:T(8,128)S(1)}) custom-call(s32[3]{0:T(128)S(1)} %pad_add_fusion.place.refs_0_, s32[2,256,1]{2,1,0:T(8,128)S(1)} %get-tuple-element.81.refs_2_.refs_8_.refs_1_.refs_5_, bf16[7,14,256,256]{3,2,1,0:T(8,128)(2,1)} %bitcast.10, ...), custom_call_target="tpu_custom_call" | custom-call | flops 1024 | bytes 1024 | tf_op jit(solution)/shard_map/update_columns/pallas_call | solution.py:205
  106.0 1.0 finish.3
  107.2 1.8 %collective-permute-done.24.refs_7_ = bf16[4,256,256]{2,1,0:T(8,128)(2,1)S(1)} collective-permute-done((bf16[4,256,256]{2,1,0:T(8,128)(2,1)S(1)}, bf16[4,256,256]{2,1,0:T(8,128)(2,1)S(1)}, u32[]{:S(2)}, u32[]{:S(2)}) %collective-permute-start.24) | collective-permute-done | bytes 524320 | tf_op jit(solution)/shard_map/ppermute | solution.py:648
  109.0 7.6 %update_columns.3 = (bf16[7,14,256,256]{3,2,1,0:T(8,128)(2,1)}, f32[8,128]{1,0:T(8,128)}) custom-call(s32[3]{0:T(128)S(1)} %pad_add_fusion.place.refs_0_, s32[2,256,1]{2,1,0:T(8,128)S(1)} %get-tuple-element.81.refs_2_.refs_8_.refs_1_.refs_5_, bf16[7,14,256,256]{3,2,1,0:T(8,128)(2,1)} %bitcast.11, ...), custom_call_target="tpu_custom_call", output_to_operand_aliasing={{0}: (12, {})} | custom-call | flops 1024 | bytes 1024 | tf_op jit(solution)/shard_map/update_columns/pallas_call | solution.py:205
  (45 shorter events, 13.7 us)
Async XLA Ops:
  0.1 0.7 copy-start
  5.0 4.3 %collective-permute-start = (bf16[2,256,256]{2,1,0:T(8,128)(2,1)S(1)}, bf16[2,256,256]{2,1,0:T(8,128)(2,1)S(1)}, u32[]{:S(2)}, u32[]{:S(2)}) collective-permute-start(bf16[2,256,256]{2,1,0:T(8,128)(2,1)S(1)} %get-tuple-element.84.refs_5_), channel_id=1, source_target_pairs={{0,4},{4,0},{8,12},{12,8},{16,20},{20,16},{24,28},{28,24},{1,5},{5... | collective-permute-start | bytes 786440 | tf_op jit(solution)/shard_map/ppermute | solution.py:648
  9.8 12.3 %collective-permute-start.2 = (bf16[4,256,256]{2,1,0:T(8,128)(2,1)S(1)}, bf16[4,256,256]{2,1,0:T(8,128)(2,1)S(1)}, u32[]{:S(2)}, u32[]{:S(2)}) collective-permute-start(bf16[4,256,256]{2,1,0:T(8,128)(2,1)S(1)} %get-tuple-element.91.refs_9_), channel_id=1, source_target_pairs={{0,4},{4,0},{8,12},{12,8},{16,20},{20,16},{24,28},{28,24},{1,5},{5... | collective-permute-start | bytes 1572872 | tf_op jit(solution)/shard_map/ppermute | solution.py:648
  10.0 27.2 %collective-permute-start.11 = (bf16[7,256,256]{2,1,0:T(8,128)(2,1)S(1)}, bf16[7,256,256]{2,1,0:T(8,128)(2,1)S(1)}, u32[]{:S(2)}, u32[]{:S(2)}) collective-permute-start(bf16[7,256,256]{2,1,0:T(8,128)(2,1)S(1)} %get-tuple-element.115.refs_1_.refs_2_), channel_id=1, source_target_pairs={{0,2},{1,3},{4,6},{5,7},{8,10},{9,11},{12,14},{13,15},{16,18},{17,... | collective-permute-start | bytes 2752520 | tf_op jit(solution)/shard_map/ppermute | solution.py:717
  14.9 13.0 %collective-permute-start.1 = (bf16[2,256,256]{2,1,0:T(8,128)(2,1)S(1)}, bf16[2,256,256]{2,1,0:T(8,128)(2,1)S(1)}, u32[]{:S(2)}, u32[]{:S(2)}) collective-permute-start(bf16[2,256,256]{2,1,0:T(8,128)(2,1)S(1)} %get-tuple-element.89.refs_2_.refs_3_.refs_4_), channel_id=1, source_target_pairs={{0,8},{4,12},{24,16},{28,20},{1,9},{5,13},{25,17},{29,21},{2,10},{... | collective-permute-start | bytes 786440 | tf_op jit(solution)/shard_map/ppermute | solution.py:707
  22.8 12.4 %collective-permute-start.6 = (bf16[4,256,256]{2,1,0:T(8,128)(2,1)S(1)}, bf16[4,256,256]{2,1,0:T(8,128)(2,1)S(1)}, u32[]{:S(2)}, u32[]{:S(2)}) collective-permute-start(bf16[4,256,256]{2,1,0:T(8,128)(2,1)S(1)} %get-tuple-element.103.refs_2_.refs_5_.refs_9_.refs_8_), channel_id=1, source_target_pairs={{0,8},{4,12},{24,16},{28,20},{1,9},{5,13},{25,17},{29,21},{2,10},{... | collective-permute-start | bytes 1572872 | tf_op jit(solution)/shard_map/ppermute | solution.py:707
  28.6 7.3 %collective-permute-start.5 = (bf16[4,256,256]{2,1,0:T(8,128)(2,1)S(1)}, bf16[4,256,256]{2,1,0:T(8,128)(2,1)S(1)}, u32[]{:S(2)}, u32[]{:S(2)}) collective-permute-start(bf16[4,256,256]{2,1,0:T(8,128)(2,1)S(1)} %get-tuple-element.102.refs_13_), channel_id=1, source_target_pairs={{0,4},{4,0},{8,12},{12,8},{16,20},{20,16},{24,28},{28,24},{1,5},{5... | collective-permute-start | bytes 1572872 | tf_op jit(solution)/shard_map/ppermute | solution.py:648
  28.7 7.8 %collective-permute-start.4 = (bf16[4,256,256]{2,1,0:T(8,128)(2,1)S(1)}, bf16[4,256,256]{2,1,0:T(8,128)(2,1)S(1)}, u32[]{:S(2)}, u32[]{:S(2)}) collective-permute-start(bf16[4,256,256]{2,1,0:T(8,128)(2,1)S(1)} %get-tuple-element.100.refs_5_), channel_id=1, source_target_pairs={{0,4},{4,0},{8,12},{12,8},{16,20},{20,16},{24,28},{28,24},{1,5},{5... | collective-permute-start | bytes 1572872 | tf_op jit(solution)/shard_map/ppermute | solution.py:648
  29.2 7.3 %collective-permute-start.3 = (bf16[2,256,256]{2,1,0:T(8,128)(2,1)S(1)}, bf16[2,256,256]{2,1,0:T(8,128)(2,1)S(1)}, u32[]{:S(2)}, u32[]{:S(2)}) collective-permute-start(bf16[2,256,256]{2,1,0:T(8,128)(2,1)S(1)} %get-tuple-element.98), channel_id=1, source_target_pairs={{8,16},{12,20},{16,8},{20,12},{9,17},{13,21},{17,9},{21,13},{10,18... | collective-permute-start | bytes 786440 | tf_op jit(solution)/shard_map/ppermute | solution.py:663
  37.8 22.5 %collective-permute-start.16 = (bf16[7,256,256]{2,1,0:T(8,128)(2,1)S(1)}, bf16[7,256,256]{2,1,0:T(8,128)(2,1)S(1)}, u32[]{:S(2)}, u32[]{:S(2)}) collective-permute-start(bf16[7,256,256]{2,1,0:T(8,128)(2,1)S(1)} %get-tuple-element.125), channel_id=1, source_target_pairs={{0,1},{1,0},{2,3},{3,2},{4,5},{5,4},{6,7},{7,6},{8,9},{9,8},{10,11... | collective-permute-start | bytes 2752520 | tf_op jit(solution)/shard_map/ppermute | solution.py:714
  39.4 8.9 %collective-permute-start.10 = (bf16[2,256,256]{2,1,0:T(8,128)(2,1)S(1)}, bf16[2,256,256]{2,1,0:T(8,128)(2,1)S(1)}, u32[]{:S(2)}, u32[]{:S(2)}) collective-permute-start(bf16[2,256,256]{2,1,0:T(8,128)(2,1)S(1)} %get-tuple-element.114), channel_id=1, source_target_pairs={{16,24},{20,28},{8,0},{12,4},{17,25},{21,29},{9,1},{13,5},{18,26},... | collective-permute-start | bytes 786440 | tf_op jit(solution)/shard_map/ppermute | solution.py:663
  40.7 14.4 %collective-permute-start.8 = (bf16[4,256,256]{2,1,0:T(8,128)(2,1)S(1)}, bf16[4,256,256]{2,1,0:T(8,128)(2,1)S(1)}, u32[]{:S(2)}, u32[]{:S(2)}) collective-permute-start(bf16[4,256,256]{2,1,0:T(8,128)(2,1)S(1)} %get-tuple-element.112.refs_2_.refs_6_.refs_12_), channel_id=1, source_target_pairs={{0,8},{4,12},{24,16},{28,20},{1,9},{5,13},{25,17},{29,21},{2,10},{... | collective-permute-start | bytes 1572872 | tf_op jit(solution)/shard_map/ppermute | solution.py:707
  45.3 9.8 %collective-permute-start.9 = (bf16[4,256,256]{2,1,0:T(8,128)(2,1)S(1)}, bf16[4,256,256]{2,1,0:T(8,128)(2,1)S(1)}, u32[]{:S(2)}, u32[]{:S(2)}) collective-permute-start(bf16[4,256,256]{2,1,0:T(8,128)(2,1)S(1)} %get-tuple-element.113), channel_id=1, source_target_pairs={{8,16},{12,20},{16,8},{20,12},{9,17},{13,21},{17,9},{21,13},{10,18... | collective-permute-start | bytes 1572872 | tf_op jit(solution)/shard_map/ppermute | solution.py:663
  49.1 2.5 %collective-permute-start.12 = (bf16[2,256,256]{2,1,0:T(8,128)(2,1)S(1)}, bf16[2,256,256]{2,1,0:T(8,128)(2,1)S(1)}, u32[]{:S(2)}, u32[]{:S(2)}) collective-permute-start(bf16[2,256,256]{2,1,0:T(8,128)(2,1)S(1)} %get-tuple-element.119), channel_id=1, source_target_pairs={{0,4},{4,0},{8,12},{12,8},{16,20},{20,16},{24,28},{28,24},{1,5},{5... | collective-permute-start | bytes 786440 | tf_op jit(solution)/shard_map/ppermute | solution.py:648
  49.2 40.8 %collective-permute-start.7 = (bf16[14,256,256]{2,1,0:T(8,128)(2,1)S(1)}, bf16[14,256,256]{2,1,0:T(8,128)(2,1)S(1)}, u32[]{:S(2)}, u32[]{:S(2)}) collective-permute-start(bf16[14,256,256]{2,1,0:T(8,128)(2,1)S(1)} %get-tuple-element.110), channel_id=1, source_target_pairs={{0,4},{4,0},{1,5},{5,1},{2,6},{6,2},{3,7},{7,3}} | collective-permute-start | bytes 5505032 | tf_op jit(solution)/shard_map/ppermute | solution.py:755
  52.2 10.3 %collective-permute-start.15 = (bf16[2,256,256]{2,1,0:T(8,128)(2,1)S(1)}, bf16[2,256,256]{2,1,0:T(8,128)(2,1)S(1)}, u32[]{:S(2)}, u32[]{:S(2)}) collective-permute-start(bf16[2,256,256]{2,1,0:T(8,128)(2,1)S(1)} %get-tuple-element.124.refs_1_), channel_id=1, source_target_pairs={{0,2},{1,3},{4,6},{5,7},{8,10},{9,11},{12,14},{13,15},{16,18},{17,... | collective-permute-start | bytes 786440 | tf_op jit(solution)/shard_map/ppermute | solution.py:717
  55.8 14.3 %collective-permute-start.13 = (bf16[4,256,256]{2,1,0:T(8,128)(2,1)S(1)}, bf16[4,256,256]{2,1,0:T(8,128)(2,1)S(1)}, u32[]{:S(2)}, u32[]{:S(2)}) collective-permute-start(bf16[4,256,256]{2,1,0:T(8,128)(2,1)S(1)} %get-tuple-element.122), channel_id=1, source_target_pairs={{0,8},{4,12},{24,16},{28,20},{16,24},{20,28},{8,0},{12,4},{1,9},{5... | collective-permute-start | bytes 1572872 | tf_op jit(solution)/shard_map/ppermute | solution.py:673
  59.7 10.5 %collective-permute-start.14 = (bf16[4,256,256]{2,1,0:T(8,128)(2,1)S(1)}, bf16[4,256,256]{2,1,0:T(8,128)(2,1)S(1)}, u32[]{:S(2)}, u32[]{:S(2)}) collective-permute-start(bf16[4,256,256]{2,1,0:T(8,128)(2,1)S(1)} %get-tuple-element.123), channel_id=1, source_target_pairs={{8,16},{12,20},{16,8},{20,12},{9,17},{13,21},{17,9},{21,13},{10,18... | collective-permute-start | bytes 1572872 | tf_op jit(solution)/shard_map/ppermute | solution.py:663
  63.1 6.4 %collective-permute-start.17 = (bf16[2,256,256]{2,1,0:T(8,128)(2,1)S(1)}, bf16[2,256,256]{2,1,0:T(8,128)(2,1)S(1)}, u32[]{:S(2)}, u32[]{:S(2)}) collective-permute-start(bf16[2,256,256]{2,1,0:T(8,128)(2,1)S(1)} %get-tuple-element.128), channel_id=1, source_target_pairs={{0,1},{1,0},{2,3},{3,2},{4,5},{5,4},{6,7},{7,6},{8,9},{9,8},{10,11... | collective-permute-start | bytes 786440 | tf_op jit(solution)/shard_map/ppermute | solution.py:714
  71.4 13.9 %collective-permute-start.18 = (bf16[4,256,256]{2,1,0:T(8,128)(2,1)S(1)}, bf16[4,256,256]{2,1,0:T(8,128)(2,1)S(1)}, u32[]{:S(2)}, u32[]{:S(2)}) collective-permute-start(bf16[4,256,256]{2,1,0:T(8,128)(2,1)S(1)} %get-tuple-element.131), channel_id=1, source_target_pairs={{8,16},{12,20},{16,8},{20,12},{9,17},{13,21},{17,9},{21,13},{10,18... | collective-permute-start | bytes 1572872 | tf_op jit(solution)/shard_map/ppermute | solution.py:663
  72.1 15.4 %collective-permute-start.19 = (bf16[4,256,256]{2,1,0:T(8,128)(2,1)S(1)}, bf16[4,256,256]{2,1,0:T(8,128)(2,1)S(1)}, u32[]{:S(2)}, u32[]{:S(2)}) collective-permute-start(bf16[4,256,256]{2,1,0:T(8,128)(2,1)S(1)} %get-tuple-element.132), channel_id=1, source_target_pairs={{16,24},{20,28},{8,0},{12,4},{17,25},{21,29},{9,1},{13,5},{18,26},... | collective-permute-start | bytes 1572872 | tf_op jit(solution)/shard_map/ppermute | solution.py:663
  73.4 3.4 %collective-permute-start.20 = (bf16[2,256,256]{2,1,0:T(8,128)(2,1)S(1)}, bf16[2,256,256]{2,1,0:T(8,128)(2,1)S(1)}, u32[]{:S(2)}, u32[]{:S(2)}) collective-permute-start(bf16[2,256,256]{2,1,0:T(8,128)(2,1)S(1)} %get-tuple-element.135), channel_id=1, source_target_pairs={{0,4},{4,0},{1,5},{5,1},{2,6},{6,2},{3,7},{7,3}} | collective-permute-start | bytes 786440 | tf_op jit(solution)/shard_map/ppermute | solution.py:773
  75.5 14.5 %collective-permute-start.22 = (bf16[4,256,256]{2,1,0:T(8,128)(2,1)S(1)}, bf16[4,256,256]{2,1,0:T(8,128)(2,1)S(1)}, u32[]{:S(2)}, u32[]{:S(2)}) collective-permute-start(bf16[4,256,256]{2,1,0:T(8,128)(2,1)S(1)} %get-tuple-element.144), channel_id=1, source_target_pairs={{0,4},{4,0},{8,12},{12,8},{16,20},{20,16},{24,28},{28,24},{1,5},{5... | collective-permute-start | bytes 1572872 | tf_op jit(solution)/shard_map/ppermute | solution.py:648
  88.6 2.0 %collective-permute-start.23 = (bf16[4,256,256]{2,1,0:T(8,128)(2,1)S(1)}, bf16[4,256,256]{2,1,0:T(8,128)(2,1)S(1)}, u32[]{:S(2)}, u32[]{:S(2)}) collective-permute-start(bf16[4,256,256]{2,1,0:T(8,128)(2,1)S(1)} %get-tuple-element.146), channel_id=1, source_target_pairs={{0,4},{4,0},{8,12},{12,8},{16,20},{20,16},{24,28},{28,24},{1,5},{5... | collective-permute-start | bytes 1572872 | tf_op jit(solution)/shard_map/ppermute | solution.py:648
  88.7 17.3 %collective-permute-start.21 = (bf16[4,256,256]{2,1,0:T(8,128)(2,1)S(1)}, bf16[4,256,256]{2,1,0:T(8,128)(2,1)S(1)}, u32[]{:S(2)}, u32[]{:S(2)}) collective-permute-start(bf16[4,256,256]{2,1,0:T(8,128)(2,1)S(1)} %get-tuple-element.142), channel_id=1, source_target_pairs={{16,24},{20,28},{8,0},{12,4},{17,25},{21,29},{9,1},{13,5},{18,26},... | collective-permute-start | bytes 1572872 | tf_op jit(solution)/shard_map/ppermute | solution.py:663
  107.0 2.0 %collective-permute-start.24 = (bf16[4,256,256]{2,1,0:T(8,128)(2,1)S(1)}, bf16[4,256,256]{2,1,0:T(8,128)(2,1)S(1)}, u32[]{:S(2)}, u32[]{:S(2)}) collective-permute-start(bf16[4,256,256]{2,1,0:T(8,128)(2,1)S(1)} %get-tuple-element.153), channel_id=1, source_target_pairs={{0,4},{4,0},{8,12},{12,8},{16,20},{20,16},{24,28},{28,24},{1,5},{5... | collective-permute-start | bytes 1572872 | tf_op jit(solution)/shard_map/ppermute | solution.py:648

commit v6 on v5

--- a/solution.py
+++ b/solution.py
@@ -737,9 +737,9 @@
     (others[1],) = chain.passed
     hop(0)
     theirs1 = exchange(others[1])
-    mine2, others[2] = gather(2, sizes[2])
     (native[1],) = meet(mine1, theirs1, sizes[1])
     hop(1)
+    mine2, others[2] = gather(2, sizes[2])
     mine3, others[3] = gather(3, sizes[3])
     chain.hold(others[2], others[3])
     hop(0)

time: 117 us -> 118 us (level)
  waiting for transfers between devices: 18.7 us -> 20 us
    ppermute x7, waiting for transfers between devices: 4.51 us -> 5.69 us  [go(): hops[i].append(lax.ppermute(out[0], 'row', hop_pairs(h)))]
  transfers between devices with their start and end apart: 25 -> 25, of which waited for: 8 -> 8; matrix products, arithmetic and copies ran while one was open for 0% -> 0% of each run, Pallas kernels for 41% -> 40%
where the time goes in v6:
time: 118 us
  Pallas kernels  61.3 us (52%)
  starting transfers between devices  35.2 us (30%)
  waiting for transfers between devices  20 us (17%)
    pallas_call x23, Pallas kernels, run(): pl.pallas_call(inner, in_specs=in_specs + [ANY] * (len(waits) + passed),...  57.1 us
    ppermute x3, starting transfers between devices, hop(): hops[i].append(lax.ppermute(native[i], 'row', hop_pairs(0)))  9.41 us
    ppermute x7, starting transfers between devices, go(): hops[i].append(lax.ppermute(out[0], 'row', hop_pairs(h)))  6.6 us
    ppermute x2, starting transfers between devices, down(): return lax.ppermute(own, 'col', down_pairs)  6.58 us
    ppermute x2, waiting for transfers between devices, side(): return lax.ppermute(out, 'col', side_pairs)  5.84 us
    ppermute x7, waiting for transfers between devices, go(): hops[i].append(lax.ppermute(out[0], 'row', hop_pairs(h)))  5.69 us
    ppermute x3, waiting for transfers between devices, hop(): hops[i].append(lax.ppermute(native[i], 'row', hop_pairs(0)))  5.36 us
    pallas_call x1, Pallas kernels, start(): pl.pallas_call(functools.partial(start_kernel, rows), grid=(1,), in_specs...  4.2 us
  transfers between devices with their start and end apart: 25, of which 8 were waited for; matrix products, arithmetic and copies ran while one was open for 0% of the time, Pallas kernels for 40%

profile of v6, /device:TPU:0, one launch (start us, length us, event | category | flops | bytes accessed | tf_op | source)
XLA Modules:
  0.0 117.7 jit_solution(9935932648919611734)
XLA Ops:
  0.8 4.2 %start.1 = (bf16[512,1792]{1,0:T(8,128)(2,1)S(1)}, s32[2,256,1]{2,1,0:T(8,128)S(1)}, s32[2,256,1]{2,1,0:T(8,128)S(1)}, s32[2,256]{1,0:T(2,128)S(1)}, bf16[7,256,...) custom-call(s32[3]{0:T(128)S(1)} %pad_add_fusion.place.refs_0_, ...), custom_call_target="tpu_custom_call" | custom-call | flops 1024 | bytes 1024 | tf_op jit(solution)/shard_map/start/pallas_call | solution.py:161
  5.5 3.8 %gather_rows.3 = (bf16[4,256,256]{2,1,0:T(8,128)(2,1)S(1)}, bf16[4,256,256]{2,1,0:T(8,128)(2,1)S(1)}, f32[8,128]{1,0:T(8,128)S(1)}) custom-call(bf16[512,1792]{1,0:T(8,128)(2,1)S(1)} %get-tuple-element.85.refs_0_.refs_1_, bf16[7,14,256,256]{3,2,1,0:T(8,128)(2,1)} %bitcast.7, f32[8,128]{1,0:T(8,128)S(1)} %get-tuple-element.86.refs_2_), custom_call_target="tpu_custom_call" | custom-call | flops 1024 | bytes 1024 | tf_op jit(solution)/shard_map/gather_rows/pallas_call | solution.py:205
  10.0 4.9 %collective-permute-start.11 = (bf16[7,256,256]{2,1,0:T(8,128)(2,1)S(1)}, bf16[7,256,256]{2,1,0:T(8,128)(2,1)S(1)}, u32[]{:S(2)}, u32[]{:S(2)}) collective-permute-start(bf16[7,256,256]{2,1,0:T(8,128)(2,1)S(1)} %get-tuple-element.115.refs_1_.refs_2_), channel_id=1, source_target_pairs={{0,2},{1,3},{4,6},{5,7},{8,10},{9,11},{12,14},{13,15},{16,18},{17,... | collective-permute-start | bytes 2752520 | tf_op jit(solution)/shard_map/ppermute | solution.py:717
  14.9 3.5 %collective-permute-start.1 = (bf16[2,256,256]{2,1,0:T(8,128)(2,1)S(1)}, bf16[2,256,256]{2,1,0:T(8,128)(2,1)S(1)}, u32[]{:S(2)}, u32[]{:S(2)}) collective-permute-start(bf16[2,256,256]{2,1,0:T(8,128)(2,1)S(1)} %get-tuple-element.89.refs_2_.refs_3_.refs_4_), channel_id=1, source_target_pairs={{0,8},{4,12},{24,16},{28,20},{1,9},{5,13},{25,17},{29,21},{2,10},{... | collective-permute-start | bytes 786440 | tf_op jit(solution)/shard_map/ppermute | solution.py:707
  19.0 1.3 %collective-permute-start.6 = (bf16[4,256,256]{2,1,0:T(8,128)(2,1)S(1)}, bf16[4,256,256]{2,1,0:T(8,128)(2,1)S(1)}, u32[]{:S(2)}, u32[]{:S(2)}) collective-permute-start(bf16[4,256,256]{2,1,0:T(8,128)(2,1)S(1)} %get-tuple-element.103.refs_2_.refs_5_.refs_9_.refs_8_), channel_id=1, source_target_pairs={{0,8},{4,12},{24,16},{28,20},{1,9},{5,13},{25,17},{29,21},{2,10},{... | collective-permute-start | bytes 1572872 | tf_op jit(solution)/shard_map/ppermute | solution.py:707
  20.4 3.8 %gather_rows.4 = (bf16[4,256,256]{2,1,0:T(8,128)(2,1)S(1)}, bf16[4,256,256]{2,1,0:T(8,128)(2,1)S(1)}, f32[8,128]{1,0:T(8,128)S(1)}) custom-call(bf16[512,1792]{1,0:T(8,128)(2,1)S(1)} %get-tuple-element.85.refs_0_.refs_1_, bf16[7,14,256,256]{3,2,1,0:T(8,128)(2,1)} %bitcast.8, f32[8,128]{1,0:T(8,128)S(1)} %get-tuple-element.93.refs_2_), custom_call_target="tpu_custom_call" | custom-call | flops 1024 | bytes 1024 | tf_op jit(solution)/shard_map/gather_rows/pallas_call | solution.py:205
  24.1 3.8 %gather_rows.5 = (bf16[4,256,256]{2,1,0:T(8,128)(2,1)S(1)}, bf16[4,256,256]{2,1,0:T(8,128)(2,1)S(1)}, f32[8,128]{1,0:T(8,128)S(1)}) custom-call(bf16[512,1792]{1,0:T(8,128)(2,1)S(1)} %get-tuple-element.85.refs_0_.refs_1_, bf16[7,14,256,256]{3,2,1,0:T(8,128)(2,1)} %bitcast.9, f32[8,128]{1,0:T(8,128)S(1)} %get-tuple-element.94.refs_2_), custom_call_target="tpu_custom_call" | custom-call | flops 1024 | bytes 1024 | tf_op jit(solution)/shard_map/gather_rows/pallas_call | solution.py:205
  29.9 1.1 placement.1
  30.9 4.1 %collective-permute-done.6.refs_3_.refs_10_ = bf16[4,256,256]{2,1,0:T(8,128)(2,1)S(1)} collective-permute-done((bf16[4,256,256]{2,1,0:T(8,128)(2,1)S(1)}, bf16[4,256,256]{2,1,0:T(8,128)(2,1)S(1)}, u32[]{:S(2)}, u32[]{:S(2)}) %collective-permute-start.6) | collective-permute-done | bytes 524320 | tf_op jit(solution)/shard_map/ppermute | solution.py:707
  37.7 1.6 %collective-permute-start.16 = (bf16[7,256,256]{2,1,0:T(8,128)(2,1)S(1)}, bf16[7,256,256]{2,1,0:T(8,128)(2,1)S(1)}, u32[]{:S(2)}, u32[]{:S(2)}) collective-permute-start(bf16[7,256,256]{2,1,0:T(8,128)(2,1)S(1)} %get-tuple-element.125), channel_id=1, source_target_pairs={{0,1},{1,0},{2,3},{3,2},{4,5},{5,4},{6,7},{7,6},{8,9},{9,8},{10,11... | collective-permute-start | bytes 2752520 | tf_op jit(solution)/shard_map/ppermute | solution.py:714
  39.3 1.3 %collective-permute-start.10 = (bf16[2,256,256]{2,1,0:T(8,128)(2,1)S(1)}, bf16[2,256,256]{2,1,0:T(8,128)(2,1)S(1)}, u32[]{:S(2)}, u32[]{:S(2)}) collective-permute-start(bf16[2,256,256]{2,1,0:T(8,128)(2,1)S(1)} %get-tuple-element.114), channel_id=1, source_target_pairs={{16,24},{20,28},{8,0},{12,4},{17,25},{21,29},{9,1},{13,5},{18,26},... | collective-permute-start | bytes 786440 | tf_op jit(solution)/shard_map/ppermute | solution.py:663
  40.6 4.6 %collective-permute-start.8 = (bf16[4,256,256]{2,1,0:T(8,128)(2,1)S(1)}, bf16[4,256,256]{2,1,0:T(8,128)(2,1)S(1)}, u32[]{:S(2)}, u32[]{:S(2)}) collective-permute-start(bf16[4,256,256]{2,1,0:T(8,128)(2,1)S(1)} %get-tuple-element.112.refs_2_.refs_6_.refs_12_), channel_id=1, source_target_pairs={{0,8},{4,12},{24,16},{28,20},{1,9},{5,13},{25,17},{29,21},{2,10},{... | collective-permute-start | bytes 1572872 | tf_op jit(solution)/shard_map/ppermute | solution.py:707
  45.9 2.7 %collective-permute-done.10.refs_6_ = bf16[2,256,256]{2,1,0:T(8,128)(2,1)S(1)} collective-permute-done((bf16[2,256,256]{2,1,0:T(8,128)(2,1)S(1)}, bf16[2,256,256]{2,1,0:T(8,128)(2,1)S(1)}, u32[]{:S(2)}, u32[]{:S(2)}) %collective-permute-start.10) | collective-permute-done | bytes 262176 | tf_op jit(solution)/shard_map/ppermute | solution.py:663
  48.6 0.9 finish.2
  49.5 2.4 %collective-permute-start.7 = (bf16[14,256,256]{2,1,0:T(8,128)(2,1)S(1)}, bf16[14,256,256]{2,1,0:T(8,128)(2,1)S(1)}, u32[]{:S(2)}, u32[]{:S(2)}) collective-permute-start(bf16[14,256,256]{2,1,0:T(8,128)(2,1)S(1)} %get-tuple-element.110), channel_id=1, source_target_pairs={{0,4},{4,0},{1,5},{5,1},{2,6},{6,2},{3,7},{7,3}} | collective-permute-start | bytes 5505032 | tf_op jit(solution)/shard_map/ppermute | solution.py:755
  52.5 1.7 %collective-permute-start.15 = (bf16[2,256,256]{2,1,0:T(8,128)(2,1)S(1)}, bf16[2,256,256]{2,1,0:T(8,128)(2,1)S(1)}, u32[]{:S(2)}, u32[]{:S(2)}) collective-permute-start(bf16[2,256,256]{2,1,0:T(8,128)(2,1)S(1)} %get-tuple-element.124.refs_1_), channel_id=1, source_target_pairs={{0,2},{1,3},{4,6},{5,7},{8,10},{9,11},{12,14},{13,15},{16,18},{17,... | collective-permute-start | bytes 786440 | tf_op jit(solution)/shard_map/ppermute | solution.py:717
  54.2 1.2 %collective-permute-done.8.refs_3_.refs_7_ = bf16[4,256,256]{2,1,0:T(8,128)(2,1)S(1)} collective-permute-done((bf16[4,256,256]{2,1,0:T(8,128)(2,1)S(1)}, bf16[4,256,256]{2,1,0:T(8,128)(2,1)S(1)}, u32[]{:S(2)}, u32[]{:S(2)}) %collective-permute-start.8) | collective-permute-done | bytes 524320 | tf_op jit(solution)/shard_map/ppermute | solution.py:707
  56.1 3.8 %collective-permute-start.13 = (bf16[4,256,256]{2,1,0:T(8,128)(2,1)S(1)}, bf16[4,256,256]{2,1,0:T(8,128)(2,1)S(1)}, u32[]{:S(2)}, u32[]{:S(2)}) collective-permute-start(bf16[4,256,256]{2,1,0:T(8,128)(2,1)S(1)} %get-tuple-element.122), channel_id=1, source_target_pairs={{0,8},{4,12},{24,16},{28,20},{16,24},{20,28},{8,0},{12,4},{1,9},{5... | collective-permute-start | bytes 1572872 | tf_op jit(solution)/shard_map/ppermute | solution.py:673
  60.7 2.2 %panel_rows.1 = (bf16[2,7,256,256]{3,2,1,0:T(8,128)(2,1)S(1)}, bf16[2,512,256]{2,1,0:T(8,128)(2,1)S(1)}, bf16[2,256,256]{2,1,0:T(8,128)(2,1)S(1)}, f32[8,128]{1,0:T(8,128)S(1)}) custom-call(s32[3]{0:T(128)S(1)} %pad_add_fusion.place.refs_0_, bf16[512,1792]{1,0:T(8,128)(2,1)S(1)} %get-tuple-element.85.refs_0_.refs_1_, ...), custom_call_target="tpu_custom_call" | custom-call | flops 1024 | bytes 1024 | tf_op jit(solution)/shard_map/panel_rows/pallas_call | solution.py:205
  64.0 5.8 %collective-permute-done.17.refs_3_ = bf16[2,256,256]{2,1,0:T(8,128)(2,1)S(1)} collective-permute-done((bf16[2,256,256]{2,1,0:T(8,128)(2,1)S(1)}, bf16[2,256,256]{2,1,0:T(8,128)(2,1)S(1)}, u32[]{:S(2)}, u32[]{:S(2)}) %collective-permute-start.17) | collective-permute-done | bytes 262176 | tf_op jit(solution)/shard_map/ppermute | solution.py:714
  70.5 1.2 %merge_merge_finish.1 = (bf16[4,256,256]{2,1,0:T(8,128)(2,1)S(1)}, bf16[4,256,256]{2,1,0:T(8,128)(2,1)S(1)}, bf16[4,256,256]{2,1,0:T(8,128)(2,1)S(1)}, bf16[4,256,256]{2,1,0:T(8,128)(2,1)S(1)}, f32[8,128]{1,0:T(8,128)S(1)}) custom-call(s32[3]{0:T(128)S(1)} %pad_add_fusion.place.refs_0_, s32[2,256,1]{2,1,0:T(8,128)S(1)} %get-tuple-element.82.refs_1_.refs_4_.refs_7_, ...), custom_call_target="tpu_custom_call" | custom-call | flops 1024 | bytes 1024 | tf_op jit(solution)/shard_map/merge_merge_finish/pallas_call | solution.py:205
  72.4 1.3 %collective-permute-start.19 = (bf16[4,256,256]{2,1,0:T(8,128)(2,1)S(1)}, bf16[4,256,256]{2,1,0:T(8,128)(2,1)S(1)}, u32[]{:S(2)}, u32[]{:S(2)}) collective-permute-start(bf16[4,256,256]{2,1,0:T(8,128)(2,1)S(1)} %get-tuple-element.132), channel_id=1, source_target_pairs={{16,24},{20,28},{8,0},{12,4},{17,25},{21,29},{9,1},{13,5},{18,26},... | collective-permute-start | bytes 1572872 | tf_op jit(solution)/shard_map/ppermute | solution.py:663
  73.7 2.1 %collective-permute-start.20 = (bf16[2,256,256]{2,1,0:T(8,128)(2,1)S(1)}, bf16[2,256,256]{2,1,0:T(8,128)(2,1)S(1)}, u32[]{:S(2)}, u32[]{:S(2)}) collective-permute-start(bf16[2,256,256]{2,1,0:T(8,128)(2,1)S(1)} %get-tuple-element.135), channel_id=1, source_target_pairs={{0,4},{4,0},{1,5},{5,1},{2,6},{6,2},{3,7},{7,3}} | collective-permute-start | bytes 786440 | tf_op jit(solution)/shard_map/ppermute | solution.py:773
  76.3 0.8 collective-permute-done.20.refs_4_
  77.1 8.4 %factor_panels.1 = (bf16[7,256,768]{2,1,0:T(8,128)(2,1)S(1)}, bf16[7,256,256]{2,1,0:T(8,128)(2,1)S(1)}, bf16[256,256]{1,0:T(8,128)(2,1)S(1)}, f32[8,128]{1,0:T(8,128)S(1)}) custom-call(s32[3]{0:T(128)S(1)} %pad_add_fusion.place.refs_0_, s32[2,256,1]{2,1,0:T(8,128)S(1)} %get-tuple-element.81.refs_2_.refs_8_.refs_1_.refs_5_, ...), custom_call_target="tpu_custom_call" | custom-call | flops 1024 | bytes 1024 | tf_op jit(solution)/shard_map/factor_panels/pallas_call | solution.py:205
  85.5 3.0 %collective-permute-done.19.refs_9_ = bf16[4,256,256]{2,1,0:T(8,128)(2,1)S(1)} collective-permute-done((bf16[4,256,256]{2,1,0:T(8,128)(2,1)S(1)}, bf16[4,256,256]{2,1,0:T(8,128)(2,1)S(1)}, u32[]{:S(2)}, u32[]{:S(2)}) %collective-permute-start.19) | collective-permute-done | bytes 524320 | tf_op jit(solution)/shard_map/ppermute | solution.py:663
  88.5 1.1 merge_finish.1
  89.8 1.3 %collective-permute-start.21 = (bf16[4,256,256]{2,1,0:T(8,128)(2,1)S(1)}, bf16[4,256,256]{2,1,0:T(8,128)(2,1)S(1)}, u32[]{:S(2)}, u32[]{:S(2)}) collective-permute-start(bf16[4,256,256]{2,1,0:T(8,128)(2,1)S(1)} %get-tuple-element.142), channel_id=1, source_target_pairs={{16,24},{20,28},{8,0},{12,4},{17,25},{21,29},{9,1},{13,5},{18,26},... | collective-permute-start | bytes 1572872 | tf_op jit(solution)/shard_map/ppermute | solution.py:663
  91.7 15.4 %update_columns.2 = (bf16[7,14,256,256]{3,2,1,0:T(8,128)(2,1)}, f32[8,128]{1,0:T(8,128)S(1)}) custom-call(s32[3]{0:T(128)S(1)} %pad_add_fusion.place.refs_0_, s32[2,256,1]{2,1,0:T(8,128)S(1)} %get-tuple-element.81.refs_2_.refs_8_.refs_1_.refs_5_, bf16[7,14,256,256]{3,2,1,0:T(8,128)(2,1)} %bitcast.10, ...), custom_call_target="tpu_custom_call" | custom-call | flops 1024 | bytes 1024 | tf_op jit(solution)/shard_map/update_columns/pallas_call | solution.py:205
  107.1 1.0 finish.3
  108.3 1.8 %collective-permute-done.24.refs_7_ = bf16[4,256,256]{2,1,0:T(8,128)(2,1)S(1)} collective-permute-done((bf16[4,256,256]{2,1,0:T(8,128)(2,1)S(1)}, bf16[4,256,256]{2,1,0:T(8,128)(2,1)S(1)}, u32[]{:S(2)}, u32[]{:S(2)}) %collective-permute-start.24) | collective-permute-done | bytes 524320 | tf_op jit(solution)/shard_map/ppermute | solution.py:648
  110.1 7.6 %update_columns.3 = (bf16[7,14,256,256]{3,2,1,0:T(8,128)(2,1)}, f32[8,128]{1,0:T(8,128)}) custom-call(s32[3]{0:T(128)S(1)} %pad_add_fusion.place.refs_0_, s32[2,256,1]{2,1,0:T(8,128)S(1)} %get-tuple-element.81.refs_2_.refs_8_.refs_1_.refs_5_, bf16[7,14,256,256]{3,2,1,0:T(8,128)(2,1)} %bitcast.11, ...), custom_call_target="tpu_custom_call", output_to_operand_aliasing={{0}: (12, {})} | custom-call | flops 1024 | bytes 1024 | tf_op jit(solution)/shard_map/update_columns/pallas_call | solution.py:205
  (45 shorter events, 13.7 us)
Async XLA Ops:
  0.1 0.7 copy-start
  5.0 4.3 %collective-permute-start = (bf16[2,256,256]{2,1,0:T(8,128)(2,1)S(1)}, bf16[2,256,256]{2,1,0:T(8,128)(2,1)S(1)}, u32[]{:S(2)}, u32[]{:S(2)}) collective-permute-start(bf16[2,256,256]{2,1,0:T(8,128)(2,1)S(1)} %get-tuple-element.84.refs_5_), channel_id=1, source_target_pairs={{0,4},{4,0},{8,12},{12,8},{16,20},{20,16},{24,28},{28,24},{1,5},{5... | collective-permute-start | bytes 786440 | tf_op jit(solution)/shard_map/ppermute | solution.py:648
  9.8 8.6 %collective-permute-start.2 = (bf16[4,256,256]{2,1,0:T(8,128)(2,1)S(1)}, bf16[4,256,256]{2,1,0:T(8,128)(2,1)S(1)}, u32[]{:S(2)}, u32[]{:S(2)}) collective-permute-start(bf16[4,256,256]{2,1,0:T(8,128)(2,1)S(1)} %get-tuple-element.91.refs_9_), channel_id=1, source_target_pairs={{0,4},{4,0},{8,12},{12,8},{16,20},{20,16},{24,28},{28,24},{1,5},{5... | collective-permute-start | bytes 1572872 | tf_op jit(solution)/shard_map/ppermute | solution.py:648
  10.0 27.1 %collective-permute-start.11 = (bf16[7,256,256]{2,1,0:T(8,128)(2,1)S(1)}, bf16[7,256,256]{2,1,0:T(8,128)(2,1)S(1)}, u32[]{:S(2)}, u32[]{:S(2)}) collective-permute-start(bf16[7,256,256]{2,1,0:T(8,128)(2,1)S(1)} %get-tuple-element.115.refs_1_.refs_2_), channel_id=1, source_target_pairs={{0,2},{1,3},{4,6},{5,7},{8,10},{9,11},{12,14},{13,15},{16,18},{17,... | collective-permute-start | bytes 2752520 | tf_op jit(solution)/shard_map/ppermute | solution.py:717
  14.9 13.0 %collective-permute-start.1 = (bf16[2,256,256]{2,1,0:T(8,128)(2,1)S(1)}, bf16[2,256,256]{2,1,0:T(8,128)(2,1)S(1)}, u32[]{:S(2)}, u32[]{:S(2)}) collective-permute-start(bf16[2,256,256]{2,1,0:T(8,128)(2,1)S(1)} %get-tuple-element.89.refs_2_.refs_3_.refs_4_), channel_id=1, source_target_pairs={{0,8},{4,12},{24,16},{28,20},{1,9},{5,13},{25,17},{29,21},{2,10},{... | collective-permute-start | bytes 786440 | tf_op jit(solution)/shard_map/ppermute | solution.py:707
  19.0 16.1 %collective-permute-start.6 = (bf16[4,256,256]{2,1,0:T(8,128)(2,1)S(1)}, bf16[4,256,256]{2,1,0:T(8,128)(2,1)S(1)}, u32[]{:S(2)}, u32[]{:S(2)}) collective-permute-start(bf16[4,256,256]{2,1,0:T(8,128)(2,1)S(1)} %get-tuple-element.103.refs_2_.refs_5_.refs_9_.refs_8_), channel_id=1, source_target_pairs={{0,8},{4,12},{24,16},{28,20},{1,9},{5,13},{25,17},{29,21},{2,10},{... | collective-permute-start | bytes 1572872 | tf_op jit(solution)/shard_map/ppermute | solution.py:707
  28.6 7.1 %collective-permute-start.5 = (bf16[4,256,256]{2,1,0:T(8,128)(2,1)S(1)}, bf16[4,256,256]{2,1,0:T(8,128)(2,1)S(1)}, u32[]{:S(2)}, u32[]{:S(2)}) collective-permute-start(bf16[4,256,256]{2,1,0:T(8,128)(2,1)S(1)} %get-tuple-element.102.refs_13_), channel_id=1, source_target_pairs={{0,4},{4,0},{8,12},{12,8},{16,20},{20,16},{24,28},{28,24},{1,5},{5... | collective-permute-start | bytes 1572872 | tf_op jit(solution)/shard_map/ppermute | solution.py:648
  28.7 7.7 %collective-permute-start.4 = (bf16[4,256,256]{2,1,0:T(8,128)(2,1)S(1)}, bf16[4,256,256]{2,1,0:T(8,128)(2,1)S(1)}, u32[]{:S(2)}, u32[]{:S(2)}) collective-permute-start(bf16[4,256,256]{2,1,0:T(8,128)(2,1)S(1)} %get-tuple-element.100.refs_5_), channel_id=1, source_target_pairs={{0,4},{4,0},{8,12},{12,8},{16,20},{20,16},{24,28},{28,24},{1,5},{5... | collective-permute-start | bytes 1572872 | tf_op jit(solution)/shard_map/ppermute | solution.py:648
  29.2 7.2 %collective-permute-start.3 = (bf16[2,256,256]{2,1,0:T(8,128)(2,1)S(1)}, bf16[2,256,256]{2,1,0:T(8,128)(2,1)S(1)}, u32[]{:S(2)}, u32[]{:S(2)}) collective-permute-start(bf16[2,256,256]{2,1,0:T(8,128)(2,1)S(1)} %get-tuple-element.98), channel_id=1, source_target_pairs={{8,16},{12,20},{16,8},{20,12},{9,17},{13,21},{17,9},{21,13},{10,18... | collective-permute-start | bytes 786440 | tf_op jit(solution)/shard_map/ppermute | solution.py:663
  37.7 22.9 %collective-permute-start.16 = (bf16[7,256,256]{2,1,0:T(8,128)(2,1)S(1)}, bf16[7,256,256]{2,1,0:T(8,128)(2,1)S(1)}, u32[]{:S(2)}, u32[]{:S(2)}) collective-permute-start(bf16[7,256,256]{2,1,0:T(8,128)(2,1)S(1)} %get-tuple-element.125), channel_id=1, source_target_pairs={{0,1},{1,0},{2,3},{3,2},{4,5},{5,4},{6,7},{7,6},{8,9},{9,8},{10,11... | collective-permute-start | bytes 2752520 | tf_op jit(solution)/shard_map/ppermute | solution.py:714
  39.3 9.3 %collective-permute-start.10 = (bf16[2,256,256]{2,1,0:T(8,128)(2,1)S(1)}, bf16[2,256,256]{2,1,0:T(8,128)(2,1)S(1)}, u32[]{:S(2)}, u32[]{:S(2)}) collective-permute-start(bf16[2,256,256]{2,1,0:T(8,128)(2,1)S(1)} %get-tuple-element.114), channel_id=1, source_target_pairs={{16,24},{20,28},{8,0},{12,4},{17,25},{21,29},{9,1},{13,5},{18,26},... | collective-permute-start | bytes 786440 | tf_op jit(solution)/shard_map/ppermute | solution.py:663
  40.6 14.8 %collective-permute-start.8 = (bf16[4,256,256]{2,1,0:T(8,128)(2,1)S(1)}, bf16[4,256,256]{2,1,0:T(8,128)(2,1)S(1)}, u32[]{:S(2)}, u32[]{:S(2)}) collective-permute-start(bf16[4,256,256]{2,1,0:T(8,128)(2,1)S(1)} %get-tuple-element.112.refs_2_.refs_6_.refs_12_), channel_id=1, source_target_pairs={{0,8},{4,12},{24,16},{28,20},{1,9},{5,13},{25,17},{29,21},{2,10},{... | collective-permute-start | bytes 1572872 | tf_op jit(solution)/shard_map/ppermute | solution.py:707
  45.2 10.2 %collective-permute-start.9 = (bf16[4,256,256]{2,1,0:T(8,128)(2,1)S(1)}, bf16[4,256,256]{2,1,0:T(8,128)(2,1)S(1)}, u32[]{:S(2)}, u32[]{:S(2)}) collective-permute-start(bf16[4,256,256]{2,1,0:T(8,128)(2,1)S(1)} %get-tuple-element.113), channel_id=1, source_target_pairs={{8,16},{12,20},{16,8},{20,12},{9,17},{13,21},{17,9},{21,13},{10,18... | collective-permute-start | bytes 1572872 | tf_op jit(solution)/shard_map/ppermute | solution.py:663
  49.4 2.5 %collective-permute-start.12 = (bf16[2,256,256]{2,1,0:T(8,128)(2,1)S(1)}, bf16[2,256,256]{2,1,0:T(8,128)(2,1)S(1)}, u32[]{:S(2)}, u32[]{:S(2)}) collective-permute-start(bf16[2,256,256]{2,1,0:T(8,128)(2,1)S(1)} %get-tuple-element.119), channel_id=1, source_target_pairs={{0,4},{4,0},{8,12},{12,8},{16,20},{20,16},{24,28},{28,24},{1,5},{5... | collective-permute-start | bytes 786440 | tf_op jit(solution)/shard_map/ppermute | solution.py:648
  49.5 41.6 %collective-permute-start.7 = (bf16[14,256,256]{2,1,0:T(8,128)(2,1)S(1)}, bf16[14,256,256]{2,1,0:T(8,128)(2,1)S(1)}, u32[]{:S(2)}, u32[]{:S(2)}) collective-permute-start(bf16[14,256,256]{2,1,0:T(8,128)(2,1)S(1)} %get-tuple-element.110), channel_id=1, source_target_pairs={{0,4},{4,0},{1,5},{5,1},{2,6},{6,2},{3,7},{7,3}} | collective-permute-start | bytes 5505032 | tf_op jit(solution)/shard_map/ppermute | solution.py:755
  52.5 10.3 %collective-permute-start.15 = (bf16[2,256,256]{2,1,0:T(8,128)(2,1)S(1)}, bf16[2,256,256]{2,1,0:T(8,128)(2,1)S(1)}, u32[]{:S(2)}, u32[]{:S(2)}) collective-permute-start(bf16[2,256,256]{2,1,0:T(8,128)(2,1)S(1)} %get-tuple-element.124.refs_1_), channel_id=1, source_target_pairs={{0,2},{1,3},{4,6},{5,7},{8,10},{9,11},{12,14},{13,15},{16,18},{17,... | collective-permute-start | bytes 786440 | tf_op jit(solution)/shard_map/ppermute | solution.py:717
  56.1 14.3 %collective-permute-start.13 = (bf16[4,256,256]{2,1,0:T(8,128)(2,1)S(1)}, bf16[4,256,256]{2,1,0:T(8,128)(2,1)S(1)}, u32[]{:S(2)}, u32[]{:S(2)}) collective-permute-start(bf16[4,256,256]{2,1,0:T(8,128)(2,1)S(1)} %get-tuple-element.122), channel_id=1, source_target_pairs={{0,8},{4,12},{24,16},{28,20},{16,24},{20,28},{8,0},{12,4},{1,9},{5... | collective-permute-start | bytes 1572872 | tf_op jit(solution)/shard_map/ppermute | solution.py:673
  60.0 10.5 %collective-permute-start.14 = (bf16[4,256,256]{2,1,0:T(8,128)(2,1)S(1)}, bf16[4,256,256]{2,1,0:T(8,128)(2,1)S(1)}, u32[]{:S(2)}, u32[]{:S(2)}) collective-permute-start(bf16[4,256,256]{2,1,0:T(8,128)(2,1)S(1)} %get-tuple-element.123), channel_id=1, source_target_pairs={{8,16},{12,20},{16,8},{20,12},{9,17},{13,21},{17,9},{21,13},{10,18... | collective-permute-start | bytes 1572872 | tf_op jit(solution)/shard_map/ppermute | solution.py:663
  63.4 6.4 %collective-permute-start.17 = (bf16[2,256,256]{2,1,0:T(8,128)(2,1)S(1)}, bf16[2,256,256]{2,1,0:T(8,128)(2,1)S(1)}, u32[]{:S(2)}, u32[]{:S(2)}) collective-permute-start(bf16[2,256,256]{2,1,0:T(8,128)(2,1)S(1)} %get-tuple-element.128), channel_id=1, source_target_pairs={{0,1},{1,0},{2,3},{3,2},{4,5},{5,4},{6,7},{7,6},{8,9},{9,8},{10,11... | collective-permute-start | bytes 786440 | tf_op jit(solution)/shard_map/ppermute | solution.py:714
  71.7 13.9 %collective-permute-start.18 = (bf16[4,256,256]{2,1,0:T(8,128)(2,1)S(1)}, bf16[4,256,256]{2,1,0:T(8,128)(2,1)S(1)}, u32[]{:S(2)}, u32[]{:S(2)}) collective-permute-start(bf16[4,256,256]{2,1,0:T(8,128)(2,1)S(1)} %get-tuple-element.131), channel_id=1, source_target_pairs={{8,16},{12,20},{16,8},{20,12},{9,17},{13,21},{17,9},{21,13},{10,18... | collective-permute-start | bytes 1572872 | tf_op jit(solution)/shard_map/ppermute | solution.py:663
  72.4 16.2 %collective-permute-start.19 = (bf16[4,256,256]{2,1,0:T(8,128)(2,1)S(1)}, bf16[4,256,256]{2,1,0:T(8,128)(2,1)S(1)}, u32[]{:S(2)}, u32[]{:S(2)}) collective-permute-start(bf16[4,256,256]{2,1,0:T(8,128)(2,1)S(1)} %get-tuple-element.132), channel_id=1, source_target_pairs={{16,24},{20,28},{8,0},{12,4},{17,25},{21,29},{9,1},{13,5},{18,26},... | collective-permute-start | bytes 1572872 | tf_op jit(solution)/shard_map/ppermute | solution.py:663
  73.7 3.4 %collective-permute-start.20 = (bf16[2,256,256]{2,1,0:T(8,128)(2,1)S(1)}, bf16[2,256,256]{2,1,0:T(8,128)(2,1)S(1)}, u32[]{:S(2)}, u32[]{:S(2)}) collective-permute-start(bf16[2,256,256]{2,1,0:T(8,128)(2,1)S(1)} %get-tuple-element.135), channel_id=1, source_target_pairs={{0,4},{4,0},{1,5},{5,1},{2,6},{6,2},{3,7},{7,3}} | collective-permute-start | bytes 786440 | tf_op jit(solution)/shard_map/ppermute | solution.py:773
  75.8 15.3 %collective-permute-start.22 = (bf16[4,256,256]{2,1,0:T(8,128)(2,1)S(1)}, bf16[4,256,256]{2,1,0:T(8,128)(2,1)S(1)}, u32[]{:S(2)}, u32[]{:S(2)}) collective-permute-start(bf16[4,256,256]{2,1,0:T(8,128)(2,1)S(1)} %get-tuple-element.144), channel_id=1, source_target_pairs={{0,4},{4,0},{8,12},{12,8},{16,20},{20,16},{24,28},{28,24},{1,5},{5... | collective-permute-start | bytes 1572872 | tf_op jit(solution)/shard_map/ppermute | solution.py:648
  89.7 2.0 %collective-permute-start.23 = (bf16[4,256,256]{2,1,0:T(8,128)(2,1)S(1)}, bf16[4,256,256]{2,1,0:T(8,128)(2,1)S(1)}, u32[]{:S(2)}, u32[]{:S(2)}) collective-permute-start(bf16[4,256,256]{2,1,0:T(8,128)(2,1)S(1)} %get-tuple-element.146), channel_id=1, source_target_pairs={{0,4},{4,0},{8,12},{12,8},{16,20},{20,16},{24,28},{28,24},{1,5},{5... | collective-permute-start | bytes 1572872 | tf_op jit(solution)/shard_map/ppermute | solution.py:648
  89.8 17.3 %collective-permute-start.21 = (bf16[4,256,256]{2,1,0:T(8,128)(2,1)S(1)}, bf16[4,256,256]{2,1,0:T(8,128)(2,1)S(1)}, u32[]{:S(2)}, u32[]{:S(2)}) collective-permute-start(bf16[4,256,256]{2,1,0:T(8,128)(2,1)S(1)} %get-tuple-element.142), channel_id=1, source_target_pairs={{16,24},{20,28},{8,0},{12,4},{17,25},{21,29},{9,1},{13,5},{18,26},... | collective-permute-start | bytes 1572872 | tf_op jit(solution)/shard_map/ppermute | solution.py:663
  108.1 2.0 %collective-permute-start.24 = (bf16[4,256,256]{2,1,0:T(8,128)(2,1)S(1)}, bf16[4,256,256]{2,1,0:T(8,128)(2,1)S(1)}, u32[]{:S(2)}, u32[]{:S(2)}) collective-permute-start(bf16[4,256,256]{2,1,0:T(8,128)(2,1)S(1)} %get-tuple-element.153), channel_id=1, source_target_pairs={{0,4},{4,0},{8,12},{12,8},{16,20},{20,16},{24,28},{28,24},{1,5},{5... | collective-permute-start | bytes 1572872 | tf_op jit(solution)/shard_map/ppermute | solution.py:648
